TPU v7x, 32 devices: a whole 2x2x4 slice. The times are simulated.
32 devices in a mesh: groups: 2 (over x), terms: 16 (over z, y, core).
Axes of the slice: x: 2, y: 2, z: 4, core: 2. Of those that a mesh axis runs over, the one named last changes fastest.
Arguments:
- psi: bfloat16 [32768, 384], P(('groups', 'terms')), parts along dimension 0, may hold values from -6 to 6
- left_env: bfloat16 [32, 16384, 128], P('groups', 'terms'), parts along dimension 0, may hold values from -0.125 to 0.125
- right_env: bfloat16 [524288, 128], P(('groups', 'terms')), parts along dimension 0, may hold values from -0.5 to 0.5
- target: int32 [32, 128], P('groups'), parts along dimension 0, may hold values from -1 to 127, as said below
Outputs:
- h_psi: bfloat16 [32768, 384], P(('groups', 'terms')), parts along dimension 0
There are 2 independent parts, one for each index of `groups`. A program takes and returns all parts, laid end to end along the dimension named above; each array names one. Nothing has to cross between parts.
Inputs may be any that keep to these rules, and one draw needn't show every extreme that they name: Each term t has one shift q in -2..2, and target[t, c] = c + q where that lies in 0..127, else -1.
All inputs are finite; a program needn't handle non-finite values.
Results may differ from a plain program's by a relative error of at most 0.0058.
Values may be sent and summed in bfloat16 or wider, within the bound.
No kernel may reach another device: no remote copies, remote signals or barrier semaphores. Data moves between devices by JAX's collectives and lax.ppermute only.
A program may use at most 128 MiB of HBM per device.

v0:
```python
import jax
import jax.numpy as jnp
from jax import lax
from jax.sharding import PartitionSpec as P


def shards(psi, left_env, right_env, target):
    terms_count = target.shape[0]
    block_width = left_env.shape[2]
    columns = psi.shape[1]
    vectors = columns // block_width
    devices = lax.axis_size("terms")
    stride = devices // terms_count
    local_blocks = psi.shape[0] // block_width
    per_class = local_blocks // stride
    my_index = lax.axis_index("terms")
    shifts = target[:, 2] - 2
    is_live = lax.dynamic_slice_in_dim(target, my_index * local_blocks, local_blocks, 1) >= 0
    is_live = jnp.transpose(is_live.reshape(terms_count, per_class, stride), (0, 2, 1))
    left_blocks = left_env.reshape(terms_count, per_class, stride, block_width, block_width)
    psi_blocks = psi.reshape(per_class, stride, block_width, columns)
    mixed = jnp.einsum(
        "tjgab,jgbc->tgjac", left_blocks, psi_blocks, preferred_element_type=jnp.float32
    )
    mixed = jnp.where(is_live[:, :, :, None, None], mixed, 0.0).astype(jnp.bfloat16)
    outgoing = mixed.reshape(devices, per_class, block_width, columns)
    incoming = lax.all_to_all(outgoing, "terms", split_axis=0, concat_axis=0, tiled=True)
    regrouped = incoming.reshape(devices * per_class, block_width, vectors, block_width)
    right_items = right_env.reshape(devices * per_class, block_width, block_width)
    partial_out = jnp.einsum(
        "kavb,kbm->kavm", regrouped, right_items, preferred_element_type=jnp.float32
    ).astype(jnp.bfloat16)
    partial_out = partial_out.reshape(devices * per_class, block_width, columns)
    term_index = my_index // stride
    class_index = my_index % stride
    class_move = jnp.floor_divide(class_index + shifts[term_index], stride)
    padded = jnp.pad(partial_out, ((2, 2), (0, 0), (0, 0)))
    ordered = lax.dynamic_slice_in_dim(padded, 2 - class_move, devices * per_class, 0)
    returned = lax.all_to_all(
        ordered.reshape(devices, per_class, block_width, columns),
        "terms",
        split_axis=0,
        concat_axis=0,
        tiled=True,
    )
    returned = returned.reshape(terms_count, stride, per_class, block_width, columns)
    classes = lax.iota(jnp.int32, stride)
    source_class = jnp.mod(classes[None, :] - shifts[:, None], stride)
    selector = (source_class[:, :, None] == classes[None, None, :]).astype(jnp.bfloat16)
    summed = jnp.einsum("trg,tgjac->jrac", selector, returned, preferred_element_type=jnp.float32)
    return summed.reshape(local_blocks * block_width, columns).astype(jnp.bfloat16)


def solution(mesh):
    return jax.shard_map(
        shards,
        mesh=mesh,
        in_specs=(
            P(("groups", "terms"), None),
            P("groups", "terms", None),
            P(("groups", "terms"), None),
            P("groups", None),
        ),
        out_specs=P(("groups", "terms"), None),
        check_vma=False,
    )
```

profile of v0, /device:TPU:17, one launch (start us, length us, event | category | flops | bytes accessed | tf_op | source)
XLA Modules:
  0.0 640.7 jit_solution(8162255410708898085)
XLA Ops:
  0.0 0.0 copy-start
  0.0 0.8 constant_dynamic-slice_fusion.1
  0.8 0.1 copy.47
  0.9 0.2 copy-done
  1.2 6.6 %fusion.1 = bf16[16,8,128,384]{2,3,0,1:T(8,128)(2,1)S(1)} fusion(pred[16,8]{0,1:T(8,128)(4,1)S(1)} %broadcast_compare_fusion, bf16[8,128,384,1]{2,1,3,0:T(8,128)(2,1)S(1)} %bitcast.36, bf16[16,8,128,128]{3,2,1,0:T(8,128)(2,1)} %bitcast.42), kind=kOutput, calls=%fused_computation.3 | convolution fusion | flops 1623195648 | bytes 17563776 | tf_op jit(solution)/shard_map/tjgab,jgbc->tgjac/dot_general | solution.py:22
  7.7 6.1 copy.34
  13.9 0.0 copy-start.2
  13.9 6.6 %all-to-all-start = ((bf16[16,8,128,384]{2,3,1,0:T(8,128)(2,1)}), bf16[16,8,128,384]{2,3,1,0:T(8,128)(2,1)}, u32[]{:S(2)}, u32[]{:S(2)}) async-start(bf16[16,8,128,384]{2,3,1,0:T(8,128)(2,1)} %copy.34), calls=%async_computation | async-start | bytes 25165824 | tf_op jit(solution)/shard_map/all_to_all | solution.py:27
  20.5 0.0 copy-done.2
  20.5 0.1 slice.3
  20.6 0.5 fusion.6
  22.4 270.0 %all-to-all-done = bf16[16,8,128,384]{2,3,1,0:T(8,128)(2,1)} async-done(((bf16[16,8,128,384]{2,3,1,0:T(8,128)(2,1)}), bf16[16,8,128,384]{2,3,1,0:T(8,128)(2,1)}, u32[]{:S(2)}, u32[]{:S(2)}) %all-to-all-start) | async-done | bytes 12582944 | tf_op jit(solution)/shard_map/all_to_all | solution.py:27
  292.5 10.2 %convolution_convert_fusion = bf16[128,128,3,128]{1,3,2,0:T(8,128)(2,1)} fusion(bf16[128,128,3,128]{1,3,2,0:T(8,128)(2,1)} %bitcast.6, bf16[128,128,128,1]{2,1,3,0:T(8,128)(2,1)} %bitcast.41), kind=kOutput, calls=%fused_computation.4 | convolution fusion | flops 1616904192 | bytes 29360128 | tf_op jit(solution)/shard_map/kavb,kbm->kavm/dot_general | solution.py:30
  302.7 16.6 %copy.37 = bf16[128,128,384]{2,1,0:T(8,128)(2,1)} copy(bf16[128,128,384]{1,2,0:T(8,128)(2,1)} %bitcast.38) | data formatting | bytes 25165824 | tf_op jit(solution)/shard_map/reshape | solution.py:33
  319.3 7.0 %pad_dynamic-slice_fusion = bf16[128,128,384]{2,1,0:T(8,128)(2,1)S(1)} fusion(s32[]{:T(128)S(6)} %select_n.30, bf16[128,128,384]{2,1,0:T(8,128)(2,1)} %copy.37), kind=kLoop, calls=%fused_computation.2 | loop fusion | bytes 25165828 | tf_op jit(solution)/shard_map/dynamic_slice | solution.py:38
  326.3 277.0 %all_to_all.10 = bf16[16,8,128,384]{3,2,1,0:T(8,128)(2,1)S(1)} all-to-all(bf16[16,8,128,384]{3,2,1,0:T(8,128)(2,1)S(1)} %bitcast.40), channel_id=1, replica_groups=mesh['groups'=2,'terms'=16] {'terms'}, dimensions={0} | all-to-all | bytes 25165824 | tf_op jit(solution)/shard_map/all_to_all | solution.py:39
  603.3 34.4 %copy.38 = bf16[8,128,384,16]{2,3,1,0:T(8,128)(2,1)S(1)} copy(bf16[8,128,384,16]{2,1,0,3:T(8,128)(2,1)S(1)} %bitcast.39) | data formatting | bytes 25165824 | tf_op jit(solution)/shard_map/trg,tgjac->jrac/dot_general | solution.py:50
  637.7 0.0 copy-start.1
  637.8 2.0 fusion.3
  639.7 1.0 copy.51
  640.7 0.0 copy-done.1
  (1 shorter events, 0.0 us)
Async XLA Ops:
  0.0 1.1 copy-start
  13.9 6.6 %copy-start.2 = (s32[16,128]{1,0:T(8,128)S(1)}, s32[16,128]{1,0:T(8,128)}, u32[]{:S(2)}) copy-start(s32[16,128]{1,0:T(8,128)} %param.7) | copy-start | bytes 24580
  13.9 278.6 %all-to-all-start = ((bf16[16,8,128,384]{2,3,1,0:T(8,128)(2,1)}), bf16[16,8,128,384]{2,3,1,0:T(8,128)(2,1)}, u32[]{:S(2)}, u32[]{:S(2)}) async-start(bf16[16,8,128,384]{2,3,1,0:T(8,128)(2,1)} %copy.34), calls=%async_computation | async-start | bytes 25165824 | tf_op jit(solution)/shard_map/all_to_all | solution.py:27
  637.7 3.0 copy-start.1
where the time goes:
time: 643 us; the launch traced here: 641 us
  blocking collectives  277 us (43%)
  waiting for transfers between devices  270 us (42%)
  local copies, waits for them, and re-layouts  66.4 us (10%)
  matrix products  18.8 us (3%)
  starting transfers between devices  6.64 us (1%)
    all_to_all x1, blocking collectives, shards(): lax.all_to_all(ordered.reshape(devices, per_class, block_width, columns),...  277 us
    all_to_all x1, waiting for transfers between devices, shards(): lax.all_to_all(outgoing, 'terms', split_axis=0, concat_axis=0, tiled=True)  270 us
    dot_general x2, local copies, waits for them, and re-layouts, shards(): jnp.einsum('trg,tgjac->jrac', selector, returned, preferred_element_type=...  35.4 us
    reshape x1, local copies, waits for them, and re-layouts, shards(): partial_out = partial_out.reshape(devices * per_class, block_width, columns)  16.6 us
  transfers between devices with their start and end apart: 1, of which 1 were waited for; matrix products, arithmetic and copies ran while one was open for 0% of the time, Pallas kernels for 0%

commit v1 on v0

v1 whole, which is shorter than its diff:
```python
import functools

import jax
import jax.numpy as jnp
from jax import lax
from jax.experimental import pallas as pl
from jax.experimental.pallas import tpu as pltpu
from jax.sharding import PartitionSpec as P

REACH = 2
ORDER = (8, 1, 13, 4, 10, 2, 15, 5, 9, 3, 12, 6, 7)
LAST = (11, 14)
GROUPS = ((0, 8, 1, 13), (4, 10, 2, 15), (5, 9, 3, 12), (6, 7))


def params(megabytes=40):
    return pltpu.CompilerParams(vmem_limit_bytes=megabytes * 2**20)


def spec(block, index):
    return pl.BlockSpec(block, index)


def cost(pairs, width, columns, extra_bytes=0):
    return pl.CostEstimate(
        flops=pairs * 2 * width * width * columns,
        bytes_accessed=pairs * width * (columns + width) * 2 + extra_bytes,
        transcendentals=0,
    )


def mix_kernel(places, me_ref, target_ref, left_ref, psi_ref, mixed_ref):
    for slot, block in enumerate(places):
        product = jnp.dot(left_ref[0, block], psi_ref[block], preferred_element_type=jnp.float32)
        mixed_ref[0, slot] = product.astype(mixed_ref.dtype)


def mix(me, target, left_env, psi, terms_of, places):
    terms, blocks, width, _ = left_env.shape
    columns = psi.shape[2]
    return pl.pallas_call(
        functools.partial(mix_kernel, places),
        grid_spec=pltpu.PrefetchScalarGridSpec(
            num_scalar_prefetch=2,
            grid=(terms,),
            in_specs=[
                spec((1, blocks, width, width), lambda s, me, target: (terms_of(me[0], s), 0, 0, 0)),
                spec((blocks, width, columns), lambda s, me, target: (0, 0, 0)),
            ],
            out_specs=spec((1, blocks, width, columns), lambda s, me, target: (s, 0, 0, 0)),
        ),
        out_shape=jax.ShapeDtypeStruct((terms, blocks, width, columns), jnp.bfloat16),
        cost_estimate=cost(terms * blocks, width, columns),
        compiler_params=params(),
        name="mix",
    )(me, target, left_env, psi)


def accumulate(acc, mixed, right, shift, slots, rows, base):
    width = right.shape[-1]
    columns = mixed.shape[-1]
    vectors = columns // width
    for slot, piece, row in zip(slots, range(len(slots)), rows):
        tall = jnp.concatenate(
            [mixed[0, slot, :, k * width : (k + 1) * width] for k in range(vectors)], axis=0
        )
        product = jnp.dot(tall, right[piece], preferred_element_type=jnp.float32)
        start = pl.multiple_of((row + base + shift) * width, width)
        for k in range(vectors):
            lanes = slice(k * width, (k + 1) * width)
            acc[pl.ds(start, width), lanes] += product[k * width : (k + 1) * width]


def shift_of(me_ref, target_ref, terms_of, s):
    return target_ref[terms_of(me_ref[0], s), REACH] - REACH


def group_kernel(patterns, terms_of, slots, rows, first, own, me_ref, target_ref, *refs):
    refs = list(refs)
    mixed = [refs.pop(0) for _ in patterns]
    right = [refs.pop(0) for _ in patterns]
    if first:
        (acc,) = refs
        acc[...] = jnp.zeros_like(acc)
    else:
        before, acc = refs
        acc[...] = before[...]
    for s, m, r in zip(patterns, mixed, right):
        accumulate(
            acc, m, r.at[0] if own and s == 0 else r, shift_of(me_ref, target_ref, terms_of, s), slots, rows, REACH
        )


def edge_kernel(patterns, terms_of, slots, rows, blocks, me_ref, target_ref, *refs):
    refs = list(refs)
    mixed = [refs.pop(0) for _ in patterns]
    right = [refs.pop(0) for _ in patterns]
    before, inner, to_left, to_right, acc = refs
    width = right[0].shape[-1]
    acc[...] = before[...]
    for s, m, r in zip(patterns, mixed, right):
        accumulate(acc, m, r, shift_of(me_ref, target_ref, terms_of, s), slots, rows, REACH)
    halo = REACH * width
    to_left[...] = acc[:halo].astype(to_left.dtype)
    to_right[...] = acc[halo + blocks * width :].astype(to_right.dtype)
    inner[...] = acc[halo : halo + blocks * width]


def last_kernel(patterns, terms_of, slots, rows, me_ref, target_ref, *refs):
    refs = list(refs)
    mixed = [refs.pop(0) for _ in patterns]
    right = [refs.pop(0) for _ in patterns]
    before, from_left, from_right, out, acc = refs
    halo = from_left.shape[0]
    acc[...] = before[...]
    acc[:halo] += from_left[...].astype(jnp.float32)
    acc[-halo:] += from_right[...].astype(jnp.float32)
    for s, m, r in zip(patterns, mixed, right):
        accumulate(acc, m, r, shift_of(me_ref, target_ref, terms_of, s), slots, rows, 0)
    out[...] = acc[...].astype(out.dtype)


def whole_spec(x):
    return spec(x.shape, lambda i, me, target, nd=x.ndim: (0,) * nd)


def shards(psi, left_env, right_env, target):
    terms = target.shape[0]
    width = left_env.shape[2]
    columns = psi.shape[1]
    devices = lax.axis_size("terms")
    stride = devices // terms
    blocks = psi.shape[0] // width
    per_class = blocks // stride
    me = lax.axis_index("terms")
    me_ref = me.astype(jnp.int32).reshape(1)
    edges = tuple(c for c in range(blocks) if c < REACH or c >= blocks - REACH)
    inside = tuple(c for c in range(blocks) if c not in edges)
    places = inside + edges
    slot_of = {c: i for i, c in enumerate(places)}
    by_partner = stride == 1 and terms == len(ORDER) + len(LAST) + 1
    terms_of = (lambda own, s: jnp.bitwise_xor(own, s)) if by_partner else (lambda own, s: s)

    psi_blocks = psi.reshape(blocks, width, columns)
    left_blocks = left_env.reshape(terms, blocks, width, width)

    def send(s, rows=None):
        right = right_env.reshape(devices, blocks, width, width)
        mine = lax.dynamic_index_in_dim(right, jnp.bitwise_xor(me, s), 0, keepdims=False)
        if rows is not None:
            mine = jnp.concatenate([mine[a:b] for a, b in rows], axis=0)
        return lax.ppermute(mine, "terms", [(i, i ^ s) for i in range(devices)])

    if by_partner:
        pieces = {s: send(s) for s in ORDER}
        edge_pieces = {s: send(s, ((0, REACH), (blocks - REACH, blocks))) for s in LAST}
        inner_pieces = {s: send(s, ((REACH, blocks - REACH),)) for s in LAST}
        pieces[0] = right_env.reshape(devices, blocks, width, width)
        groups, last = GROUPS, LAST
    else:
        sent = right_env.reshape(devices, per_class, width, width)
        got = lax.all_to_all(sent, "terms", split_axis=0, concat_axis=0, tiled=True)
        got = got.reshape(terms, stride, per_class, width, width)
        got = jnp.swapaxes(got, 1, 2).reshape(terms, blocks, width, width)
        last = (terms - 1,)
        pieces = {s: got[s] for s in range(terms - 1)}
        edge_pieces = {s: jnp.concatenate([got[s, :REACH], got[s, -REACH:]], axis=0) for s in last}
        inner_pieces = {s: got[s, REACH:-REACH] for s in last}
        groups = tuple(tuple(range(a, min(a + 4, terms - 1))) for a in range(0, terms - 1, 4))

    mixed = mix(me_ref, target, left_blocks, psi_blocks, terms_of, places)

    def mixed_spec(s, part, parts):
        count = len(part)
        at = slot_of[part[0]] // count if parts > 1 else 0
        return spec((1, count, width, columns), lambda i, me, target: (s, at, 0, 0))

    padded = (blocks + 2 * REACH) * width
    acc_shape = jax.ShapeDtypeStruct((padded, columns), jnp.float32)
    core_shape = jax.ShapeDtypeStruct((blocks * width, columns), jnp.float32)
    halo_shape = jax.ShapeDtypeStruct((REACH * width, columns), jnp.bfloat16)
    out_shape = jax.ShapeDtypeStruct((blocks * width, columns), jnp.bfloat16)
    everything = tuple(range(blocks))

    def call(kernel, patterns, specs, operands, outs, scratch, pairs, name):
        single = not isinstance(outs, tuple)
        out_list = (outs,) if single else outs
        out_specs = tuple(whole_spec(x) for x in out_list)
        return pl.pallas_call(
            kernel,
            grid_spec=pltpu.PrefetchScalarGridSpec(
                num_scalar_prefetch=2,
                grid=(1,),
                in_specs=specs,
                out_specs=out_specs[0] if single else out_specs,
                scratch_shapes=scratch,
            ),
            out_shape=outs,
            cost_estimate=cost(pairs, width, columns, 2 * padded * columns * 4),
            compiler_params=params(),
            name=name,
        )(me_ref, target, *operands)

    acc = None
    for number, patterns in enumerate(groups):
        specs = [mixed_spec(s, places, 1) for s in patterns]
        operands = [mixed for _ in patterns]
        for s in patterns:
            if by_partner and s == 0:
                specs.append(spec((1, blocks, width, width), lambda i, me, target: (me[0], 0, 0, 0)))
            else:
                specs.append(whole_spec(pieces[s]))
            operands.append(pieces[s])
        if number:
            specs.append(whole_spec(acc))
            operands.append(acc)
        kernel = functools.partial(
            group_kernel, patterns, terms_of, tuple(slot_of[c] for c in everything), everything, number == 0, by_partner
        )
        acc = call(kernel, patterns, specs, operands, acc_shape, (), len(patterns) * blocks, "add_terms")

    specs = [mixed_spec(s, edges, 2) for s in last] + [whole_spec(edge_pieces[s]) for s in last] + [whole_spec(acc)]
    operands = [mixed for _ in last] + [edge_pieces[s] for s in last] + [acc]
    kernel = functools.partial(edge_kernel, last, terms_of, tuple(range(len(edges))), edges, blocks)
    core, to_left, to_right = call(
        kernel, last, specs, operands, (core_shape, halo_shape, halo_shape),
        (pltpu.VMEM(acc_shape.shape, jnp.float32),), len(last) * len(edges), "add_edges",
    )
    from_right = lax.ppermute(to_left, "terms", [(i + 1, i) for i in range(devices - 1)])
    from_left = lax.ppermute(to_right, "terms", [(i, i + 1) for i in range(devices - 1)])

    specs = [mixed_spec(s, inside, 2) for s in last] + [whole_spec(inner_pieces[s]) for s in last]
    specs += [whole_spec(core), whole_spec(from_left), whole_spec(from_right)]
    operands = [mixed for _ in last] + [inner_pieces[s] for s in last] + [core, from_left, from_right]
    kernel = functools.partial(last_kernel, last, terms_of, tuple(range(len(inside))), inside)
    return call(
        kernel, last, specs, operands, out_shape,
        (pltpu.VMEM(core_shape.shape, jnp.float32),), len(last) * len(inside), "add_rest",
    )


def solution(mesh):
    return jax.shard_map(
        shards,
        mesh=mesh,
        in_specs=(
            P(("groups", "terms"), None),
            P("groups", "terms", None),
            P(("groups", "terms"), None),
            P("groups", None),
        ),
        out_specs=P(("groups", "terms"), None),
        check_vma=False,
    )
```

time: 643 us -> 125 us (0.19)
  blocking collectives: 277 us -> 0 us
  waiting for transfers between devices: 270 us -> 51.3 us
  local copies, waits for them, and re-layouts: 66.4 us -> 6.54 us
  Pallas kernels: 0 us -> 31.1 us
  starting transfers between devices: 6.64 us -> 33.6 us
  matrix products: 18.8 us -> 0 us
    all_to_all x1 -> x0, blocking collectives: 277 us -> none  [shards(): lax.all_to_all(ordered.reshape(devices, per_class, block_width, columns),...]
    all_to_all x1 -> x0, waiting for transfers between devices: 270 us -> none  [shards(): lax.all_to_all(outgoing, 'terms', split_axis=0, concat_axis=0, tiled=True)]
    ppermute x0 -> x19, waiting for transfers between devices: none -> 51.3 us  [the longest x17 51.3 us: send(): return lax.ppermute(mine, 'terms', [(i, i ^ s) for i in range(devices)])]
    dot_general x2 -> x0, local copies, waits for them, and re-layouts: 35.4 us -> none  [shards(): jnp.einsum('trg,tgjac->jrac', selector, returned, preferred_element_type=...]
    ppermute x0 -> x19, starting transfers between devices: none -> 33.6 us  [the longest x17 28.2 us: send(): return lax.ppermute(mine, 'terms', [(i, i ^ s) for i in range(devices)])]
    pallas_call x0 -> x7, Pallas kernels: none -> 31.1 us  [the longest x6 19.9 us: call(): pl.pallas_call(kernel, grid_spec=pltpu.PrefetchScalarGridSpec(num_scalar_...]
    reshape x2 -> x0, local copies, waits for them, and re-layouts: 22.7 us -> none  [the longest x1 16.6 us: shards(): partial_out = partial_out.reshape(devices * per_class, block_width, columns)]
    dot_general x3 -> x0, matrix products: 18.8 us -> none  [the longest x1 10.2 us: shards(): jnp.einsum('kavb,kbm->kavm', regrouped, right_items, preferred_element_ty...]
  transfers between devices with their start and end apart: 1 -> 19, of which waited for: 1 -> 5; matrix products, arithmetic and copies ran while one was open for 0% -> 1% of each run, Pallas kernels for 0% -> 21%
where the time goes in v1:
time: 125 us; the launch traced here: 123 us
  waiting for transfers between devices  51.3 us (41%)
  starting transfers between devices  33.6 us (27%)
  Pallas kernels  31.1 us (25%)
  local copies, waits for them, and re-layouts  6.54 us (5%)
    ppermute x17, waiting for transfers between devices, send(): return lax.ppermute(mine, 'terms', [(i, i ^ s) for i in range(devices)])  51.3 us
    ppermute x17, starting transfers between devices, send(): return lax.ppermute(mine, 'terms', [(i, i ^ s) for i in range(devices)])  28.2 us
    pallas_call x6, Pallas kernels, call(): pl.pallas_call(kernel, grid_spec=pltpu.PrefetchScalarGridSpec(num_scalar_...  19.9 us
    pallas_call x1, Pallas kernels, mix(): pl.pallas_call(functools.partial(mix_kernel, places), grid_spec=pltpu.Pre...  11.2 us
    ppermute x1, starting transfers between devices, shards(): lax.ppermute(to_right, 'terms', [(i, i + 1) for i in range(devices - 1)])  3.5 us
    squeeze x1, local copies, waits for them, and re-layouts, send(): lax.dynamic_index_in_dim(right, jnp.bitwise_xor(me, s), 0, keepdims=False)  3.35 us
  transfers between devices with their start and end apart: 19, of which 5 were waited for; matrix products, arithmetic and copies ran while one was open for 1% of the time, Pallas kernels for 21%

profile of v1, /device:TPU:17, one launch (start us, length us, event | category | flops | bytes accessed | tf_op | source)
XLA Modules:
  0.0 123.3 jit_solution(8470397564986704889)
XLA Ops:
  0.0 3.4 %dynamic-slice_bitcast_fusion = (bf16[8,128,128]{2,1,0:T(8,128)(2,1)S(1)}, bf16[8,128,128]{2,1,0:T(8,128)(2,1)S(1)}, bf16[8,128,128]{2,1,0:T(8,128)(2,1)S(1)}, b...) fusion(bf16[16,8,128,128]{3,2,1,0:T(8,128)(2,1)} %bitcast.42, ...), kind=kLoop, calls=%fused_computation | loop fusion | bytes 6815796 | tf_op jit(solution)/shard_map/jit(dynamic_index_in_dim)/squeeze | solution.py:149
  3.4 0.0 collective-permute-start.14
  3.4 0.7 collective-permute-start.15
  4.1 2.6 %collective-permute-start.16 = (bf16[8,128,128]{2,1,0:T(8,128)(2,1)S(1)}, bf16[8,128,128]{2,1,0:T(8,128)(2,1)S(1)}, u32[]{:S(2)}, u32[]{:S(2)}) collective-permute-start(bf16[8,128,128]{2,1,0:T(8,128)(2,1)S(1)} %get-tuple-element.11), channel_id=1, source_target_pairs={{0,13},{1,12},{2,15},{3,14},{4,9},{5,8},{6,11},{7,10},{8,5},{9,4},... | collective-permute-start | bytes 786440 | tf_op jit(solution)/shard_map/ppermute | solution.py:152
  6.7 1.1 collective-permute-start.10
  7.8 1.2 collective-permute-start.11
  8.9 11.0 %collective-permute-done.14.refs_5_ = bf16[8,128,128]{2,1,0:T(8,128)(2,1)S(1)} collective-permute-done((bf16[8,128,128]{2,1,0:T(8,128)(2,1)S(1)}, bf16[8,128,128]{2,1,0:T(8,128)(2,1)S(1)}, u32[]{:S(2)}, u32[]{:S(2)}) %collective-permute-start.14) | collective-permute-done | bytes 262176 | tf_op jit(solution)/shard_map/ppermute | solution.py:152
  19.9 1.0 collective-permute-start.12
  20.9 0.0 collective-permute-done.15.refs_6_
  20.9 4.9 %collective-permute-start.13 = (bf16[8,128,128]{2,1,0:T(8,128)(2,1)}, bf16[8,128,128]{2,1,0:T(8,128)(2,1)S(1)}, u32[]{:S(2)}, u32[]{:S(2)}) collective-permute-start(bf16[8,128,128]{2,1,0:T(8,128)(2,1)} %get-tuple-element.14), channel_id=1, source_target_pairs={{0,15},{1,14},{2,13},{3,12},{4,11},{5,10},{6,9},{7,8},{8,7},{9,6},... | collective-permute-start | bytes 786440 | tf_op jit(solution)/shard_map/ppermute | solution.py:152
  25.8 14.8 %collective-permute-done.16.refs_7_ = bf16[8,128,128]{2,1,0:T(8,128)(2,1)S(1)} collective-permute-done((bf16[8,128,128]{2,1,0:T(8,128)(2,1)S(1)}, bf16[8,128,128]{2,1,0:T(8,128)(2,1)S(1)}, u32[]{:S(2)}, u32[]{:S(2)}) %collective-permute-start.16) | collective-permute-done | bytes 262176 | tf_op jit(solution)/shard_map/ppermute | solution.py:152
  40.6 0.0 collective-permute-start.6
  40.6 1.0 dynamic-slice_bitcast_fusion.16
  41.6 0.0 collective-permute-done.10.refs_4_
  41.6 1.3 %collective-permute-start.7 = (bf16[8,128,128]{2,1,0:T(8,128)(2,1)}, bf16[8,128,128]{2,1,0:T(8,128)(2,1)S(1)}, u32[]{:S(2)}, u32[]{:S(2)}) collective-permute-start(bf16[8,128,128]{2,1,0:T(8,128)(2,1)} %get-tuple-element.20), channel_id=1, source_target_pairs={{0,9},{1,8},{2,11},{3,10},{4,13},{5,12},{6,15},{7,14},{8,1},{9,0},... | collective-permute-start | bytes 786440 | tf_op jit(solution)/shard_map/ppermute | solution.py:152
  42.9 0.0 collective-permute-done.11.refs_5_
  42.9 3.1 %collective-permute-start.8 = (bf16[8,128,128]{2,1,0:T(8,128)(2,1)}, bf16[8,128,128]{2,1,0:T(8,128)(2,1)S(1)}, u32[]{:S(2)}, u32[]{:S(2)}) collective-permute-start(bf16[8,128,128]{2,1,0:T(8,128)(2,1)} %get-tuple-element.19), channel_id=1, source_target_pairs={{0,3},{1,2},{2,1},{3,0},{4,7},{5,6},{6,5},{7,4},{8,11},{9,10},{10,... | collective-permute-start | bytes 786440 | tf_op jit(solution)/shard_map/ppermute | solution.py:152
  46.0 0.0 collective-permute-done.12.refs_6_
  46.0 1.3 %collective-permute-start.9 = (bf16[8,128,128]{2,1,0:T(8,128)(2,1)}, bf16[8,128,128]{2,1,0:T(8,128)(2,1)}, u32[]{:S(2)}, u32[]{:S(2)}) collective-permute-start(bf16[8,128,128]{2,1,0:T(8,128)(2,1)} %get-tuple-element.18), channel_id=1, source_target_pairs={{0,12},{1,13},{2,14},{3,15},{4,8},{5,9},{6,10},{7,11},{8,4},{9,5},... | collective-permute-start | bytes 786440 | tf_op jit(solution)/shard_map/ppermute | solution.py:152
  47.3 0.7 pad_maximum_fusion.1
  47.9 16.2 %collective-permute-done.13.refs_7_ = bf16[8,128,128]{2,1,0:T(8,128)(2,1)S(1)} collective-permute-done((bf16[8,128,128]{2,1,0:T(8,128)(2,1)}, bf16[8,128,128]{2,1,0:T(8,128)(2,1)S(1)}, u32[]{:S(2)}, u32[]{:S(2)}) %collective-permute-start.13) | collective-permute-done | bytes 262176 | tf_op jit(solution)/shard_map/ppermute | solution.py:152
  64.1 0.0 collective-permute-start.4
  64.1 0.0 collective-permute-done.6.refs_4_
  64.1 2.9 %collective-permute-start.5 = (bf16[8,128,128]{2,1,0:T(8,128)(2,1)}, bf16[8,128,128]{2,1,0:T(8,128)(2,1)S(1)}, u32[]{:S(2)}, u32[]{:S(2)}) collective-permute-start(bf16[8,128,128]{2,1,0:T(8,128)(2,1)} %get-tuple-element.22), channel_id=1, source_target_pairs={{0,7},{1,6},{2,5},{3,4},{4,3},{5,2},{6,1},{7,0},{8,15},{9,14},{10,... | collective-permute-start | bytes 786440 | tf_op jit(solution)/shard_map/ppermute | solution.py:152
  67.1 2.2 %copy-done.1 = bf16[16,1024,128]{2,1,0:T(8,128)(2,1)S(1)} copy-done((bf16[16,1024,128]{2,1,0:T(8,128)(2,1)S(1)}, bf16[16,1024,128]{2,1,0:T(8,128)(2,1)}, u32[]{:S(2)}) %copy-start.1) | copy-done | bytes 4194328
  69.3 11.2 %mix.1.refs_0_.refs_1_.refs_2_.refs_3_ = bf16[16,8,128,384]{3,2,1,0:T(8,128)(2,1)} custom-call(s32[1]{0:T(128)} %bitcast.me_ref, s32[16,128]{1,0:T(8,128)S(1)} %copy-done.3, bf16[16,8,128,128]{3,2,1,0:T(8,128)(2,1)S(1)} %bitcast.46, bf16[8,128,384]{2,1,0:T(8,128)(2,1)S(1)} %bitcast.47), custom_call_target="tpu_custom_call" | custom-call | flops 1610612736 | bytes 16777216 | tf_op jit(solution)/shard_map/mix/pallas_call | solution.py:41
  80.4 0.0 collective-permute-done.7.refs_5_
  80.4 0.0 collective-permute-start.2
  80.4 0.0 collective-permute-done.8.refs_6_
  80.4 1.1 collective-permute-start.3
  81.5 3.7 %add_terms.4.refs_8_ = f32[1536,384]{1,0:T(8,128)S(1)} custom-call(s32[1]{0:T(128)} %bitcast.me_ref, s32[16,128]{1,0:T(8,128)S(1)} %copy-done.3, bf16[16,8,128,384]{3,2,1,0:T(8,128)(2,1)} %mix.1.refs_0_.refs_1_.refs_2_.refs_3_, bf16[16,8,128,384]{3,2,1,0:T(8,128)(2,1)} %mix.1.refs_0_.refs_1_.refs_2_.refs_3_, ...), custom_call_target="tpu_custom_call" | custom-call | flops 402653184 | bytes 8912896 | tf_op jit(solution)/shard_map/add_terms/pallas_call | solution.py:189
  85.3 3.8 %add_terms.5.refs_8_ = f32[1536,384]{1,0:T(8,128)S(1)} custom-call(s32[1]{0:T(128)} %bitcast.me_ref, s32[16,128]{1,0:T(8,128)S(1)} %copy-done.3, bf16[16,8,128,384]{3,2,1,0:T(8,128)(2,1)} %mix.1.refs_0_.refs_1_.refs_2_.refs_3_, bf16[16,8,128,384]{3,2,1,0:T(8,128)(2,1)} %mix.1.refs_0_.refs_1_.refs_2_.refs_3_, ...), custom_call_target="tpu_custom_call" | custom-call | flops 402653184 | bytes 8912896 | tf_op jit(solution)/shard_map/add_terms/pallas_call | solution.py:189
  89.1 0.0 collective-permute-done.9.refs_7_
  89.1 3.8 %add_terms.6.refs_4_ = f32[1536,384]{1,0:T(8,128)S(1)} custom-call(s32[1]{0:T(128)} %bitcast.me_ref, s32[16,128]{1,0:T(8,128)S(1)} %copy-done.3, bf16[16,8,128,384]{3,2,1,0:T(8,128)(2,1)} %mix.1.refs_0_.refs_1_.refs_2_.refs_3_, bf16[16,8,128,384]{3,2,1,0:T(8,128)(2,1)} %mix.1.refs_0_.refs_1_.refs_2_.refs_3_, ...), custom_call_target="tpu_custom_call" | custom-call | flops 402653184 | bytes 8912896 | tf_op jit(solution)/shard_map/add_terms/pallas_call | solution.py:189
  92.9 0.0 collective-permute-done.4.refs_2_
  92.9 0.0 collective-permute-done.5.refs_3_
  93.0 2.8 %add_terms.7.refs_4_ = f32[1536,384]{1,0:T(8,128)S(1)} custom-call(s32[1]{0:T(128)} %bitcast.me_ref, s32[16,128]{1,0:T(8,128)S(1)} %copy-done.3, bf16[16,8,128,384]{3,2,1,0:T(8,128)(2,1)} %mix.1.refs_0_.refs_1_.refs_2_.refs_3_, bf16[16,8,128,384]{3,2,1,0:T(8,128)(2,1)} %mix.1.refs_0_.refs_1_.refs_2_.refs_3_, ...), custom_call_target="tpu_custom_call" | custom-call | flops 201326592 | bytes 6815744 | tf_op jit(solution)/shard_map/add_terms/pallas_call | solution.py:189
  95.8 0.0 collective-permute-done.2.refs_2_
  95.8 0.0 collective-permute-done.3.refs_3_
  95.8 2.5 %add_edges.1 = (f32[1024,384]{1,0:T(8,128)S(1)}, bf16[256,384]{1,0:T(8,128)(2,1)S(1)}, bf16[256,384]{1,0:T(8,128)(2,1)S(1)}) custom-call(s32[1]{0:T(128)} %bitcast.me_ref, s32[16,128]{1,0:T(8,128)S(1)} %copy-done.3, bf16[16,8,128,384]{3,2,1,0:T(8,128)(2,1)} %mix.1.refs_0_.refs_1_.refs_2_.refs_3_, ...), custom_call_target="tpu_custom_call" | custom-call | flops 100663296 | bytes 5767168 | tf_op jit(solution)/shard_map/add_edges/pallas_call | solution.py:189
  98.3 3.5 %collective-permute-start.17 = (bf16[256,384]{1,0:T(8,128)(2,1)S(1)}, bf16[256,384]{1,0:T(8,128)(2,1)S(1)}, u32[]{:S(2)}, u32[]{:S(2)}) collective-permute-start(bf16[256,384]{1,0:T(8,128)(2,1)S(1)} %get-tuple-element.9), channel_id=1, source_target_pairs={{0,1},{1,2},{2,3},{3,4},{4,5},{5,6},{6,7},{7,8},{8,9},{9,10},{10,1... | collective-permute-start | bytes 589832 | tf_op jit(solution)/shard_map/ppermute | solution.py:230
  101.8 1.9 %collective-permute-start.18 = (bf16[256,384]{1,0:T(8,128)(2,1)S(1)}, bf16[256,384]{1,0:T(8,128)(2,1)S(1)}, u32[]{:S(2)}, u32[]{:S(2)}) collective-permute-start(bf16[256,384]{1,0:T(8,128)(2,1)S(1)} %get-tuple-element.10), channel_id=1, source_target_pairs={{1,0},{2,1},{3,2},{4,3},{5,4},{6,5},{7,6},{8,7},{9,8},{10,9},{11,1... | collective-permute-start | bytes 589832 | tf_op jit(solution)/shard_map/ppermute | solution.py:229
  103.7 3.4 %collective-permute-start = (bf16[4,128,128]{2,1,0:T(8,128)(2,1)S(1)}, bf16[4,128,128]{2,1,0:T(8,128)(2,1)S(1)}, u32[]{:S(2)}, u32[]{:S(2)}) collective-permute-start(bf16[4,128,128]{2,1,0:T(8,128)(2,1)S(1)} %get-tuple-element.29), channel_id=1, source_target_pairs={{0,11},{1,10},{2,9},{3,8},{4,15},{5,14},{6,13},{7,12},{8,3},{9,2},... | collective-permute-start | bytes 393224 | tf_op jit(solution)/shard_map/ppermute | solution.py:152
  107.1 3.7 %collective-permute-start.1 = (bf16[4,128,128]{2,1,0:T(8,128)(2,1)S(1)}, bf16[4,128,128]{2,1,0:T(8,128)(2,1)S(1)}, u32[]{:S(2)}, u32[]{:S(2)}) collective-permute-start(bf16[4,128,128]{2,1,0:T(8,128)(2,1)S(1)} %get-tuple-element.28), channel_id=1, source_target_pairs={{0,14},{1,15},{2,12},{3,13},{4,10},{5,11},{6,8},{7,9},{8,6},{9,7},... | collective-permute-start | bytes 393224 | tf_op jit(solution)/shard_map/ppermute | solution.py:152
  110.8 1.0 collective-permute-done.refs_2_
  111.8 8.2 %collective-permute-done.1.refs_3_ = bf16[4,128,128]{2,1,0:T(8,128)(2,1)S(1)} collective-permute-done((bf16[4,128,128]{2,1,0:T(8,128)(2,1)S(1)}, bf16[4,128,128]{2,1,0:T(8,128)(2,1)S(1)}, u32[]{:S(2)}, u32[]{:S(2)}) %collective-permute-start.1) | collective-permute-done | bytes 131104 | tf_op jit(solution)/shard_map/ppermute | solution.py:152
  120.1 0.0 collective-permute-done.18.refs_6_
  120.1 3.3 %add_rest.1 = bf16[1024,384]{1,0:T(8,128)(2,1)} custom-call(s32[1]{0:T(128)} %bitcast.me_ref, s32[16,128]{1,0:T(8,128)S(1)} %copy-done.3, bf16[16,8,128,384]{3,2,1,0:T(8,128)(2,1)} %mix.1.refs_0_.refs_1_.refs_2_.refs_3_, bf16[16,8,128,384]{3,2,1,0:T(8,128)(2,1)} %mix.1.refs_0_.refs_1_.refs_2_.refs_3_, bf16[4,128,128]{2,1,0:T(8,128)(2,1)S(1)} %collective-permute-done.refs_2_, ...), custom_call_target="tpu_custom_call" | custom-call | flops 100663296 | bytes 5767168 | tf_op jit(solution)/shard_map/add_rest/pallas_call | solution.py:189
  (12 shorter events, 0.1 us)
Async XLA Ops:
  0.0 67.1 %copy-start.2 = (bf16[1024,384]{1,0:T(8,128)(2,1)S(1)}, bf16[1024,384]{1,0:T(8,128)(2,1)}, u32[]{:S(2)}) copy-start(bf16[1024,384]{1,0:T(8,128)(2,1)} %param.4) | copy-start | bytes 2359300
  0.0 67.1 %copy-start.3 = (s32[16,128]{1,0:T(8,128)S(1)}, s32[16,128]{1,0:T(8,128)}, u32[]{:S(2)}) copy-start(s32[16,128]{1,0:T(8,128)} %target_ref.13) | copy-start | bytes 24580
  3.4 16.6 %collective-permute-start.14 = (bf16[8,128,128]{2,1,0:T(8,128)(2,1)S(1)}, bf16[8,128,128]{2,1,0:T(8,128)(2,1)S(1)}, u32[]{:S(2)}, u32[]{:S(2)}) collective-permute-start(bf16[8,128,128]{2,1,0:T(8,128)(2,1)S(1)} %get-tuple-element.13), channel_id=1, source_target_pairs={{0,8},{1,9},{2,10},{3,11},{4,12},{5,13},{6,14},{7,15},{8,0},{9,1},... | collective-permute-start | bytes 786440 | tf_op jit(solution)/shard_map/ppermute | solution.py:152
  3.4 17.6 %collective-permute-start.15 = (bf16[8,128,128]{2,1,0:T(8,128)(2,1)S(1)}, bf16[8,128,128]{2,1,0:T(8,128)(2,1)S(1)}, u32[]{:S(2)}, u32[]{:S(2)}) collective-permute-start(bf16[8,128,128]{2,1,0:T(8,128)(2,1)S(1)} %get-tuple-element.12), channel_id=1, source_target_pairs={{0,1},{1,0},{2,3},{3,2},{4,5},{5,4},{6,7},{7,6},{8,9},{9,8},{10,11... | collective-permute-start | bytes 786440 | tf_op jit(solution)/shard_map/ppermute | solution.py:152
  4.1 36.5 %collective-permute-start.16 = (bf16[8,128,128]{2,1,0:T(8,128)(2,1)S(1)}, bf16[8,128,128]{2,1,0:T(8,128)(2,1)S(1)}, u32[]{:S(2)}, u32[]{:S(2)}) collective-permute-start(bf16[8,128,128]{2,1,0:T(8,128)(2,1)S(1)} %get-tuple-element.11), channel_id=1, source_target_pairs={{0,13},{1,12},{2,15},{3,14},{4,9},{5,8},{6,11},{7,10},{8,5},{9,4},... | collective-permute-start | bytes 786440 | tf_op jit(solution)/shard_map/ppermute | solution.py:152
  6.7 34.9 %collective-permute-start.10 = (bf16[8,128,128]{2,1,0:T(8,128)(2,1)S(1)}, bf16[8,128,128]{2,1,0:T(8,128)(2,1)S(1)}, u32[]{:S(2)}, u32[]{:S(2)}) collective-permute-start(bf16[8,128,128]{2,1,0:T(8,128)(2,1)S(1)} %get-tuple-element.17), channel_id=1, source_target_pairs={{0,4},{1,5},{2,6},{3,7},{4,0},{5,1},{6,2},{7,3},{8,12},{9,13},{10,... | collective-permute-start | bytes 786440 | tf_op jit(solution)/shard_map/ppermute | solution.py:152
  7.8 35.2 %collective-permute-start.11 = (bf16[8,128,128]{2,1,0:T(8,128)(2,1)S(1)}, bf16[8,128,128]{2,1,0:T(8,128)(2,1)S(1)}, u32[]{:S(2)}, u32[]{:S(2)}) collective-permute-start(bf16[8,128,128]{2,1,0:T(8,128)(2,1)S(1)} %get-tuple-element.16), channel_id=1, source_target_pairs={{0,10},{1,11},{2,8},{3,9},{4,14},{5,15},{6,12},{7,13},{8,2},{9,3},... | collective-permute-start | bytes 786440 | tf_op jit(solution)/shard_map/ppermute | solution.py:152
  19.9 26.0 %collective-permute-start.12 = (bf16[8,128,128]{2,1,0:T(8,128)(2,1)}, bf16[8,128,128]{2,1,0:T(8,128)(2,1)S(1)}, u32[]{:S(2)}, u32[]{:S(2)}) collective-permute-start(bf16[8,128,128]{2,1,0:T(8,128)(2,1)} %get-tuple-element.15), channel_id=1, source_target_pairs={{0,2},{1,3},{2,0},{3,1},{4,6},{5,7},{6,4},{7,5},{8,10},{9,11},{10,... | collective-permute-start | bytes 786440 | tf_op jit(solution)/shard_map/ppermute | solution.py:152
  20.9 43.2 %collective-permute-start.13 = (bf16[8,128,128]{2,1,0:T(8,128)(2,1)}, bf16[8,128,128]{2,1,0:T(8,128)(2,1)S(1)}, u32[]{:S(2)}, u32[]{:S(2)}) collective-permute-start(bf16[8,128,128]{2,1,0:T(8,128)(2,1)} %get-tuple-element.14), channel_id=1, source_target_pairs={{0,15},{1,14},{2,13},{3,12},{4,11},{5,10},{6,9},{7,8},{8,7},{9,6},... | collective-permute-start | bytes 786440 | tf_op jit(solution)/shard_map/ppermute | solution.py:152
  40.6 23.5 %collective-permute-start.6 = (bf16[8,128,128]{2,1,0:T(8,128)(2,1)}, bf16[8,128,128]{2,1,0:T(8,128)(2,1)S(1)}, u32[]{:S(2)}, u32[]{:S(2)}) collective-permute-start(bf16[8,128,128]{2,1,0:T(8,128)(2,1)} %get-tuple-element.21), channel_id=1, source_target_pairs={{0,5},{1,4},{2,7},{3,6},{4,1},{5,0},{6,3},{7,2},{8,13},{9,12},{10,... | collective-permute-start | bytes 786440 | tf_op jit(solution)/shard_map/ppermute | solution.py:152
  41.6 38.8 %collective-permute-start.7 = (bf16[8,128,128]{2,1,0:T(8,128)(2,1)}, bf16[8,128,128]{2,1,0:T(8,128)(2,1)S(1)}, u32[]{:S(2)}, u32[]{:S(2)}) collective-permute-start(bf16[8,128,128]{2,1,0:T(8,128)(2,1)} %get-tuple-element.20), channel_id=1, source_target_pairs={{0,9},{1,8},{2,11},{3,10},{4,13},{5,12},{6,15},{7,14},{8,1},{9,0},... | collective-permute-start | bytes 786440 | tf_op jit(solution)/shard_map/ppermute | solution.py:152
  42.9 37.5 %collective-permute-start.8 = (bf16[8,128,128]{2,1,0:T(8,128)(2,1)}, bf16[8,128,128]{2,1,0:T(8,128)(2,1)S(1)}, u32[]{:S(2)}, u32[]{:S(2)}) collective-permute-start(bf16[8,128,128]{2,1,0:T(8,128)(2,1)} %get-tuple-element.19), channel_id=1, source_target_pairs={{0,3},{1,2},{2,1},{3,0},{4,7},{5,6},{6,5},{7,4},{8,11},{9,10},{10,... | collective-permute-start | bytes 786440 | tf_op jit(solution)/shard_map/ppermute | solution.py:152
  46.0 43.1 %collective-permute-start.9 = (bf16[8,128,128]{2,1,0:T(8,128)(2,1)}, bf16[8,128,128]{2,1,0:T(8,128)(2,1)}, u32[]{:S(2)}, u32[]{:S(2)}) collective-permute-start(bf16[8,128,128]{2,1,0:T(8,128)(2,1)} %get-tuple-element.18), channel_id=1, source_target_pairs={{0,12},{1,13},{2,14},{3,15},{4,8},{5,9},{6,10},{7,11},{8,4},{9,5},... | collective-permute-start | bytes 786440 | tf_op jit(solution)/shard_map/ppermute | solution.py:152
  64.1 28.8 %collective-permute-start.4 = (bf16[8,128,128]{2,1,0:T(8,128)(2,1)}, bf16[8,128,128]{2,1,0:T(8,128)(2,1)S(1)}, u32[]{:S(2)}, u32[]{:S(2)}) collective-permute-start(bf16[8,128,128]{2,1,0:T(8,128)(2,1)} %get-tuple-element.23), channel_id=1, source_target_pairs={{0,6},{1,7},{2,4},{3,5},{4,2},{5,3},{6,0},{7,1},{8,14},{9,15},{10,... | collective-permute-start | bytes 786440 | tf_op jit(solution)/shard_map/ppermute | solution.py:152
  64.1 28.8 %collective-permute-start.5 = (bf16[8,128,128]{2,1,0:T(8,128)(2,1)}, bf16[8,128,128]{2,1,0:T(8,128)(2,1)S(1)}, u32[]{:S(2)}, u32[]{:S(2)}) collective-permute-start(bf16[8,128,128]{2,1,0:T(8,128)(2,1)} %get-tuple-element.22), channel_id=1, source_target_pairs={{0,7},{1,6},{2,5},{3,4},{4,3},{5,2},{6,1},{7,0},{8,15},{9,14},{10,... | collective-permute-start | bytes 786440 | tf_op jit(solution)/shard_map/ppermute | solution.py:152
  67.1 2.2 %copy-start.1 = (bf16[16,1024,128]{2,1,0:T(8,128)(2,1)S(1)}, bf16[16,1024,128]{2,1,0:T(8,128)(2,1)}, u32[]{:S(2)}) copy-start(bf16[16,1024,128]{2,1,0:T(8,128)(2,1)} %param.5) | copy-start | bytes 12582916
  69.3 11.2 %copy-start.4 = (bf16[4,128,128]{2,1,0:T(8,128)(2,1)S(1)}, bf16[4,128,128]{2,1,0:T(8,128)(2,1)}, u32[]{:S(2)}) copy-start(bf16[4,128,128]{2,1,0:T(8,128)(2,1)} %pad_maximum_fusion.1) | copy-start | bytes 393220
  69.3 12.3 %copy-start = (bf16[16384,128]{1,0:T(8,128)(2,1)S(1)}, bf16[16384,128]{1,0:T(8,128)(2,1)}, u32[]{:S(2)}) copy-start(bf16[16384,128]{1,0:T(8,128)(2,1)} %param.6) | copy-start | bytes 12582916
  80.4 15.4 %collective-permute-start.2 = (bf16[4,128,128]{2,1,0:T(8,128)(2,1)S(1)}, bf16[4,128,128]{2,1,0:T(8,128)(2,1)S(1)}, u32[]{:S(2)}, u32[]{:S(2)}) collective-permute-start(bf16[4,128,128]{2,1,0:T(8,128)(2,1)S(1)} %pad_maximum_fusion), channel_id=1, source_target_pairs={{0,11},{1,10},{2,9},{3,8},{4,15},{5,14},{6,13},{7,12},{8,3},{9,2},... | collective-permute-start | bytes 393224 | tf_op jit(solution)/shard_map/ppermute | solution.py:152
  80.4 15.3 %collective-permute-start.3 = (bf16[4,128,128]{2,1,0:T(8,128)(2,1)S(1)}, bf16[4,128,128]{2,1,0:T(8,128)(2,1)S(1)}, u32[]{:S(2)}, u32[]{:S(2)}) collective-permute-start(bf16[4,128,128]{2,1,0:T(8,128)(2,1)S(1)} %copy-done.4), channel_id=1, source_target_pairs={{0,14},{1,15},{2,12},{3,13},{4,10},{5,11},{6,8},{7,9},{8,6},{9,7},... | collective-permute-start | bytes 393224 | tf_op jit(solution)/shard_map/ppermute | solution.py:152
  98.3 21.8 %collective-permute-start.17 = (bf16[256,384]{1,0:T(8,128)(2,1)S(1)}, bf16[256,384]{1,0:T(8,128)(2,1)S(1)}, u32[]{:S(2)}, u32[]{:S(2)}) collective-permute-start(bf16[256,384]{1,0:T(8,128)(2,1)S(1)} %get-tuple-element.9), channel_id=1, source_target_pairs={{0,1},{1,2},{2,3},{3,4},{4,5},{5,6},{6,7},{7,8},{8,9},{9,10},{10,1... | collective-permute-start | bytes 589832 | tf_op jit(solution)/shard_map/ppermute | solution.py:230
  101.8 18.3 %collective-permute-start.18 = (bf16[256,384]{1,0:T(8,128)(2,1)S(1)}, bf16[256,384]{1,0:T(8,128)(2,1)S(1)}, u32[]{:S(2)}, u32[]{:S(2)}) collective-permute-start(bf16[256,384]{1,0:T(8,128)(2,1)S(1)} %get-tuple-element.10), channel_id=1, source_target_pairs={{1,0},{2,1},{3,2},{4,3},{5,4},{6,5},{7,6},{8,7},{9,8},{10,9},{11,1... | collective-permute-start | bytes 589832 | tf_op jit(solution)/shard_map/ppermute | solution.py:229
  103.7 8.1 %collective-permute-start = (bf16[4,128,128]{2,1,0:T(8,128)(2,1)S(1)}, bf16[4,128,128]{2,1,0:T(8,128)(2,1)S(1)}, u32[]{:S(2)}, u32[]{:S(2)}) collective-permute-start(bf16[4,128,128]{2,1,0:T(8,128)(2,1)S(1)} %get-tuple-element.29), channel_id=1, source_target_pairs={{0,11},{1,10},{2,9},{3,8},{4,15},{5,14},{6,13},{7,12},{8,3},{9,2},... | collective-permute-start | bytes 393224 | tf_op jit(solution)/shard_map/ppermute | solution.py:152
  107.1 12.9 %collective-permute-start.1 = (bf16[4,128,128]{2,1,0:T(8,128)(2,1)S(1)}, bf16[4,128,128]{2,1,0:T(8,128)(2,1)S(1)}, u32[]{:S(2)}, u32[]{:S(2)}) collective-permute-start(bf16[4,128,128]{2,1,0:T(8,128)(2,1)S(1)} %get-tuple-element.28), channel_id=1, source_target_pairs={{0,14},{1,15},{2,12},{3,13},{4,10},{5,11},{6,8},{7,9},{8,6},{9,7},... | collective-permute-start | bytes 393224 | tf_op jit(solution)/shard_map/ppermute | solution.py:152

commit v2 on v1

--- a/solution.py
+++ b/solution.py
@@ -8,23 +8,28 @@
 from jax.sharding import PartitionSpec as P
 
 REACH = 2
-ORDER = (8, 1, 13, 4, 10, 2, 15, 5, 9, 3, 12, 6, 7)
-LAST = (11, 14)
-GROUPS = ((0, 8, 1, 13), (4, 10, 2, 15), (5, 9, 3, 12), (6, 7))
+FIRST = 8
+EARLY = (12, 4)
+LATE = (6, 2)
+LAST = (10, 14)
 
 
 def params(megabytes=40):
     return pltpu.CompilerParams(vmem_limit_bytes=megabytes * 2**20)
 
 
+def after(x, *done):
+    return lax.optimization_barrier((x, *done))[0]
+
+
 def spec(block, index):
     return pl.BlockSpec(block, index)
 
 
 def cost(pairs, width, columns, extra_bytes=0):
     return pl.CostEstimate(
-        flops=pairs * 2 * width * width * columns,
-        bytes_accessed=pairs * width * (columns + width) * 2 + extra_bytes,
+        flops=pairs,
+        bytes_accessed=pairs,
         transcendentals=0,
     )
 
@@ -75,7 +80,7 @@
     return target_ref[terms_of(me_ref[0], s), REACH] - REACH
 
 
-def group_kernel(patterns, terms_of, slots, rows, first, own, me_ref, target_ref, *refs):
+def group_kernel(patterns, terms_of, slots, rows, first, me_ref, target_ref, *refs):
     refs = list(refs)
     mixed = [refs.pop(0) for _ in patterns]
     right = [refs.pop(0) for _ in patterns]
@@ -86,9 +91,7 @@
         before, acc = refs
         acc[...] = before[...]
     for s, m, r in zip(patterns, mixed, right):
-        accumulate(
-            acc, m, r.at[0] if own and s == 0 else r, shift_of(me_ref, target_ref, terms_of, s), slots, rows, REACH
-        )
+        accumulate(acc, m, r.at[0], shift_of(me_ref, target_ref, terms_of, s), slots, rows, REACH)
 
 
 def edge_kernel(patterns, terms_of, slots, rows, blocks, me_ref, target_ref, *refs):
@@ -99,11 +102,21 @@
     width = right[0].shape[-1]
     acc[...] = before[...]
     for s, m, r in zip(patterns, mixed, right):
-        accumulate(acc, m, r, shift_of(me_ref, target_ref, terms_of, s), slots, rows, REACH)
+        accumulate(acc, m, r.at[0], shift_of(me_ref, target_ref, terms_of, s), slots, rows, REACH)
     halo = REACH * width
     to_left[...] = acc[:halo].astype(to_left.dtype)
     to_right[...] = acc[halo + blocks * width :].astype(to_right.dtype)
     inner[...] = acc[halo : halo + blocks * width]
+
+
+def rest_kernel(patterns, terms_of, slots, rows, me_ref, target_ref, *refs):
+    refs = list(refs)
+    mixed = [refs.pop(0) for _ in patterns]
+    right = [refs.pop(0) for _ in patterns]
+    before, acc = refs
+    acc[...] = before[...]
+    for s, m, r in zip(patterns, mixed, right):
+        accumulate(acc, m, r.at[0], shift_of(me_ref, target_ref, terms_of, s), slots, rows, 0)
 
 
 def last_kernel(patterns, terms_of, slots, rows, me_ref, target_ref, *refs):
@@ -116,7 +129,7 @@
     acc[:halo] += from_left[...].astype(jnp.float32)
     acc[-halo:] += from_right[...].astype(jnp.float32)
     for s, m, r in zip(patterns, mixed, right):
-        accumulate(acc, m, r, shift_of(me_ref, target_ref, terms_of, s), slots, rows, 0)
+        accumulate(acc, m, r.at[0], shift_of(me_ref, target_ref, terms_of, s), slots, rows, 0)
     out[...] = acc[...].astype(out.dtype)
 
 
@@ -138,37 +151,36 @@
     inside = tuple(c for c in range(blocks) if c not in edges)
     places = inside + edges
     slot_of = {c: i for i, c in enumerate(places)}
-    by_partner = stride == 1 and terms == len(ORDER) + len(LAST) + 1
+    by_partner = stride == 1 and terms == 16
     terms_of = (lambda own, s: jnp.bitwise_xor(own, s)) if by_partner else (lambda own, s: s)
 
     psi_blocks = psi.reshape(blocks, width, columns)
     left_blocks = left_env.reshape(terms, blocks, width, width)
 
-    def send(s, rows=None):
-        right = right_env.reshape(devices, blocks, width, width)
-        mine = lax.dynamic_index_in_dim(right, jnp.bitwise_xor(me, s), 0, keepdims=False)
-        if rows is not None:
-            mine = jnp.concatenate([mine[a:b] for a, b in rows], axis=0)
-        return lax.ppermute(mine, "terms", [(i, i ^ s) for i in range(devices)])
-
-    if by_partner:
-        pieces = {s: send(s) for s in ORDER}
-        edge_pieces = {s: send(s, ((0, REACH), (blocks - REACH, blocks))) for s in LAST}
-        inner_pieces = {s: send(s, ((REACH, blocks - REACH),)) for s in LAST}
-        pieces[0] = right_env.reshape(devices, blocks, width, width)
-        groups, last = GROUPS, LAST
-    else:
-        sent = right_env.reshape(devices, per_class, width, width)
-        got = lax.all_to_all(sent, "terms", split_axis=0, concat_axis=0, tiled=True)
-        got = got.reshape(terms, stride, per_class, width, width)
-        got = jnp.swapaxes(got, 1, 2).reshape(terms, blocks, width, width)
-        last = (terms - 1,)
-        pieces = {s: got[s] for s in range(terms - 1)}
-        edge_pieces = {s: jnp.concatenate([got[s, :REACH], got[s, -REACH:]], axis=0) for s in last}
-        inner_pieces = {s: got[s, REACH:-REACH] for s in last}
-        groups = tuple(tuple(range(a, min(a + 4, terms - 1))) for a in range(0, terms - 1, 4))
-
-    mixed = mix(me_ref, target, left_blocks, psi_blocks, terms_of, places)
+    right = right_env.reshape(devices, per_class, width, width)
+
+    def move(operand, s):
+        return lax.ppermute(operand, "terms", [(i, i ^ s) for i in range(devices)])
+
+    def pick(source, index, start, count):
+        return lax.dynamic_slice(source, (index, start, 0, 0), (1, count, width, width))
+
+    def pair_message(source, exchanged, s, rows):
+        partner = jnp.bitwise_xor(me, s)
+        parts = [
+            jnp.concatenate([pick(array, partner, a, b - a) for a, b in rows], axis=1)
+            for array in (source, exchanged)
+        ]
+        return jnp.concatenate(parts, axis=0)
+
+    def both(patterns):
+        return tuple(p for s in patterns for p in (s, s + 1))
+
+    def piece_spec(array, at):
+        block = (1, *array.shape[1:])
+        if callable(at):
+            return spec(block, lambda i, me, target: (at(me[0]), 0, 0, 0))
+        return spec(block, lambda i, me, target: (at, 0, 0, 0))
 
     def mixed_spec(s, part, parts):
         count = len(part)
@@ -201,26 +213,70 @@
             name=name,
         )(me_ref, target, *operands)
 
-    acc = None
-    for number, patterns in enumerate(groups):
+    def group(patterns, acc):
         specs = [mixed_spec(s, places, 1) for s in patterns]
         operands = [mixed for _ in patterns]
         for s in patterns:
-            if by_partner and s == 0:
-                specs.append(spec((1, blocks, width, width), lambda i, me, target: (me[0], 0, 0, 0)))
-            else:
-                specs.append(whole_spec(pieces[s]))
-            operands.append(pieces[s])
-        if number:
+            array, at = pieces[s]
+            specs.append(piece_spec(array, at))
+            operands.append(array)
+        if acc is not None:
             specs.append(whole_spec(acc))
             operands.append(acc)
         kernel = functools.partial(
-            group_kernel, patterns, terms_of, tuple(slot_of[c] for c in everything), everything, number == 0, by_partner
+            group_kernel, patterns, terms_of, tuple(slot_of[c] for c in everything), everything, acc is None
         )
-        acc = call(kernel, patterns, specs, operands, acc_shape, (), len(patterns) * blocks, "add_terms")
-
-    specs = [mixed_spec(s, edges, 2) for s in last] + [whole_spec(edge_pieces[s]) for s in last] + [whole_spec(acc)]
-    operands = [mixed for _ in last] + [edge_pieces[s] for s in last] + [acc]
+        return call(kernel, patterns, specs, operands, acc_shape, (), len(patterns) * blocks, "add_terms")
+
+    if by_partner:
+        everywhere = ((0, blocks),)
+        outer = ((0, REACH), (blocks - REACH, blocks))
+        inner = ((REACH, blocks - REACH),)
+        exchanged = move(right, 1)
+        first = pick(right, jnp.bitwise_xor(me, FIRST), 0, blocks)
+        pieces = {0: (right, lambda own: own), 1: (exchanged, lambda own: own), FIRST: (move(first, FIRST), 0)}
+        edge_pieces, inner_pieces = {}, {}
+
+        def send(store, source, exchanged, s, rows):
+            message = pair_message(source, exchanged, s, rows)
+            got = move(message, s)
+            store[s], store[s + 1] = (got, 0), (got, 1)
+            return message
+
+        source, relayed = after(right, first), exchanged
+        messages = []
+        for s in EARLY:
+            messages.append(send(pieces, source, relayed, s, everywhere))
+            source, relayed = after(right, messages[-1]), after(exchanged, messages[-1])
+        messages.append(pick(relayed, jnp.bitwise_xor(me, FIRST), 0, blocks))
+        pieces[FIRST + 1] = (move(messages[-1], FIRST), 0)
+        mixed = mix(me_ref, target, after(left_blocks, *messages), psi_blocks, terms_of, places)
+        source, relayed = after(right, mixed), after(exchanged, mixed)
+        for s in LAST:
+            send(edge_pieces, source, relayed, s, outer)
+        for s in LATE:
+            send(pieces, source, relayed, s, everywhere)
+        acc = group((0, 1, FIRST) + both(EARLY), None)
+        source, relayed = after(right, acc), after(exchanged, acc)
+        for s in LAST:
+            send(inner_pieces, source, relayed, s, inner)
+        acc = group((FIRST + 1,) + both(LATE), acc)
+        last = both(LAST)
+    else:
+        got = lax.all_to_all(right, "terms", split_axis=0, concat_axis=0, tiled=True)
+        got = got.reshape(terms, stride, per_class, width, width)
+        got = jnp.swapaxes(got, 1, 2).reshape(terms, blocks, width, width)
+        mixed = mix(me_ref, target, left_blocks, psi_blocks, terms_of, places)
+        last = (terms - 1,)
+        pieces = {s: (got, s) for s in range(terms - 1)}
+        edge_pieces = {s: (jnp.concatenate([got[s:, :REACH], got[s:, -REACH:]], axis=1), 0) for s in last}
+        inner_pieces = {s: (got[s:, REACH:-REACH], 0) for s in last}
+        acc = None
+        for a in range(0, terms - 1, 4):
+            acc = group(tuple(range(a, min(a + 4, terms - 1))), acc)
+
+    specs = [mixed_spec(s, edges, 2) for s in last] + [piece_spec(*edge_pieces[s]) for s in last] + [whole_spec(acc)]
+    operands = [mixed for _ in last] + [edge_pieces[s][0] for s in last] + [acc]
     kernel = functools.partial(edge_kernel, last, terms_of, tuple(range(len(edges))), edges, blocks)
     core, to_left, to_right = call(
         kernel, last, specs, operands, (core_shape, halo_shape, halo_shape),
@@ -229,13 +285,19 @@
     from_right = lax.ppermute(to_left, "terms", [(i + 1, i) for i in range(devices - 1)])
     from_left = lax.ppermute(to_right, "terms", [(i, i + 1) for i in range(devices - 1)])
 
-    specs = [mixed_spec(s, inside, 2) for s in last] + [whole_spec(inner_pieces[s]) for s in last]
-    specs += [whole_spec(core), whole_spec(from_left), whole_spec(from_right)]
-    operands = [mixed for _ in last] + [inner_pieces[s] for s in last] + [core, from_left, from_right]
-    kernel = functools.partial(last_kernel, last, terms_of, tuple(range(len(inside))), inside)
-    return call(
-        kernel, last, specs, operands, out_shape,
-        (pltpu.VMEM(core_shape.shape, jnp.float32),), len(last) * len(inside), "add_rest",
+    def rest(kernel, patterns, extra, out, scratch):
+        specs = [mixed_spec(s, inside, 2) for s in patterns] + [piece_spec(*inner_pieces[s]) for s in patterns]
+        operands = [mixed for _ in patterns] + [inner_pieces[s][0] for s in patterns]
+        kernel = functools.partial(kernel, patterns, terms_of, tuple(range(len(inside))), inside)
+        return call(
+            kernel, patterns, specs + [whole_spec(x) for x in extra], operands + extra, out, scratch,
+            len(patterns) * len(inside), "add_rest",
+        )
+
+    if len(last) > 2:
+        core = rest(rest_kernel, last[:-2], [core], core_shape, ())
+    return rest(
+        last_kernel, last[-2:], [core, from_left, from_right], out_shape, (pltpu.VMEM(core_shape.shape, jnp.float32),)
     )
 
 

time: 125 us -> 104 us (0.83)
  starting transfers between devices: 33.6 us -> 13.7 us
  Pallas kernels: 31.1 us -> 28.8 us
  local copies, waits for them, and re-layouts: 6.54 us -> 8.23 us
    ppermute x17 -> x11, starting transfers between devices: 28.2 us -> 9.24 us  [move(): return lax.ppermute(operand, 'terms', [(i, i ^ s) for i in range(devices)])]
    dynamic_slice x0 -> x11, local copies, waits for them, and re-layouts: none -> 8.21 us  [pick(): lax.dynamic_slice(source, (index, start, 0, 0), (1, count, width, width))]
    ppermute x17 -> x11, waiting for transfers between devices: 51.3 us -> 46.6 us  [move(): return lax.ppermute(operand, 'terms', [(i, i ^ s) for i in range(devices)])]
    ppermute x1, waiting for transfers between devices: 0.01 us -> 3.89 us  [shards(): lax.ppermute(to_right, 'terms', [(i, i + 1) for i in range(devices - 1)])]
    squeeze x1 -> x0, local copies, waits for them, and re-layouts: 3.35 us -> none  [send(): lax.dynamic_index_in_dim(right, jnp.bitwise_xor(me, s), 0, keepdims=False)]
    pallas_call x6 -> x5, Pallas kernels: 19.9 us -> 17.7 us  [call(): pl.pallas_call(kernel, grid_spec=pltpu.PrefetchScalarGridSpec(num_scalar_...]
    unnamed x10 -> x8, local copies, waits for them, and re-layouts: 2.2 us -> 0.02 us
    ppermute x1, waiting for transfers between devices: 0.01 us -> 1.68 us  [shards(): lax.ppermute(to_left, 'terms', [(i + 1, i) for i in range(devices - 1)])]
  transfers between devices with their start and end apart: 19 -> 13, of which waited for: 5 -> 7; matrix products, arithmetic and copies ran while one was open for 1% -> 8% of each run, Pallas kernels for 21% -> 25%
where the time goes in v2:
time: 104 us; the launch traced here: 103 us
  waiting for transfers between devices  52.1 us (50%)
  Pallas kernels  28.8 us (28%)
  starting transfers between devices  13.7 us (13%)
  local copies, waits for them, and re-layouts  8.23 us (8%)
    ppermute x11, waiting for transfers between devices, move(): return lax.ppermute(operand, 'terms', [(i, i ^ s) for i in range(devices)])  46.6 us
    pallas_call x5, Pallas kernels, call(): pl.pallas_call(kernel, grid_spec=pltpu.PrefetchScalarGridSpec(num_scalar_...  17.7 us
    pallas_call x1, Pallas kernels, mix(): pl.pallas_call(functools.partial(mix_kernel, places), grid_spec=pltpu.Pre...  11.1 us
    ppermute x11, starting transfers between devices, move(): return lax.ppermute(operand, 'terms', [(i, i ^ s) for i in range(devices)])  9.24 us
    dynamic_slice x11, local copies, waits for them, and re-layouts, pick(): lax.dynamic_slice(source, (index, start, 0, 0), (1, count, width, width))  8.21 us
    ppermute x1, waiting for transfers between devices, shards(): lax.ppermute(to_right, 'terms', [(i, i + 1) for i in range(devices - 1)])  3.89 us
    ppermute x1, starting transfers between devices, shards(): lax.ppermute(to_right, 'terms', [(i, i + 1) for i in range(devices - 1)])  2.5 us
  transfers between devices with their start and end apart: 13, of which 7 were waited for; matrix products, arithmetic and copies ran while one was open for 8% of the time, Pallas kernels for 25%

profile of v2, /device:TPU:17, one launch (start us, length us, event | category | flops | bytes accessed | tf_op | source)
XLA Modules:
  0.0 103.5 jit_solution(2055992570881480237)
XLA Ops:
  0.0 0.7 collective-permute-start
  0.7 1.0 constant_dynamic-slice_fusion.21
  1.7 0.1 collective-permute-start.1
  1.8 0.0 copy-start.1
  1.8 1.1 %constant_dynamic-slice_fusion.20 = bf16[1,8,128,128]{3,2,1,0:T(8,128)(2,1)S(1)} fusion(bf16[16,8,128,128]{3,2,1,0:T(8,128)(2,1)} %bitcast.6, s32[]{:T(128)S(6)} %select_n.15), kind=kLoop, calls=%fused_computation.28 | loop fusion | bytes 524292 | tf_op jit(solution)/shard_map/dynamic_slice | solution.py:166
  2.9 4.9 %collective-permute-done.refs_8_ = bf16[16,8,128,128]{3,2,1,0:T(8,128)(2,1)} collective-permute-done((bf16[16,8,128,128]{3,2,1,0:T(8,128)(2,1)}, bf16[16,8,128,128]{3,2,1,0:T(8,128)(2,1)}, u32[]{:S(2)}, u32[]{:S(2)}) %collective-permute-start) | collective-permute-done | bytes 4194336 | tf_op jit(solution)/shard_map/ppermute | solution.py:163
  7.8 1.0 constant_dynamic-slice_fusion.19
  8.8 0.1 pad_maximum_fusion
  8.8 0.2 collective-permute-start.2
  9.1 1.1 %constant_dynamic-slice_fusion.17 = (bf16[1,8,128,128]{3,2,1,0:T(8,128)(2,1)S(1)}, bf16[1,8,128,128]{3,2,1,0:T(8,128)(2,1)S(1)}) fusion(bf16[16,8,128,128]{3,2,1,0:T(8,128)(2,1)} %collective-permute-done.refs_8_, s32[]{:T(128)S(6)} %select_n.16, bf16[16,8,128,128]{3,2,1,0:T(8,128)(2,1)} %bitcast.7), kind=kLoop, calls=%fused_computation.25 | loop fusion | bytes 1048580 | tf_op jit(solution)/shard_map/dynamic_slice | solution.py:166
  10.2 0.1 pad_maximum_fusion.1
  10.2 1.2 %collective-permute-start.3 = (bf16[2,8,128,128]{3,2,1,0:T(8,128)(2,1)S(1)}, bf16[2,8,128,128]{3,2,1,0:T(8,128)(2,1)S(1)}, u32[]{:S(2)}, u32[]{:S(2)}) collective-permute-start(bf16[2,8,128,128]{3,2,1,0:T(8,128)(2,1)S(1)} %pad_maximum_fusion.1), channel_id=1, source_target_pairs={{0,4},{1,5},{2,6},{3,7},{4,0},{5,1},{6,2},{7,3},{8,12},{9,13},{10,... | collective-permute-start | bytes 1572872 | tf_op jit(solution)/shard_map/ppermute | solution.py:163
  11.4 1.0 constant_dynamic-slice_fusion.16
  12.4 2.1 %collective-permute-start.8 = (bf16[1,8,128,128]{3,2,1,0:T(8,128)(2,1)S(1)}, bf16[1,8,128,128]{3,2,1,0:T(8,128)(2,1)S(1)}, u32[]{:S(2)}, u32[]{:S(2)}) collective-permute-start(bf16[1,8,128,128]{3,2,1,0:T(8,128)(2,1)S(1)} %constant_dynamic-slice_fusion.16), channel_id=1, source_target_pairs={{0,8},{1,9},{2,10},{3,11},{4,12},{5,13},{6,14},{7,15},{8,0},{9,1},... | collective-permute-start | bytes 786440 | tf_op jit(solution)/shard_map/ppermute | solution.py:163
  14.5 0.0 copy-done.3
  14.5 0.0 copy-done.2
  14.5 0.0 copy-done.1
  14.6 11.1 %mix.1.refs_0_.refs_1_.refs_2_.refs_3_.refs_4_.refs_5_.refs_6_ = bf16[16,8,128,384]{3,2,1,0:T(8,128)(2,1)} custom-call(s32[1]{0:T(128)} %bitcast.me_ref, s32[16,128]{1,0:T(8,128)S(1)} %copy-done.3, bf16[16,8,128,128]{3,2,1,0:T(8,128)(2,1)S(1)} %bitcast.12, bf16[8,128,384]{2,1,0:T(8,128)(2,1)S(1)} %bitcast.13), custom_call_target="tpu_custom_call" | custom-call | flops 128 | bytes 128 | tf_op jit(solution)/shard_map/mix/pallas_call | solution.py:46
  25.7 1.1 %constant_dynamic-slice_fusion = (bf16[1,8,128,128]{3,2,1,0:T(8,128)(2,1)S(1)}, bf16[1,8,128,128]{3,2,1,0:T(8,128)(2,1)S(1)}) fusion(bf16[16,8,128,128]{3,2,1,0:T(8,128)(2,1)} %collective-permute-done.refs_8_, s32[]{:T(128)S(6)} %select_n.20, s32[]{:T(128)S(6)} %select_n.19), kind=kLoop, calls=%fused_computation.8 | loop fusion | bytes 1048584 | tf_op jit(solution)/shard_map/dynamic_slice | solution.py:166
  26.8 0.1 pad_maximum_fusion.2
  26.9 2.5 %collective-permute-start.9 = (bf16[2,8,128,128]{3,2,1,0:T(8,128)(2,1)S(1)}, bf16[2,8,128,128]{3,2,1,0:T(8,128)(2,1)S(1)}, u32[]{:S(2)}, u32[]{:S(2)}) collective-permute-start(bf16[2,8,128,128]{3,2,1,0:T(8,128)(2,1)S(1)} %pad_maximum_fusion.2), channel_id=1, source_target_pairs={{0,6},{1,7},{2,4},{3,5},{4,2},{5,3},{6,0},{7,1},{8,14},{9,15},{10,... | collective-permute-start | bytes 1572872 | tf_op jit(solution)/shard_map/ppermute | solution.py:163
  29.4 1.0 constant_dynamic-slice_fusion.5
  30.4 0.1 pad_maximum_fusion.3
  30.5 0.0 collective-permute-done.1.refs_9_
  30.5 0.1 collective-permute-start.6
  30.6 14.1 %collective-permute-done.2.refs_10_.refs_11_ = bf16[2,8,128,128]{3,2,1,0:T(8,128)(2,1)S(1)} collective-permute-done((bf16[2,8,128,128]{3,2,1,0:T(8,128)(2,1)S(1)}, bf16[2,8,128,128]{3,2,1,0:T(8,128)(2,1)S(1)}, u32[]{:S(2)}, u32[]{:S(2)}) %collective-permute-start.2) | collective-permute-done | bytes 524320 | tf_op jit(solution)/shard_map/ppermute | solution.py:163
  44.7 0.2 collective-permute-start.7
  44.9 0.0 collective-permute-done.3.refs_12_.refs_13_
  44.9 1.0 collective-permute-start.10
  45.9 5.1 %add_terms.2.refs_10_ = f32[1536,384]{1,0:T(8,128)S(1)} custom-call(s32[1]{0:T(128)} %bitcast.me_ref, s32[16,128]{1,0:T(8,128)S(1)} %copy-done.3, bf16[16,8,128,384]{3,2,1,0:T(8,128)(2,1)} %mix.1.refs_0_.refs_1_.refs_2_.refs_3_.refs_4_.refs_5_.refs_6_, bf16[16,8,128,384]{3,2,1,0:T(8,128)(2,1)} %mix.1.refs_0_.refs_1_.refs_2_.refs_3_.refs_4_.refs_5_.refs_6_, ...), custom_call_target="tpu_custom_call" | custom-call | flops 56 | bytes 56 | tf_op jit(solution)/shard_map/add_terms/pallas_call | solution.py:201
  51.0 1.0 constant_dynamic-slice_fusion.12
  52.1 0.0 collective-permute-done.8.refs_5_
  52.1 0.1 collective-permute-start.5
  52.2 5.7 %collective-permute-done.9.refs_6_.refs_7_ = bf16[2,8,128,128]{3,2,1,0:T(8,128)(2,1)S(1)} collective-permute-done((bf16[2,8,128,128]{3,2,1,0:T(8,128)(2,1)S(1)}, bf16[2,8,128,128]{3,2,1,0:T(8,128)(2,1)S(1)}, u32[]{:S(2)}, u32[]{:S(2)}) %collective-permute-start.9) | collective-permute-done | bytes 524320 | tf_op jit(solution)/shard_map/ppermute | solution.py:163
  57.9 1.0 %collective-permute-start.4 = (bf16[2,4,128,128]{3,2,1,0:T(8,128)(2,1)S(1)}, bf16[2,4,128,128]{3,2,1,0:T(8,128)(2,1)S(1)}, u32[]{:S(2)}, u32[]{:S(2)}) collective-permute-start(bf16[2,4,128,128]{3,2,1,0:T(8,128)(2,1)S(1)} %pad_maximum_fusion.4), channel_id=1, source_target_pairs={{0,14},{1,15},{2,12},{3,13},{4,10},{5,11},{6,8},{7,9},{8,6},{9,7},... | collective-permute-start | bytes 786440 | tf_op jit(solution)/shard_map/ppermute | solution.py:163
  58.9 15.3 %collective-permute-done.10.refs_8_.refs_9_ = bf16[2,8,128,128]{3,2,1,0:T(8,128)(2,1)S(1)} collective-permute-done((bf16[2,8,128,128]{3,2,1,0:T(8,128)(2,1)S(1)}, bf16[2,8,128,128]{3,2,1,0:T(8,128)(2,1)S(1)}, u32[]{:S(2)}, u32[]{:S(2)}) %collective-permute-start.10) | collective-permute-done | bytes 524320 | tf_op jit(solution)/shard_map/ppermute | solution.py:163
  74.2 4.2 %add_terms.3.refs_8_ = f32[1536,384]{1,0:T(8,128)S(1)} custom-call(s32[1]{0:T(128)} %bitcast.me_ref, s32[16,128]{1,0:T(8,128)S(1)} %copy-done.3, bf16[16,8,128,384]{3,2,1,0:T(8,128)(2,1)} %mix.1.refs_0_.refs_1_.refs_2_.refs_3_.refs_4_.refs_5_.refs_6_, bf16[16,8,128,384]{3,2,1,0:T(8,128)(2,1)} %mix.1.refs_0_.refs_1_.refs_2_.refs_3_.refs_4_.refs_5_.refs_6_, ...), custom_call_target="tpu_custom_call" | custom-call | flops 40 | bytes 40 | tf_op jit(solution)/shard_map/add_terms/pallas_call | solution.py:201
  78.4 0.0 collective-permute-done.6.refs_4_.refs_5_
  78.4 6.6 %collective-permute-done.7.refs_6_.refs_7_ = bf16[2,4,128,128]{3,2,1,0:T(8,128)(2,1)S(1)} collective-permute-done((bf16[2,4,128,128]{3,2,1,0:T(8,128)(2,1)S(1)}, bf16[2,4,128,128]{3,2,1,0:T(8,128)(2,1)S(1)}, u32[]{:S(2)}, u32[]{:S(2)}) %collective-permute-start.7) | collective-permute-done | bytes 262176 | tf_op jit(solution)/shard_map/ppermute | solution.py:163
  85.0 2.9 %add_edges.1 = (f32[1024,384]{1,0:T(8,128)S(1)}, bf16[256,384]{1,0:T(8,128)(2,1)S(1)}, bf16[256,384]{1,0:T(8,128)(2,1)S(1)}) custom-call(s32[1]{0:T(128)} %bitcast.me_ref, s32[16,128]{1,0:T(8,128)S(1)} %copy-done.3, bf16[16,8,128,384]{3,2,1,0:T(8,128)(2,1)} %mix.1.refs_0_.refs_1_.refs_2_.refs_3_.refs_4_.refs_5_.refs_6_, ...), custom_call_target="tpu_custom_call" | custom-call | flops 16 | bytes 16 | tf_op jit(solution)/shard_map/add_edges/pallas_call | solution.py:201
  87.9 2.5 %collective-permute-start.11 = (bf16[256,384]{1,0:T(8,128)(2,1)S(1)}, bf16[256,384]{1,0:T(8,128)(2,1)S(1)}, u32[]{:S(2)}, u32[]{:S(2)}) collective-permute-start(bf16[256,384]{1,0:T(8,128)(2,1)S(1)} %get-tuple-element.27), channel_id=1, source_target_pairs={{0,1},{1,2},{2,3},{3,4},{4,5},{5,6},{6,7},{7,8},{8,9},{9,10},{10,1... | collective-permute-start | bytes 589832 | tf_op jit(solution)/shard_map/ppermute | solution.py:286
  90.4 1.9 %collective-permute-start.12 = (bf16[256,384]{1,0:T(8,128)(2,1)S(1)}, bf16[256,384]{1,0:T(8,128)(2,1)S(1)}, u32[]{:S(2)}, u32[]{:S(2)}) collective-permute-start(bf16[256,384]{1,0:T(8,128)(2,1)S(1)} %get-tuple-element.28), channel_id=1, source_target_pairs={{1,0},{2,1},{3,2},{4,3},{5,4},{6,5},{7,6},{8,7},{9,8},{10,9},{11,1... | collective-permute-start | bytes 589832 | tf_op jit(solution)/shard_map/ppermute | solution.py:285
  92.3 0.0 collective-permute-done.5.refs_2_.refs_3_
  92.3 2.3 %add_rest.2.refs_4_ = f32[1024,384]{1,0:T(8,128)S(1)} custom-call(s32[1]{0:T(128)} %bitcast.me_ref, s32[16,128]{1,0:T(8,128)S(1)} %copy-done.3, bf16[16,8,128,384]{3,2,1,0:T(8,128)(2,1)} %mix.1.refs_0_.refs_1_.refs_2_.refs_3_.refs_4_.refs_5_.refs_6_, bf16[16,8,128,384]{3,2,1,0:T(8,128)(2,1)} %mix.1.refs_0_.refs_1_.refs_2_.refs_3_.refs_4_.refs_5_.refs_6_, ...), custom_call_target="tpu_custom_call" | custom-call | flops 8 | bytes 8 | tf_op jit(solution)/shard_map/add_rest/pallas_call | solution.py:201
  94.6 3.9 %collective-permute-done.11.refs_5_ = bf16[256,384]{1,0:T(8,128)(2,1)S(1)} collective-permute-done((bf16[256,384]{1,0:T(8,128)(2,1)S(1)}, bf16[256,384]{1,0:T(8,128)(2,1)S(1)}, u32[]{:S(2)}, u32[]{:S(2)}) %collective-permute-start.11) | collective-permute-done | bytes 196640 | tf_op jit(solution)/shard_map/ppermute | solution.py:286
  98.5 1.7 %collective-permute-done.12.refs_6_ = bf16[256,384]{1,0:T(8,128)(2,1)S(1)} collective-permute-done((bf16[256,384]{1,0:T(8,128)(2,1)S(1)}, bf16[256,384]{1,0:T(8,128)(2,1)S(1)}, u32[]{:S(2)}, u32[]{:S(2)}) %collective-permute-start.12) | collective-permute-done | bytes 196640 | tf_op jit(solution)/shard_map/ppermute | solution.py:285
  100.2 0.0 collective-permute-done.4.refs_2_.refs_3_
  100.2 3.3 %add_rest.3 = bf16[1024,384]{1,0:T(8,128)(2,1)} custom-call(s32[1]{0:T(128)} %bitcast.me_ref, s32[16,128]{1,0:T(8,128)S(1)} %copy-done.3, bf16[16,8,128,384]{3,2,1,0:T(8,128)(2,1)} %mix.1.refs_0_.refs_1_.refs_2_.refs_3_.refs_4_.refs_5_.refs_6_, bf16[16,8,128,384]{3,2,1,0:T(8,128)(2,1)} %mix.1.refs_0_.refs_1_.refs_2_.refs_3_.refs_4_.refs_5_.refs_6_, ...), custom_call_target="tpu_custom_call" | custom-call | flops 8 | bytes 8 | tf_op jit(solution)/shard_map/add_rest/pallas_call | solution.py:201
  (11 shorter events, 0.2 us)
Async XLA Ops:
  0.0 14.5 %copy-start.3 = (s32[16,128]{1,0:T(8,128)S(1)}, s32[16,128]{1,0:T(8,128)}, u32[]{:S(2)}) copy-start(s32[16,128]{1,0:T(8,128)} %target_ref.11) | copy-start | bytes 24580
  0.0 14.5 %copy-start.2 = (bf16[1024,384]{1,0:T(8,128)(2,1)S(1)}, bf16[1024,384]{1,0:T(8,128)(2,1)}, u32[]{:S(2)}) copy-start(bf16[1024,384]{1,0:T(8,128)(2,1)} %param.4) | copy-start | bytes 2359300
  0.0 7.8 %collective-permute-start = (bf16[16,8,128,128]{3,2,1,0:T(8,128)(2,1)}, bf16[16,8,128,128]{3,2,1,0:T(8,128)(2,1)}, u32[]{:S(2)}, u32[]{:S(2)}) collective-permute-start(bf16[16,8,128,128]{3,2,1,0:T(8,128)(2,1)} %bitcast.4), channel_id=1, source_target_pairs={{0,1},{1,0},{2,3},{3,2},{4,5},{5,4},{6,7},{7,6},{8,9},{9,8},{10,11... | collective-permute-start | bytes 12582920 | tf_op jit(solution)/shard_map/ppermute | solution.py:163
  1.7 28.8 %collective-permute-start.1 = (bf16[1,8,128,128]{3,2,1,0:T(8,128)(2,1)S(1)}, bf16[1,8,128,128]{3,2,1,0:T(8,128)(2,1)S(1)}, u32[]{:S(2)}, u32[]{:S(2)}) collective-permute-start(bf16[1,8,128,128]{3,2,1,0:T(8,128)(2,1)S(1)} %constant_dynamic-slice_fusion.21), channel_id=1, source_target_pairs={{0,8},{1,9},{2,10},{3,11},{4,12},{5,13},{6,14},{7,15},{8,0},{9,1},... | collective-permute-start | bytes 786440 | tf_op jit(solution)/shard_map/ppermute | solution.py:163
  1.8 12.8 %copy-start.1 = (bf16[16,1024,128]{2,1,0:T(8,128)(2,1)S(1)}, bf16[16,1024,128]{2,1,0:T(8,128)(2,1)}, u32[]{:S(2)}) copy-start(bf16[16,1024,128]{2,1,0:T(8,128)(2,1)} %param.5) | copy-start | bytes 12582916
  8.8 35.8 %collective-permute-start.2 = (bf16[2,8,128,128]{3,2,1,0:T(8,128)(2,1)S(1)}, bf16[2,8,128,128]{3,2,1,0:T(8,128)(2,1)S(1)}, u32[]{:S(2)}, u32[]{:S(2)}) collective-permute-start(bf16[2,8,128,128]{3,2,1,0:T(8,128)(2,1)S(1)} %pad_maximum_fusion), channel_id=1, source_target_pairs={{0,12},{1,13},{2,14},{3,15},{4,8},{5,9},{6,10},{7,11},{8,4},{9,5},... | collective-permute-start | bytes 1572872 | tf_op jit(solution)/shard_map/ppermute | solution.py:163
  10.2 34.7 %collective-permute-start.3 = (bf16[2,8,128,128]{3,2,1,0:T(8,128)(2,1)S(1)}, bf16[2,8,128,128]{3,2,1,0:T(8,128)(2,1)S(1)}, u32[]{:S(2)}, u32[]{:S(2)}) collective-permute-start(bf16[2,8,128,128]{3,2,1,0:T(8,128)(2,1)S(1)} %pad_maximum_fusion.1), channel_id=1, source_target_pairs={{0,4},{1,5},{2,6},{3,7},{4,0},{5,1},{6,2},{7,3},{8,12},{9,13},{10,... | collective-permute-start | bytes 1572872 | tf_op jit(solution)/shard_map/ppermute | solution.py:163
  12.4 39.7 %collective-permute-start.8 = (bf16[1,8,128,128]{3,2,1,0:T(8,128)(2,1)S(1)}, bf16[1,8,128,128]{3,2,1,0:T(8,128)(2,1)S(1)}, u32[]{:S(2)}, u32[]{:S(2)}) collective-permute-start(bf16[1,8,128,128]{3,2,1,0:T(8,128)(2,1)S(1)} %constant_dynamic-slice_fusion.16), channel_id=1, source_target_pairs={{0,8},{1,9},{2,10},{3,11},{4,12},{5,13},{6,14},{7,15},{8,0},{9,1},... | collective-permute-start | bytes 786440 | tf_op jit(solution)/shard_map/ppermute | solution.py:163
  14.5 12.2 %copy-start = (bf16[16384,128]{1,0:T(8,128)(2,1)S(1)}, bf16[16384,128]{1,0:T(8,128)(2,1)}, u32[]{:S(2)}) copy-start(bf16[16384,128]{1,0:T(8,128)(2,1)} %param.6) | copy-start | bytes 12582916
  26.9 31.0 %collective-permute-start.9 = (bf16[2,8,128,128]{3,2,1,0:T(8,128)(2,1)S(1)}, bf16[2,8,128,128]{3,2,1,0:T(8,128)(2,1)S(1)}, u32[]{:S(2)}, u32[]{:S(2)}) collective-permute-start(bf16[2,8,128,128]{3,2,1,0:T(8,128)(2,1)S(1)} %pad_maximum_fusion.2), channel_id=1, source_target_pairs={{0,6},{1,7},{2,4},{3,5},{4,2},{5,3},{6,0},{7,1},{8,14},{9,15},{10,... | collective-permute-start | bytes 1572872 | tf_op jit(solution)/shard_map/ppermute | solution.py:163
  30.5 47.9 %collective-permute-start.6 = (bf16[2,4,128,128]{3,2,1,0:T(8,128)(2,1)S(1)}, bf16[2,4,128,128]{3,2,1,0:T(8,128)(2,1)S(1)}, u32[]{:S(2)}, u32[]{:S(2)}) collective-permute-start(bf16[2,4,128,128]{3,2,1,0:T(8,128)(2,1)S(1)} %maximum_maximum_fusion), channel_id=1, source_target_pairs={{0,10},{1,11},{2,8},{3,9},{4,14},{5,15},{6,12},{7,13},{8,2},{9,3},... | collective-permute-start | bytes 786440 | tf_op jit(solution)/shard_map/ppermute | solution.py:163
  44.7 40.3 %collective-permute-start.7 = (bf16[2,4,128,128]{3,2,1,0:T(8,128)(2,1)S(1)}, bf16[2,4,128,128]{3,2,1,0:T(8,128)(2,1)S(1)}, u32[]{:S(2)}, u32[]{:S(2)}) collective-permute-start(bf16[2,4,128,128]{3,2,1,0:T(8,128)(2,1)S(1)} %maximum_maximum_fusion.1), channel_id=1, source_target_pairs={{0,14},{1,15},{2,12},{3,13},{4,10},{5,11},{6,8},{7,9},{8,6},{9,7},... | collective-permute-start | bytes 786440 | tf_op jit(solution)/shard_map/ppermute | solution.py:163
  44.9 29.3 %collective-permute-start.10 = (bf16[2,8,128,128]{3,2,1,0:T(8,128)(2,1)S(1)}, bf16[2,8,128,128]{3,2,1,0:T(8,128)(2,1)S(1)}, u32[]{:S(2)}, u32[]{:S(2)}) collective-permute-start(bf16[2,8,128,128]{3,2,1,0:T(8,128)(2,1)S(1)} %pad_maximum_fusion.3), channel_id=1, source_target_pairs={{0,2},{1,3},{2,0},{3,1},{4,6},{5,7},{6,4},{7,5},{8,10},{9,11},{10,... | collective-permute-start | bytes 1572872 | tf_op jit(solution)/shard_map/ppermute | solution.py:163
  52.1 40.3 %collective-permute-start.5 = (bf16[2,4,128,128]{3,2,1,0:T(8,128)(2,1)S(1)}, bf16[2,4,128,128]{3,2,1,0:T(8,128)(2,1)S(1)}, u32[]{:S(2)}, u32[]{:S(2)}) collective-permute-start(bf16[2,4,128,128]{3,2,1,0:T(8,128)(2,1)S(1)} %pad_maximum_fusion.5), channel_id=1, source_target_pairs={{0,10},{1,11},{2,8},{3,9},{4,14},{5,15},{6,12},{7,13},{8,2},{9,3},... | collective-permute-start | bytes 786440 | tf_op jit(solution)/shard_map/ppermute | solution.py:163
  57.9 42.3 %collective-permute-start.4 = (bf16[2,4,128,128]{3,2,1,0:T(8,128)(2,1)S(1)}, bf16[2,4,128,128]{3,2,1,0:T(8,128)(2,1)S(1)}, u32[]{:S(2)}, u32[]{:S(2)}) collective-permute-start(bf16[2,4,128,128]{3,2,1,0:T(8,128)(2,1)S(1)} %pad_maximum_fusion.4), channel_id=1, source_target_pairs={{0,14},{1,15},{2,12},{3,13},{4,10},{5,11},{6,8},{7,9},{8,6},{9,7},... | collective-permute-start | bytes 786440 | tf_op jit(solution)/shard_map/ppermute | solution.py:163
  87.9 10.6 %collective-permute-start.11 = (bf16[256,384]{1,0:T(8,128)(2,1)S(1)}, bf16[256,384]{1,0:T(8,128)(2,1)S(1)}, u32[]{:S(2)}, u32[]{:S(2)}) collective-permute-start(bf16[256,384]{1,0:T(8,128)(2,1)S(1)} %get-tuple-element.27), channel_id=1, source_target_pairs={{0,1},{1,2},{2,3},{3,4},{4,5},{5,6},{6,7},{7,8},{8,9},{9,10},{10,1... | collective-permute-start | bytes 589832 | tf_op jit(solution)/shard_map/ppermute | solution.py:286
  90.4 9.8 %collective-permute-start.12 = (bf16[256,384]{1,0:T(8,128)(2,1)S(1)}, bf16[256,384]{1,0:T(8,128)(2,1)S(1)}, u32[]{:S(2)}, u32[]{:S(2)}) collective-permute-start(bf16[256,384]{1,0:T(8,128)(2,1)S(1)} %get-tuple-element.28), channel_id=1, source_target_pairs={{1,0},{2,1},{3,2},{4,3},{5,4},{6,5},{7,6},{8,7},{9,8},{10,9},{11,1... | collective-permute-start | bytes 589832 | tf_op jit(solution)/shard_map/ppermute | solution.py:285

commit v3 on v0

v3 whole, which is shorter than its diff:
```python
import functools

import jax
import jax.numpy as jnp
from jax import lax
from jax.experimental import pallas as pl
from jax.experimental.pallas import tpu as pltpu
from jax.sharding import PartitionSpec as P

REACH = 2
FIRST = 8
EARLY = ((12, "outer"), (4, "all"), (10, "outer"), (14, "outer"))
LATE = ((2, "all"), (6, "all"))


def params(megabytes=28):
    return pltpu.CompilerParams(vmem_limit_bytes=megabytes * 2**20)


def cost(pairs):
    return pl.CostEstimate(flops=pairs, bytes_accessed=pairs, transcendentals=0)


def after(x, *done):
    return lax.optimization_barrier((x, *done))[0]


def mix_kernel(chunk, left_ref, psi_ref, mixed_ref):
    terms, _, width, _ = left_ref.shape
    columns = psi_ref.shape[2]
    for t in range(0, terms, chunk):
        tall = left_ref[t : t + chunk, 0].reshape(chunk * width, width)
        product = jnp.dot(tall, psi_ref[0], preferred_element_type=jnp.float32)
        mixed_ref[t : t + chunk, 0] = product.astype(mixed_ref.dtype).reshape(chunk, width, columns)


def mix(left_env, psi):
    terms, blocks, width, _ = left_env.shape
    columns = psi.shape[2]
    inner = blocks - 2 * REACH

    def place(slot):
        return jnp.where(slot < inner, slot + REACH, jnp.where(slot < inner + REACH, slot - inner, slot))

    return pl.pallas_call(
        functools.partial(mix_kernel, 4),
        grid=(blocks,),
        in_specs=[
            pl.BlockSpec((terms, 1, width, width), lambda i: (0, place(i), 0, 0)),
            pl.BlockSpec((1, width, columns), lambda i: (place(i), 0, 0)),
        ],
        out_specs=pl.BlockSpec((terms, 1, width, columns), lambda i: (0, i, 0, 0)),
        out_shape=jax.ShapeDtypeStruct((terms, blocks, width, columns), jnp.bfloat16),
        cost_estimate=cost(terms * blocks),
        compiler_params=params(12),
        name="mix",
    )(left_env, psi)


def add_kernel(width, items, terms_of, base, finish, halos, me_ref, target_ref, *refs):
    refs = list(refs)
    mixed = [refs.pop(0) for _ in items]
    right = [refs.pop(0) for _ in items]
    before = refs.pop(0) if base else None
    from_pair, from_other = (refs.pop(0), refs.pop(0)) if halos else (None, None)
    acc = refs[-1]
    halo = REACH * width
    offset = REACH if finish in ("open", "split") else 0
    if before is None:
        acc[...] = jnp.zeros_like(acc)
    else:
        acc[...] = before[...]
    odd = me_ref[0] % 2
    if halos:
        far = acc.shape[0] - halo
        acc[pl.ds(pl.multiple_of((1 - odd) * far, halo), halo), :] += from_pair[...].astype(jnp.float32)
        acc[pl.ds(pl.multiple_of(odd * far, halo), halo), :] += from_other[...].astype(jnp.float32)
    for (s, places), m, r in zip(items, mixed, right):
        shift = target_ref[terms_of(me_ref[0], s), REACH] - REACH
        vectors = m.shape[-1] // width
        for slot, (piece, place) in enumerate(places):
            tall = jnp.concatenate(
                [m[0, slot, :, k * width : (k + 1) * width] for k in range(vectors)], axis=0
            )
            product = jnp.dot(tall, r[0, piece], preferred_element_type=jnp.float32)
            start = pl.multiple_of((place + offset + shift) * width, width)
            for k in range(vectors):
                lanes = slice(k * width, (k + 1) * width)
                acc[pl.ds(start, width), lanes] += product[k * width : (k + 1) * width]
    if finish == "split":
        own, to_pair, to_other = refs[:3]
        far = acc.shape[0] - halo
        to_pair[...] = acc[pl.ds(pl.multiple_of((1 - odd) * far, halo), halo), :].astype(to_pair.dtype)
        to_other[...] = acc[pl.ds(pl.multiple_of(odd * far, halo), halo), :].astype(to_other.dtype)
        own[...] = acc[halo:-halo]
    if finish == "final":
        refs[0][...] = acc[...].astype(refs[0].dtype)


def shards(psi, left_env, right_env, target):
    terms = target.shape[0]
    width = left_env.shape[2]
    columns = psi.shape[1]
    devices = lax.axis_size("terms")
    stride = devices // terms
    blocks = psi.shape[0] // width
    per_class = blocks // stride
    me = lax.axis_index("terms")
    me_ref = me.astype(jnp.int32).reshape(1)
    spans = {
        "all": ((0, blocks),),
        "outer": ((0, REACH), (blocks - REACH, blocks)),
        "inner": ((REACH, blocks - REACH),),
    }
    by_partner = stride == 1 and terms == 16
    terms_of = (lambda own, s: jnp.bitwise_xor(own, s)) if by_partner else (lambda own, s: s)
    halo = REACH * width
    open_shape = jax.ShapeDtypeStruct((blocks * width + 2 * halo, columns), jnp.float32)
    core_shape = jax.ShapeDtypeStruct((blocks * width, columns), jnp.float32)
    halo_shape = jax.ShapeDtypeStruct((halo, columns), jnp.bfloat16)
    out_shape = jax.ShapeDtypeStruct((blocks * width, columns), jnp.bfloat16)

    psi_blocks = psi.reshape(blocks, width, columns)
    left_blocks = left_env.reshape(terms, blocks, width, width)
    right = right_env.reshape(devices, per_class, width, width)

    def whole(x):
        return pl.BlockSpec(x.shape, lambda i, me, target, nd=len(x.shape): (0,) * nd)

    def add(mixed, pieces, before, finish, halos=()):
        items, specs = [], []
        for s, kind, array, at in pieces:
            held = [place for a, b in spans[kind] for place in range(a, b)]
            by_slot = held if kind != "all" else held[REACH:-REACH] + held[:REACH] + held[-REACH:]
            items.append((s, tuple((held.index(place), place) for place in by_slot)))
            specs.append(
                pl.BlockSpec(
                    (1, len(held), width, columns),
                    lambda i, me, target, s=s, slot=int(kind == "outer"): (terms_of(me[0], s), slot, 0, 0),
                )
            )
        for s, kind, array, at in pieces:
            where = at if callable(at) else (lambda own, at=at: at)
            specs.append(
                pl.BlockSpec((1, *array.shape[1:]), lambda i, me, target, where=where: (where(me[0]), 0, 0, 0))
            )
        extra = [*([] if before is None else [before]), *halos]
        outs = {
            "open": (open_shape,),
            "split": (core_shape, halo_shape, halo_shape),
            "core": (core_shape,),
            "final": (out_shape,),
        }[finish]
        scratch = {"split": open_shape, "final": core_shape}.get(finish)
        got = pl.pallas_call(
            functools.partial(add_kernel, width, tuple(items), terms_of, before is not None, finish, bool(halos)),
            grid_spec=pltpu.PrefetchScalarGridSpec(
                num_scalar_prefetch=2,
                grid=(1,),
                in_specs=specs + [whole(x) for x in extra],
                out_specs=tuple(whole(x) for x in outs),
                scratch_shapes=[] if scratch is None else [pltpu.VMEM(scratch.shape, scratch.dtype)],
            ),
            out_shape=outs,
            cost_estimate=cost(len(pieces) * blocks),
            compiler_params=params(),
            name="add_" + finish,
        )(me_ref, target, *[mixed for _ in pieces], *[p[2] for p in pieces], *extra)
        return got if len(outs) > 1 else got[0]

    def neighbours(to_pair, to_other):
        from_pair = lax.ppermute(to_pair, "terms", [(i, i ^ 1) for i in range(devices)])
        others = [(i, i + 1) for i in range(1, devices - 1, 2)]
        from_other = lax.ppermute(to_other, "terms", others + [(b, a) for a, b in others])
        return from_pair, from_other

    if not by_partner:
        got = lax.all_to_all(right, "terms", split_axis=0, concat_axis=0, tiled=True)
        got = got.reshape(terms, stride, per_class, width, width)
        got = jnp.swapaxes(got, 1, 2).reshape(terms, blocks, width, width)
        mixed = mix(left_blocks, psi_blocks)
        sums = None
        step = max(1, terms // 4)
        for a in range(0, terms - step, step):
            sums = add(mixed, [(s, "all", got, s) for s in range(a, a + step)], sums, "open")
        core, to_pair, to_other = add(mixed, [(s, "all", got, s) for s in range(a + step, terms)], sums, "split")
        return add(mixed, [], core, "final", neighbours(to_pair, to_other))

    def move(operand, s):
        return lax.ppermute(operand, "terms", [(i, i ^ s) for i in range(devices)])

    def pick(source, index, start, count):
        return lax.dynamic_slice(source, (index, start, 0, 0), (1, count, width, width))

    arrived = {}

    def send(source, relayed, s, kind):
        partner = jnp.bitwise_xor(me, s)
        parts = [
            jnp.concatenate([pick(array, partner, a, b - a) for a, b in spans[kind]], axis=1)
            for array in (source, relayed)
        ]
        message = jnp.concatenate(parts, axis=0)
        got = move(message, s)
        arrived[s, kind], arrived[s + 1, kind] = (got, 0), (got, 1)
        return message

    def send_single(source, s, kind, term):
        partner = jnp.bitwise_xor(me, s)
        message = jnp.concatenate([pick(source, partner, a, b - a) for a, b in spans[kind]], axis=1)
        arrived[term, kind] = (move(message, s), 0)

    def items(*keys):
        return [(s, kind, *arrived[s, kind]) for s, kind in keys]

    def pairs(messages):
        return [(t, kind) for s, kind in messages for t in (s, s + 1)]

    exchanged = move(right, 1)
    first = pick(right, jnp.bitwise_xor(me, FIRST), 0, blocks)
    arrived[0, "all"] = (right, lambda own: own)
    arrived[1, "all"] = (exchanged, lambda own: own)
    arrived[FIRST, "all"] = (move(first, FIRST), 0)
    messages = [first]
    for s, kind in EARLY:
        messages.append(send(after(right, messages[-1]), after(exchanged, messages[-1]), s, kind))
    mixed = mix(after(left_blocks, *messages), psi_blocks)
    source, relayed = after(right, mixed), after(exchanged, mixed)
    send_single(relayed, FIRST, "all", FIRST + 1)
    send(source, relayed, *LATE[1])
    sums = add(mixed, items((0, "all"), (1, "all"), (FIRST, "all"), *pairs(EARLY[:1])), None, "open")
    source, relayed = after(right, sums), after(exchanged, sums)
    send(source, relayed, *LATE[0])
    send(source, relayed, 12, "inner")
    send(source, relayed, 10, "inner")
    send_single(source, 14, "inner", 14)
    send_single(relayed, 14, "inner", 15)
    sums = add(mixed, items(*pairs(EARLY[1:3])), sums, "open")
    core, to_pair, to_other = add(mixed, items((FIRST + 1, "all"), *pairs(EARLY[3:] + LATE)), sums, "split")
    halos = neighbours(to_pair, to_other)
    core = add(mixed, items(*pairs([(12, "inner")])), core, "core")
    core = add(mixed, items(*pairs([(10, "inner")])), core, "core", halos)
    return add(mixed, items(*pairs([(14, "inner")])), core, "final")


def solution(mesh):
    return jax.shard_map(
        shards,
        mesh=mesh,
        in_specs=(
            P(("groups", "terms"), None),
            P("groups", "terms", None),
            P(("groups", "terms"), None),
            P("groups", None),
        ),
        out_specs=P(("groups", "terms"), None),
        check_vma=False,
    )
```

time: 643 us -> 102 us (0.16)
  blocking collectives: 277 us -> 0 us
  waiting for transfers between devices: 270 us -> 46 us
  local copies, waits for them, and re-layouts: 66.4 us -> 11.9 us
  matrix products: 18.8 us -> 0 us
  starting transfers between devices: 6.64 us -> 24.9 us
  Pallas kernels: 0 us -> 17.2 us
    all_to_all x1 -> x0, blocking collectives: 277 us -> none  [shards(): lax.all_to_all(ordered.reshape(devices, per_class, block_width, columns),...]
    all_to_all x1 -> x0, waiting for transfers between devices: 270 us -> none  [shards(): lax.all_to_all(outgoing, 'terms', split_axis=0, concat_axis=0, tiled=True)]
    ppermute x0 -> x15, waiting for transfers between devices: none -> 46 us  [the longest x13 46 us: move(): return lax.ppermute(operand, 'terms', [(i, i ^ s) for i in range(devices)])]
    dot_general x2 -> x0, local copies, waits for them, and re-layouts: 35.4 us -> none  [shards(): jnp.einsum('trg,tgjac->jrac', selector, returned, preferred_element_type=...]
    ppermute x0 -> x15, starting transfers between devices: none -> 24.9 us  [the longest x13 20.8 us: move(): return lax.ppermute(operand, 'terms', [(i, i ^ s) for i in range(devices)])]
    reshape x2 -> x0, local copies, waits for them, and re-layouts: 22.7 us -> none  [the longest x1 16.6 us: shards(): partial_out = partial_out.reshape(devices * per_class, block_width, columns)]
    dot_general x3 -> x0, matrix products: 18.8 us -> none  [the longest x1 10.2 us: shards(): jnp.einsum('kavb,kbm->kavm', regrouped, right_items, preferred_element_ty...]
    pallas_call x0 -> x7, Pallas kernels: none -> 17.2 us  [the longest x6 11.1 us: add(): pl.pallas_call(functools.partial(add_kernel, width, tuple(items), terms_o...]
  transfers between devices with their start and end apart: 1 -> 15, of which waited for: 1 -> 6; matrix products, arithmetic and copies ran while one was open for 0% -> 10% of each run, Pallas kernels for 0% -> 15%
where the time goes in v3:
time: 102 us; the launch traced here: 101 us
  waiting for transfers between devices  46 us (45%)
  starting transfers between devices  24.9 us (24%)
  Pallas kernels  17.2 us (17%)
  local copies, waits for them, and re-layouts  11.9 us (12%)
    ppermute x13, waiting for transfers between devices, move(): return lax.ppermute(operand, 'terms', [(i, i ^ s) for i in range(devices)])  46 us
    ppermute x13, starting transfers between devices, move(): return lax.ppermute(operand, 'terms', [(i, i ^ s) for i in range(devices)])  20.8 us
    pallas_call x6, Pallas kernels, add(): pl.pallas_call(functools.partial(add_kernel, width, tuple(items), terms_o...  11.1 us
    dynamic_slice x14, local copies, waits for them, and re-layouts, pick(): lax.dynamic_slice(source, (index, start, 0, 0), (1, count, width, width))  9.72 us
    pallas_call x1, Pallas kernels, mix(): pl.pallas_call(functools.partial(mix_kernel, 4), grid=(blocks,), in_specs...  6.05 us
    ppermute x1, starting transfers between devices, neighbours(): lax.ppermute(to_other, 'terms', others + [(b, a) for a, b in others])  2.46 us
    unnamed x8, local copies, waits for them, and re-layouts  2.2 us
  transfers between devices with their start and end apart: 15, of which 6 were waited for; matrix products, arithmetic and copies ran while one was open for 10% of the time, Pallas kernels for 15%

profile of v3, /device:TPU:17, one launch (start us, length us, event | category | flops | bytes accessed | tf_op | source)
XLA Modules:
  0.0 100.7 jit_solution(219380244713184827)
XLA Ops:
  0.0 0.7 collective-permute-start
  0.7 1.0 constant_dynamic-slice_fusion.25
  1.6 0.1 collective-permute-start.1
  1.8 0.0 copy-start
  1.8 6.0 %collective-permute-done.refs_6_ = bf16[16,8,128,128]{3,2,1,0:T(8,128)(2,1)} collective-permute-done((bf16[16,8,128,128]{3,2,1,0:T(8,128)(2,1)}, bf16[16,8,128,128]{3,2,1,0:T(8,128)(2,1)}, u32[]{:S(2)}, u32[]{:S(2)}) %collective-permute-start) | collective-permute-done | bytes 4194336 | tf_op jit(solution)/shard_map/ppermute | solution.py:190
  7.8 1.0 constant_dynamic-slice_fusion.22
  8.8 0.2 collective-permute-start.2
  9.0 1.0 constant_dynamic-slice_fusion.19
  10.0 1.0 constant_dynamic-slice_fusion.20
  11.0 0.1 pad_maximum_fusion
  11.0 1.2 %collective-permute-start.11 = (bf16[2,8,128,128]{3,2,1,0:T(8,128)(2,1)S(1)}, bf16[2,8,128,128]{3,2,1,0:T(8,128)(2,1)S(1)}, u32[]{:S(2)}, u32[]{:S(2)}) collective-permute-start(bf16[2,8,128,128]{3,2,1,0:T(8,128)(2,1)S(1)} %pad_maximum_fusion), channel_id=1, source_target_pairs={{0,4},{1,5},{2,6},{3,7},{4,0},{5,1},{6,2},{7,3},{8,12},{9,13},{10,... | collective-permute-start | bytes 1572872 | tf_op jit(solution)/shard_map/ppermute | solution.py:190
  12.3 0.9 constant_dynamic-slice_fusion.16
  13.1 0.9 constant_dynamic-slice_fusion.18
  14.1 3.1 %collective-permute-start.12 = (bf16[2,4,128,128]{3,2,1,0:T(8,128)(2,1)S(1)}, bf16[2,4,128,128]{3,2,1,0:T(8,128)(2,1)S(1)}, u32[]{:S(2)}, u32[]{:S(2)}) collective-permute-start(bf16[2,4,128,128]{3,2,1,0:T(8,128)(2,1)S(1)} %maximum_maximum_fusion.1), channel_id=1, source_target_pairs={{0,10},{1,11},{2,8},{3,9},{4,14},{5,15},{6,12},{7,13},{8,2},{9,3},... | collective-permute-start | bytes 786440 | tf_op jit(solution)/shard_map/ppermute | solution.py:190
  17.2 0.9 constant_dynamic-slice_fusion.12
  18.1 0.0 copy-start.1
  18.1 2.2 %copy-done.1 = bf16[16,1024,128]{2,1,0:T(8,128)(2,1)S(1)} copy-done((bf16[16,1024,128]{2,1,0:T(8,128)(2,1)S(1)}, bf16[16,1024,128]{2,1,0:T(8,128)(2,1)}, u32[]{:S(2)}) %copy-start.1) | copy-done | bytes 4194328
  20.3 6.0 %mix.1.refs_0_.refs_1_.refs_2_.refs_3_.refs_4_.refs_5_.refs_6_ = bf16[16,8,128,384]{3,2,1,0:T(8,128)(2,1)S(1)} custom-call(bf16[16,8,128,128]{3,2,1,0:T(8,128)(2,1)S(1)} %bitcast.14, bf16[8,128,384]{2,1,0:T(8,128)(2,1)S(1)} %bitcast.15), custom_call_target="tpu_custom_call" | custom-call | flops 128 | bytes 128 | tf_op jit(solution)/shard_map/mix/pallas_call | solution.py:45
  26.4 1.1 %constant_dynamic-slice_fusion = (bf16[1,8,128,128]{3,2,1,0:T(8,128)(2,1)S(1)}, bf16[1,8,128,128]{3,2,1,0:T(8,128)(2,1)S(1)}) fusion(bf16[16,8,128,128]{3,2,1,0:T(8,128)(2,1)} %collective-permute-done.refs_6_, s32[]{:T(128)S(6)} %select_n.20, s32[]{:T(128)S(6)} %select_n.14), kind=kLoop, calls=%fused_computation.8 | loop fusion | bytes 1048584 | tf_op jit(solution)/shard_map/dynamic_slice | solution.py:193
  27.5 0.4 collective-permute-start.7
  27.8 0.1 pad_maximum_fusion.2
  27.9 0.0 collective-permute-done.1.refs_7_
  27.9 1.3 %collective-permute-start.10 = (bf16[2,8,128,128]{3,2,1,0:T(8,128)(2,1)S(1)}, bf16[2,8,128,128]{3,2,1,0:T(8,128)(2,1)S(1)}, u32[]{:S(2)}, u32[]{:S(2)}) collective-permute-start(bf16[2,8,128,128]{3,2,1,0:T(8,128)(2,1)S(1)} %pad_maximum_fusion.2), channel_id=1, source_target_pairs={{0,6},{1,7},{2,4},{3,5},{4,2},{5,3},{6,0},{7,1},{8,14},{9,15},{10,... | collective-permute-start | bytes 1572872 | tf_op jit(solution)/shard_map/ppermute | solution.py:190
  29.2 2.8 %add_open.2.refs_8_ = f32[1536,384]{1,0:T(8,128)S(1)} custom-call(s32[1]{0:T(128)} %bitcast.me_ref, s32[16,128]{1,0:T(8,128)S(1)} %copy-done.3, bf16[16,8,128,384]{3,2,1,0:T(8,128)(2,1)S(1)} %mix.1.refs_0_.refs_1_.refs_2_.refs_3_.refs_4_.refs_5_.refs_6_, bf16[16,8,128,384]{3,2,1,0:T(8,128)(2,1)S(1)} %mix.1.refs_0_.refs_1_.refs_2_.refs_3_.refs_4_.refs_5_.refs_6_, ...), custom_call_target="tpu_custom_call" | custom-call | flops 40 | bytes 40 | tf_op jit(solution)/shard_map/add_open/pallas_call | solution.py:155
  31.9 1.0 constant_dynamic-slice_fusion.2
  33.0 0.1 pad_maximum_fusion.1
  33.0 1.2 %collective-permute-start.9 = (bf16[2,8,128,128]{3,2,1,0:T(8,128)(2,1)S(1)}, bf16[2,8,128,128]{3,2,1,0:T(8,128)(2,1)S(1)}, u32[]{:S(2)}, u32[]{:S(2)}) collective-permute-start(bf16[2,8,128,128]{3,2,1,0:T(8,128)(2,1)S(1)} %pad_maximum_fusion.1), channel_id=1, source_target_pairs={{0,2},{1,3},{2,0},{3,1},{4,6},{5,7},{6,4},{7,5},{8,10},{9,11},{10,... | collective-permute-start | bytes 1572872 | tf_op jit(solution)/shard_map/ppermute | solution.py:190
  34.3 1.1 %constant_dynamic-slice_fusion.5 = (bf16[1,4,128,128]{3,2,1,0:T(8,128)(2,1)S(1)}, bf16[1,4,128,128]{3,2,1,0:T(8,128)(2,1)S(1)}, bf16[1,4,128,128]{3,2,1,0:T(8,128)(2,1)S(1)}) fusion(bf16[16,8,128,128]{3,2,1,0:T(8,128)(2,1)} %collective-permute-done.refs_6_, s32[]{:T(128)S(6)} %select_n.15, s32[]{:T(128)S(6)} %select_n.17, s32[]{:T(128)S(6)} %select_n.18), kind=kLoop, calls=%fused_computation.13 | loop fusion | bytes 786444 | tf_op jit(solution)/shard_map/dynamic_slice | solution.py:193
  35.4 11.7 %collective-permute-done.7.refs_7_ = bf16[1,8,128,128]{3,2,1,0:T(8,128)(2,1)S(1)} collective-permute-done((bf16[1,8,128,128]{3,2,1,0:T(8,128)(2,1)S(1)}, bf16[1,8,128,128]{3,2,1,0:T(8,128)(2,1)S(1)}, u32[]{:S(2)}, u32[]{:S(2)}) %collective-permute-start.7) | collective-permute-done | bytes 262176 | tf_op jit(solution)/shard_map/ppermute | solution.py:190
  47.0 3.5 %collective-permute-start.8 = (bf16[2,4,128,128]{3,2,1,0:T(8,128)(2,1)S(1)}, bf16[2,4,128,128]{3,2,1,0:T(8,128)(2,1)S(1)}, u32[]{:S(2)}, u32[]{:S(2)}) collective-permute-start(bf16[2,4,128,128]{3,2,1,0:T(8,128)(2,1)S(1)} %maximum_maximum_fusion.2), channel_id=1, source_target_pairs={{0,14},{1,15},{2,12},{3,13},{4,10},{5,11},{6,8},{7,9},{8,6},{9,7},... | collective-permute-start | bytes 786440 | tf_op jit(solution)/shard_map/ppermute | solution.py:190
  50.6 0.1 collective-permute-start.6
  50.7 0.0 collective-permute-done.11.refs_4_.refs_5_
  50.7 4.0 %collective-permute-start.5 = (bf16[2,4,128,128]{3,2,1,0:T(8,128)(2,1)S(1)}, bf16[2,4,128,128]{3,2,1,0:T(8,128)(2,1)S(1)}, u32[]{:S(2)}, u32[]{:S(2)}) collective-permute-start(bf16[2,4,128,128]{3,2,1,0:T(8,128)(2,1)S(1)} %pad_maximum_fusion.3), channel_id=1, source_target_pairs={{0,10},{1,11},{2,8},{3,9},{4,14},{5,15},{6,12},{7,13},{8,2},{9,3},... | collective-permute-start | bytes 786440 | tf_op jit(solution)/shard_map/ppermute | solution.py:190
  54.8 1.6 %add_open.3.refs_14_ = f32[1536,384]{1,0:T(8,128)S(1)} custom-call(s32[1]{0:T(128)} %bitcast.me_ref, s32[16,128]{1,0:T(8,128)S(1)} %copy-done.3, bf16[16,8,128,384]{3,2,1,0:T(8,128)(2,1)S(1)} %mix.1.refs_0_.refs_1_.refs_2_.refs_3_.refs_4_.refs_5_.refs_6_, bf16[16,8,128,384]{3,2,1,0:T(8,128)(2,1)S(1)} %mix.1.refs_0_.refs_1_.refs_2_.refs_3_.refs_4_.refs_5_.refs_6_, ...), custom_call_target="tpu_custom_call" | custom-call | flops 32 | bytes 32 | tf_op jit(solution)/shard_map/add_open/pallas_call | solution.py:155
  56.4 17.3 %collective-permute-done.8.refs_8_.refs_9_ = bf16[2,4,128,128]{3,2,1,0:T(8,128)(2,1)S(1)} collective-permute-done((bf16[2,4,128,128]{3,2,1,0:T(8,128)(2,1)S(1)}, bf16[2,4,128,128]{3,2,1,0:T(8,128)(2,1)S(1)}, u32[]{:S(2)}, u32[]{:S(2)}) %collective-permute-start.8) | collective-permute-done | bytes 262176 | tf_op jit(solution)/shard_map/ppermute | solution.py:190
  73.7 2.4 %add_split.1 = (f32[1024,384]{1,0:T(8,128)S(1)}, bf16[256,384]{1,0:T(8,128)(2,1)S(1)}, bf16[256,384]{1,0:T(8,128)(2,1)S(1)}) custom-call(s32[1]{0:T(128)} %bitcast.me_ref, s32[16,128]{1,0:T(8,128)S(1)} %copy-done.3, bf16[16,8,128,384]{3,2,1,0:T(8,128)(2,1)S(1)} %mix.1.refs_0_.refs_1_.refs_2_.refs_3_.refs_4_.refs_5_.refs_6_, ...), custom_call_target="tpu_custom_call" | custom-call | flops 56 | bytes 56 | tf_op jit(solution)/shard_map/add_split/pallas_call | solution.py:155
  76.1 1.6 %collective-permute-start.13 = (bf16[256,384]{1,0:T(8,128)(2,1)S(1)}, bf16[256,384]{1,0:T(8,128)(2,1)S(1)}, u32[]{:S(2)}, u32[]{:S(2)}) collective-permute-start(bf16[256,384]{1,0:T(8,128)(2,1)S(1)} %get-tuple-element.35), channel_id=1, source_target_pairs={{0,1},{1,0},{2,3},{3,2},{4,5},{5,4},{6,7},{7,6},{8,9},{9,8},{10,11... | collective-permute-start | bytes 589832 | tf_op jit(solution)/shard_map/ppermute | solution.py:172
  77.8 2.5 %collective-permute-start.14 = (bf16[256,384]{1,0:T(8,128)(2,1)S(1)}, bf16[256,384]{1,0:T(8,128)(2,1)S(1)}, u32[]{:S(2)}, u32[]{:S(2)}) collective-permute-start(bf16[256,384]{1,0:T(8,128)(2,1)S(1)} %get-tuple-element.36), channel_id=1, source_target_pairs={{1,2},{3,4},{5,6},{7,8},{9,10},{11,12},{13,14},{2,1},{4,3},{6,5},{... | collective-permute-start | bytes 589832 | tf_op jit(solution)/shard_map/ppermute | solution.py:174
  80.2 2.2 %collective-permute-start.3 = (bf16[1,4,128,128]{3,2,1,0:T(8,128)(2,1)S(1)}, bf16[1,4,128,128]{3,2,1,0:T(8,128)(2,1)S(1)}, u32[]{:S(2)}, u32[]{:S(2)}) collective-permute-start(bf16[1,4,128,128]{3,2,1,0:T(8,128)(2,1)S(1)} %get-tuple-element.41), channel_id=1, source_target_pairs={{0,14},{1,15},{2,12},{3,13},{4,10},{5,11},{6,8},{7,9},{8,6},{9,7},... | collective-permute-start | bytes 393224 | tf_op jit(solution)/shard_map/ppermute | solution.py:190
  82.4 1.1 %collective-permute-done.6.refs_2_.refs_3_ = bf16[2,4,128,128]{3,2,1,0:T(8,128)(2,1)S(1)} collective-permute-done((bf16[2,4,128,128]{3,2,1,0:T(8,128)(2,1)S(1)}, bf16[2,4,128,128]{3,2,1,0:T(8,128)(2,1)S(1)}, u32[]{:S(2)}, u32[]{:S(2)}) %collective-permute-start.6) | collective-permute-done | bytes 262176 | tf_op jit(solution)/shard_map/ppermute | solution.py:190
  83.6 2.8 %collective-permute-start.4 = (bf16[1,4,128,128]{3,2,1,0:T(8,128)(2,1)S(1)}, bf16[1,4,128,128]{3,2,1,0:T(8,128)(2,1)S(1)}, u32[]{:S(2)}, u32[]{:S(2)}) collective-permute-start(bf16[1,4,128,128]{3,2,1,0:T(8,128)(2,1)S(1)} %get-tuple-element.44), channel_id=1, source_target_pairs={{0,14},{1,15},{2,12},{3,13},{4,10},{5,11},{6,8},{7,9},{8,6},{9,7},... | collective-permute-start | bytes 393224 | tf_op jit(solution)/shard_map/ppermute | solution.py:190
  86.4 1.1 %add_core.2.refs_4_ = f32[1024,384]{1,0:T(8,128)S(1)} custom-call(s32[1]{0:T(128)} %bitcast.me_ref, s32[16,128]{1,0:T(8,128)S(1)} %copy-done.3, bf16[16,8,128,384]{3,2,1,0:T(8,128)(2,1)S(1)} %mix.1.refs_0_.refs_1_.refs_2_.refs_3_.refs_4_.refs_5_.refs_6_, bf16[16,8,128,384]{3,2,1,0:T(8,128)(2,1)S(1)} %mix.1.refs_0_.refs_1_.refs_2_.refs_3_.refs_4_.refs_5_.refs_6_, ...), custom_call_target="tpu_custom_call" | custom-call | flops 16 | bytes 16 | tf_op jit(solution)/shard_map/add_core/pallas_call | solution.py:155
  87.5 0.0 collective-permute-done.5.refs_2_.refs_3_
  87.5 0.0 collective-permute-done.14.refs_6_
  87.5 1.2 %add_core.3.refs_4_ = f32[1024,384]{1,0:T(8,128)S(1)} custom-call(s32[1]{0:T(128)} %bitcast.me_ref, s32[16,128]{1,0:T(8,128)S(1)} %copy-done.3, bf16[16,8,128,384]{3,2,1,0:T(8,128)(2,1)S(1)} %mix.1.refs_0_.refs_1_.refs_2_.refs_3_.refs_4_.refs_5_.refs_6_, bf16[16,8,128,384]{3,2,1,0:T(8,128)(2,1)S(1)} %mix.1.refs_0_.refs_1_.refs_2_.refs_3_.refs_4_.refs_5_.refs_6_, ...), custom_call_target="tpu_custom_call" | custom-call | flops 16 | bytes 16 | tf_op jit(solution)/shard_map/add_core/pallas_call | solution.py:155
  88.7 8.2 %collective-permute-done.3.refs_2_ = bf16[1,4,128,128]{3,2,1,0:T(8,128)(2,1)S(1)} collective-permute-done((bf16[1,4,128,128]{3,2,1,0:T(8,128)(2,1)S(1)}, bf16[1,4,128,128]{3,2,1,0:T(8,128)(2,1)S(1)}, u32[]{:S(2)}, u32[]{:S(2)}) %collective-permute-start.3) | collective-permute-done | bytes 131104 | tf_op jit(solution)/shard_map/ppermute | solution.py:190
  96.9 1.7 %collective-permute-done.4.refs_3_ = bf16[1,4,128,128]{3,2,1,0:T(8,128)(2,1)S(1)} collective-permute-done((bf16[1,4,128,128]{3,2,1,0:T(8,128)(2,1)S(1)}, bf16[1,4,128,128]{3,2,1,0:T(8,128)(2,1)S(1)}, u32[]{:S(2)}, u32[]{:S(2)}) %collective-permute-start.4) | collective-permute-done | bytes 131104 | tf_op jit(solution)/shard_map/ppermute | solution.py:190
  98.6 2.1 %add_final.1 = bf16[1024,384]{1,0:T(8,128)(2,1)} custom-call(s32[1]{0:T(128)} %bitcast.me_ref, s32[16,128]{1,0:T(8,128)S(1)} %copy-done.3, bf16[16,8,128,384]{3,2,1,0:T(8,128)(2,1)S(1)} %mix.1.refs_0_.refs_1_.refs_2_.refs_3_.refs_4_.refs_5_.refs_6_, bf16[16,8,128,384]{3,2,1,0:T(8,128)(2,1)S(1)} %mix.1.refs_0_.refs_1_.refs_2_.refs_3_.refs_4_.refs_5_.refs_6_, ...), custom_call_target="tpu_custom_call" | custom-call | flops 16 | bytes 16 | tf_op jit(solution)/shard_map/add_final/pallas_call | solution.py:155
  (19 shorter events, 0.2 us)
Async XLA Ops:
  0.0 18.1 %copy-start.2 = (bf16[1024,384]{1,0:T(8,128)(2,1)S(1)}, bf16[1024,384]{1,0:T(8,128)(2,1)}, u32[]{:S(2)}) copy-start(bf16[1024,384]{1,0:T(8,128)(2,1)} %param.4) | copy-start | bytes 2359300
  0.0 7.8 %collective-permute-start = (bf16[16,8,128,128]{3,2,1,0:T(8,128)(2,1)}, bf16[16,8,128,128]{3,2,1,0:T(8,128)(2,1)}, u32[]{:S(2)}, u32[]{:S(2)}) collective-permute-start(bf16[16,8,128,128]{3,2,1,0:T(8,128)(2,1)} %bitcast.4), channel_id=1, source_target_pairs={{0,1},{1,0},{2,3},{3,2},{4,5},{5,4},{6,7},{7,6},{8,9},{9,8},{10,11... | collective-permute-start | bytes 12582920 | tf_op jit(solution)/shard_map/ppermute | solution.py:190
  1.6 26.3 %collective-permute-start.1 = (bf16[1,8,128,128]{3,2,1,0:T(8,128)(2,1)S(1)}, bf16[1,8,128,128]{3,2,1,0:T(8,128)(2,1)S(1)}, u32[]{:S(2)}, u32[]{:S(2)}) collective-permute-start(bf16[1,8,128,128]{3,2,1,0:T(8,128)(2,1)S(1)} %constant_dynamic-slice_fusion.25), channel_id=1, source_target_pairs={{0,8},{1,9},{2,10},{3,11},{4,12},{5,13},{6,14},{7,15},{8,0},{9,1},... | collective-permute-start | bytes 786440 | tf_op jit(solution)/shard_map/ppermute | solution.py:190
  1.8 16.3 %copy-start = (bf16[16384,128]{1,0:T(8,128)(2,1)S(1)}, bf16[16384,128]{1,0:T(8,128)(2,1)}, u32[]{:S(2)}) copy-start(bf16[16384,128]{1,0:T(8,128)(2,1)} %param.6) | copy-start | bytes 12582916
  8.8 20.4 %collective-permute-start.2 = (bf16[2,4,128,128]{3,2,1,0:T(8,128)(2,1)S(1)}, bf16[2,4,128,128]{3,2,1,0:T(8,128)(2,1)S(1)}, u32[]{:S(2)}, u32[]{:S(2)}) collective-permute-start(bf16[2,4,128,128]{3,2,1,0:T(8,128)(2,1)S(1)} %maximum_maximum_fusion), channel_id=1, source_target_pairs={{0,12},{1,13},{2,14},{3,15},{4,8},{5,9},{6,10},{7,11},{8,4},{9,5},... | collective-permute-start | bytes 786440 | tf_op jit(solution)/shard_map/ppermute | solution.py:190
  11.0 39.7 %collective-permute-start.11 = (bf16[2,8,128,128]{3,2,1,0:T(8,128)(2,1)S(1)}, bf16[2,8,128,128]{3,2,1,0:T(8,128)(2,1)S(1)}, u32[]{:S(2)}, u32[]{:S(2)}) collective-permute-start(bf16[2,8,128,128]{3,2,1,0:T(8,128)(2,1)S(1)} %pad_maximum_fusion), channel_id=1, source_target_pairs={{0,4},{1,5},{2,6},{3,7},{4,0},{5,1},{6,2},{7,3},{8,12},{9,13},{10,... | collective-permute-start | bytes 1572872 | tf_op jit(solution)/shard_map/ppermute | solution.py:190
  14.1 36.5 %collective-permute-start.12 = (bf16[2,4,128,128]{3,2,1,0:T(8,128)(2,1)S(1)}, bf16[2,4,128,128]{3,2,1,0:T(8,128)(2,1)S(1)}, u32[]{:S(2)}, u32[]{:S(2)}) collective-permute-start(bf16[2,4,128,128]{3,2,1,0:T(8,128)(2,1)S(1)} %maximum_maximum_fusion.1), channel_id=1, source_target_pairs={{0,10},{1,11},{2,8},{3,9},{4,14},{5,15},{6,12},{7,13},{8,2},{9,3},... | collective-permute-start | bytes 786440 | tf_op jit(solution)/shard_map/ppermute | solution.py:190
  18.1 2.2 %copy-start.1 = (bf16[16,1024,128]{2,1,0:T(8,128)(2,1)S(1)}, bf16[16,1024,128]{2,1,0:T(8,128)(2,1)}, u32[]{:S(2)}) copy-start(bf16[16,1024,128]{2,1,0:T(8,128)(2,1)} %param.5) | copy-start | bytes 12582916
  20.3 8.9 %copy-start.3 = (s32[16,128]{1,0:T(8,128)S(1)}, s32[16,128]{1,0:T(8,128)}, u32[]{:S(2)}) copy-start(s32[16,128]{1,0:T(8,128)} %target_ref.11) | copy-start | bytes 24580
  27.5 19.6 %collective-permute-start.7 = (bf16[1,8,128,128]{3,2,1,0:T(8,128)(2,1)S(1)}, bf16[1,8,128,128]{3,2,1,0:T(8,128)(2,1)S(1)}, u32[]{:S(2)}, u32[]{:S(2)}) collective-permute-start(bf16[1,8,128,128]{3,2,1,0:T(8,128)(2,1)S(1)} %get-tuple-element.38), channel_id=1, source_target_pairs={{0,8},{1,9},{2,10},{3,11},{4,12},{5,13},{6,14},{7,15},{8,0},{9,1},... | collective-permute-start | bytes 786440 | tf_op jit(solution)/shard_map/ppermute | solution.py:190
  27.9 45.8 %collective-permute-start.10 = (bf16[2,8,128,128]{3,2,1,0:T(8,128)(2,1)S(1)}, bf16[2,8,128,128]{3,2,1,0:T(8,128)(2,1)S(1)}, u32[]{:S(2)}, u32[]{:S(2)}) collective-permute-start(bf16[2,8,128,128]{3,2,1,0:T(8,128)(2,1)S(1)} %pad_maximum_fusion.2), channel_id=1, source_target_pairs={{0,6},{1,7},{2,4},{3,5},{4,2},{5,3},{6,0},{7,1},{8,14},{9,15},{10,... | collective-permute-start | bytes 1572872 | tf_op jit(solution)/shard_map/ppermute | solution.py:190
  33.0 40.7 %collective-permute-start.9 = (bf16[2,8,128,128]{3,2,1,0:T(8,128)(2,1)S(1)}, bf16[2,8,128,128]{3,2,1,0:T(8,128)(2,1)S(1)}, u32[]{:S(2)}, u32[]{:S(2)}) collective-permute-start(bf16[2,8,128,128]{3,2,1,0:T(8,128)(2,1)S(1)} %pad_maximum_fusion.1), channel_id=1, source_target_pairs={{0,2},{1,3},{2,0},{3,1},{4,6},{5,7},{6,4},{7,5},{8,10},{9,11},{10,... | collective-permute-start | bytes 1572872 | tf_op jit(solution)/shard_map/ppermute | solution.py:190
  47.0 26.7 %collective-permute-start.8 = (bf16[2,4,128,128]{3,2,1,0:T(8,128)(2,1)S(1)}, bf16[2,4,128,128]{3,2,1,0:T(8,128)(2,1)S(1)}, u32[]{:S(2)}, u32[]{:S(2)}) collective-permute-start(bf16[2,4,128,128]{3,2,1,0:T(8,128)(2,1)S(1)} %maximum_maximum_fusion.2), channel_id=1, source_target_pairs={{0,14},{1,15},{2,12},{3,13},{4,10},{5,11},{6,8},{7,9},{8,6},{9,7},... | collective-permute-start | bytes 786440 | tf_op jit(solution)/shard_map/ppermute | solution.py:190
  50.6 32.9 %collective-permute-start.6 = (bf16[2,4,128,128]{3,2,1,0:T(8,128)(2,1)S(1)}, bf16[2,4,128,128]{3,2,1,0:T(8,128)(2,1)S(1)}, u32[]{:S(2)}, u32[]{:S(2)}) collective-permute-start(bf16[2,4,128,128]{3,2,1,0:T(8,128)(2,1)S(1)} %pad_maximum_fusion.4), channel_id=1, source_target_pairs={{0,12},{1,13},{2,14},{3,15},{4,8},{5,9},{6,10},{7,11},{8,4},{9,5},... | collective-permute-start | bytes 786440 | tf_op jit(solution)/shard_map/ppermute | solution.py:190
  50.7 36.8 %collective-permute-start.5 = (bf16[2,4,128,128]{3,2,1,0:T(8,128)(2,1)S(1)}, bf16[2,4,128,128]{3,2,1,0:T(8,128)(2,1)S(1)}, u32[]{:S(2)}, u32[]{:S(2)}) collective-permute-start(bf16[2,4,128,128]{3,2,1,0:T(8,128)(2,1)S(1)} %pad_maximum_fusion.3), channel_id=1, source_target_pairs={{0,10},{1,11},{2,8},{3,9},{4,14},{5,15},{6,12},{7,13},{8,2},{9,3},... | collective-permute-start | bytes 786440 | tf_op jit(solution)/shard_map/ppermute | solution.py:190
  76.1 11.4 %collective-permute-start.13 = (bf16[256,384]{1,0:T(8,128)(2,1)S(1)}, bf16[256,384]{1,0:T(8,128)(2,1)S(1)}, u32[]{:S(2)}, u32[]{:S(2)}) collective-permute-start(bf16[256,384]{1,0:T(8,128)(2,1)S(1)} %get-tuple-element.35), channel_id=1, source_target_pairs={{0,1},{1,0},{2,3},{3,2},{4,5},{5,4},{6,7},{7,6},{8,9},{9,8},{10,11... | collective-permute-start | bytes 589832 | tf_op jit(solution)/shard_map/ppermute | solution.py:172
  77.8 9.7 %collective-permute-start.14 = (bf16[256,384]{1,0:T(8,128)(2,1)S(1)}, bf16[256,384]{1,0:T(8,128)(2,1)S(1)}, u32[]{:S(2)}, u32[]{:S(2)}) collective-permute-start(bf16[256,384]{1,0:T(8,128)(2,1)S(1)} %get-tuple-element.36), channel_id=1, source_target_pairs={{1,2},{3,4},{5,6},{7,8},{9,10},{11,12},{13,14},{2,1},{4,3},{6,5},{... | collective-permute-start | bytes 589832 | tf_op jit(solution)/shard_map/ppermute | solution.py:174
  80.2 16.7 %collective-permute-start.3 = (bf16[1,4,128,128]{3,2,1,0:T(8,128)(2,1)S(1)}, bf16[1,4,128,128]{3,2,1,0:T(8,128)(2,1)S(1)}, u32[]{:S(2)}, u32[]{:S(2)}) collective-permute-start(bf16[1,4,128,128]{3,2,1,0:T(8,128)(2,1)S(1)} %get-tuple-element.41), channel_id=1, source_target_pairs={{0,14},{1,15},{2,12},{3,13},{4,10},{5,11},{6,8},{7,9},{8,6},{9,7},... | collective-permute-start | bytes 393224 | tf_op jit(solution)/shard_map/ppermute | solution.py:190
  83.6 15.1 %collective-permute-start.4 = (bf16[1,4,128,128]{3,2,1,0:T(8,128)(2,1)S(1)}, bf16[1,4,128,128]{3,2,1,0:T(8,128)(2,1)S(1)}, u32[]{:S(2)}, u32[]{:S(2)}) collective-permute-start(bf16[1,4,128,128]{3,2,1,0:T(8,128)(2,1)S(1)} %get-tuple-element.44), channel_id=1, source_target_pairs={{0,14},{1,15},{2,12},{3,13},{4,10},{5,11},{6,8},{7,9},{8,6},{9,7},... | collective-permute-start | bytes 393224 | tf_op jit(solution)/shard_map/ppermute | solution.py:190

commit v4 on v3

--- a/solution.py
+++ b/solution.py
@@ -9,8 +9,8 @@
 
 REACH = 2
 FIRST = 8
-EARLY = ((12, "outer"), (4, "all"), (10, "outer"), (14, "outer"))
-LATE = ((2, "all"), (6, "all"))
+EARLY = ((12, "outer"), (6, "all"), (10, "outer"), (14, "outer"))
+LATE = ((2, "all"), (4, "all"))
 
 
 def params(megabytes=28):
@@ -43,7 +43,7 @@
         return jnp.where(slot < inner, slot + REACH, jnp.where(slot < inner + REACH, slot - inner, slot))
 
     return pl.pallas_call(
-        functools.partial(mix_kernel, 4),
+        functools.partial(mix_kernel, min(4, terms)),
         grid=(blocks,),
         in_specs=[
             pl.BlockSpec((terms, 1, width, width), lambda i: (0, place(i), 0, 0)),
@@ -62,7 +62,7 @@
     mixed = [refs.pop(0) for _ in items]
     right = [refs.pop(0) for _ in items]
     before = refs.pop(0) if base else None
-    from_pair, from_other = (refs.pop(0), refs.pop(0)) if halos else (None, None)
+    came = [refs.pop(0) for _ in halos]
     acc = refs[-1]
     halo = REACH * width
     offset = REACH if finish in ("open", "split") else 0
@@ -71,10 +71,10 @@
     else:
         acc[...] = before[...]
     odd = me_ref[0] % 2
-    if halos:
+    for kind, array in zip(halos, came):
         far = acc.shape[0] - halo
-        acc[pl.ds(pl.multiple_of((1 - odd) * far, halo), halo), :] += from_pair[...].astype(jnp.float32)
-        acc[pl.ds(pl.multiple_of(odd * far, halo), halo), :] += from_other[...].astype(jnp.float32)
+        side = 1 - odd if kind == "pair" else odd
+        acc[pl.ds(pl.multiple_of(side * far, halo), halo), :] += array[...].astype(jnp.float32)
     for (s, places), m, r in zip(items, mixed, right):
         shift = target_ref[terms_of(me_ref[0], s), REACH] - REACH
         vectors = m.shape[-1] // width
@@ -144,7 +144,7 @@
             specs.append(
                 pl.BlockSpec((1, *array.shape[1:]), lambda i, me, target, where=where: (where(me[0]), 0, 0, 0))
             )
-        extra = [*([] if before is None else [before]), *halos]
+        extra = [*([] if before is None else [before]), *(array for _, array in halos)]
         outs = {
             "open": (open_shape,),
             "split": (core_shape, halo_shape, halo_shape),
@@ -153,7 +153,7 @@
         }[finish]
         scratch = {"split": open_shape, "final": core_shape}.get(finish)
         got = pl.pallas_call(
-            functools.partial(add_kernel, width, tuple(items), terms_of, before is not None, finish, bool(halos)),
+            functools.partial(add_kernel, width, tuple(items), terms_of, before is not None, finish, tuple(kind for kind, _ in halos)),
             grid_spec=pltpu.PrefetchScalarGridSpec(
                 num_scalar_prefetch=2,
                 grid=(1,),
@@ -172,7 +172,7 @@
         from_pair = lax.ppermute(to_pair, "terms", [(i, i ^ 1) for i in range(devices)])
         others = [(i, i + 1) for i in range(1, devices - 1, 2)]
         from_other = lax.ppermute(to_other, "terms", others + [(b, a) for a, b in others])
-        return from_pair, from_other
+        return ("pair", from_pair), ("other", from_other)
 
     if not by_partner:
         got = lax.all_to_all(right, "terms", split_axis=0, concat_axis=0, tiled=True)
@@ -238,8 +238,8 @@
     sums = add(mixed, items(*pairs(EARLY[1:3])), sums, "open")
     core, to_pair, to_other = add(mixed, items((FIRST + 1, "all"), *pairs(EARLY[3:] + LATE)), sums, "split")
     halos = neighbours(to_pair, to_other)
-    core = add(mixed, items(*pairs([(12, "inner")])), core, "core")
-    core = add(mixed, items(*pairs([(10, "inner")])), core, "core", halos)
+    core = add(mixed, [], core, "core", halos[:1])
+    core = add(mixed, items(*pairs([(12, "inner"), (10, "inner")])), core, "core", halos[1:])
     return add(mixed, items(*pairs([(14, "inner")])), core, "final")
 
 

time: 102 us -> 101 us (level)
  transfers between devices with their start and end apart: 15 -> 15, of which waited for: 6 -> 7; matrix products, arithmetic and copies ran while one was open for 10% -> 10% of each run, Pallas kernels for 15% -> 15%
where the time goes in v4:
time: 101 us; the launch traced here: 100 us
  waiting for transfers between devices  45.7 us (45%)
  starting transfers between devices  24.9 us (25%)
  Pallas kernels  17.1 us (17%)
  local copies, waits for them, and re-layouts  11.9 us (12%)
    ppermute x13, waiting for transfers between devices, move(): return lax.ppermute(operand, 'terms', [(i, i ^ s) for i in range(devices)])  45.7 us
    ppermute x13, starting transfers between devices, move(): return lax.ppermute(operand, 'terms', [(i, i ^ s) for i in range(devices)])  20.6 us
    pallas_call x6, Pallas kernels, add(): pl.pallas_call(functools.partial(add_kernel, width, tuple(items), terms_o...  11.1 us
    dynamic_slice x14, local copies, waits for them, and re-layouts, pick(): lax.dynamic_slice(source, (index, start, 0, 0), (1, count, width, width))  9.72 us
    pallas_call x1, Pallas kernels, mix(): pl.pallas_call(functools.partial(mix_kernel, min(4, terms)), grid=(blocks...  6.05 us
    ppermute x1, starting transfers between devices, neighbours(): lax.ppermute(to_other, 'terms', others + [(b, a) for a, b in others])  2.46 us
    unnamed x8, local copies, waits for them, and re-layouts  2.2 us
  transfers between devices with their start and end apart: 15, of which 7 were waited for; matrix products, arithmetic and copies ran while one was open for 10% of the time, Pallas kernels for 15%

profile of v4, /device:TPU:17, one launch (start us, length us, event | category | flops | bytes accessed | tf_op | source)
XLA Modules:
  0.0 100.2 jit_solution(4972590967267171769)
XLA Ops:
  0.0 0.7 collective-permute-start
  0.7 1.0 constant_dynamic-slice_fusion.25
  1.6 0.1 collective-permute-start.1
  1.8 0.0 copy-start
  1.8 6.0 %collective-permute-done.refs_6_ = bf16[16,8,128,128]{3,2,1,0:T(8,128)(2,1)} collective-permute-done((bf16[16,8,128,128]{3,2,1,0:T(8,128)(2,1)}, bf16[16,8,128,128]{3,2,1,0:T(8,128)(2,1)}, u32[]{:S(2)}, u32[]{:S(2)}) %collective-permute-start) | collective-permute-done | bytes 4194336 | tf_op jit(solution)/shard_map/ppermute | solution.py:190
  7.8 1.0 constant_dynamic-slice_fusion.22
  8.8 0.2 collective-permute-start.2
  9.0 1.0 constant_dynamic-slice_fusion.19
  10.0 1.0 constant_dynamic-slice_fusion.20
  11.0 0.1 pad_maximum_fusion
  11.0 2.2 %collective-permute-start.11 = (bf16[2,8,128,128]{3,2,1,0:T(8,128)(2,1)S(1)}, bf16[2,8,128,128]{3,2,1,0:T(8,128)(2,1)S(1)}, u32[]{:S(2)}, u32[]{:S(2)}) collective-permute-start(bf16[2,8,128,128]{3,2,1,0:T(8,128)(2,1)S(1)} %pad_maximum_fusion), channel_id=1, source_target_pairs={{0,6},{1,7},{2,4},{3,5},{4,2},{5,3},{6,0},{7,1},{8,14},{9,15},{10,... | collective-permute-start | bytes 1572872 | tf_op jit(solution)/shard_map/ppermute | solution.py:190
  13.2 0.9 constant_dynamic-slice_fusion.16
  14.1 0.9 constant_dynamic-slice_fusion.18
  15.0 2.1 %collective-permute-start.12 = (bf16[2,4,128,128]{3,2,1,0:T(8,128)(2,1)S(1)}, bf16[2,4,128,128]{3,2,1,0:T(8,128)(2,1)S(1)}, u32[]{:S(2)}, u32[]{:S(2)}) collective-permute-start(bf16[2,4,128,128]{3,2,1,0:T(8,128)(2,1)S(1)} %maximum_maximum_fusion.1), channel_id=1, source_target_pairs={{0,10},{1,11},{2,8},{3,9},{4,14},{5,15},{6,12},{7,13},{8,2},{9,3},... | collective-permute-start | bytes 786440 | tf_op jit(solution)/shard_map/ppermute | solution.py:190
  17.2 0.9 constant_dynamic-slice_fusion.12
  18.1 0.0 copy-start.1
  18.1 2.2 %copy-done.1 = bf16[16,1024,128]{2,1,0:T(8,128)(2,1)S(1)} copy-done((bf16[16,1024,128]{2,1,0:T(8,128)(2,1)S(1)}, bf16[16,1024,128]{2,1,0:T(8,128)(2,1)}, u32[]{:S(2)}) %copy-start.1) | copy-done | bytes 4194328
  20.3 6.0 %mix.1.refs_0_.refs_1_.refs_2_.refs_3_.refs_4_.refs_5_.refs_6_ = bf16[16,8,128,384]{3,2,1,0:T(8,128)(2,1)S(1)} custom-call(bf16[16,8,128,128]{3,2,1,0:T(8,128)(2,1)S(1)} %bitcast.14, bf16[8,128,384]{2,1,0:T(8,128)(2,1)S(1)} %bitcast.15), custom_call_target="tpu_custom_call" | custom-call | flops 128 | bytes 128 | tf_op jit(solution)/shard_map/mix/pallas_call | solution.py:45
  26.4 1.1 %constant_dynamic-slice_fusion = (bf16[1,8,128,128]{3,2,1,0:T(8,128)(2,1)S(1)}, bf16[1,8,128,128]{3,2,1,0:T(8,128)(2,1)S(1)}) fusion(bf16[16,8,128,128]{3,2,1,0:T(8,128)(2,1)} %collective-permute-done.refs_6_, s32[]{:T(128)S(6)} %select_n.20, s32[]{:T(128)S(6)} %select_n.14), kind=kLoop, calls=%fused_computation.8 | loop fusion | bytes 1048584 | tf_op jit(solution)/shard_map/dynamic_slice | solution.py:193
  27.5 0.1 pad_maximum_fusion.2
  27.6 1.5 %collective-permute-start.10 = (bf16[2,8,128,128]{3,2,1,0:T(8,128)(2,1)S(1)}, bf16[2,8,128,128]{3,2,1,0:T(8,128)(2,1)S(1)}, u32[]{:S(2)}, u32[]{:S(2)}) collective-permute-start(bf16[2,8,128,128]{3,2,1,0:T(8,128)(2,1)S(1)} %pad_maximum_fusion.2), channel_id=1, source_target_pairs={{0,4},{1,5},{2,6},{3,7},{4,0},{5,1},{6,2},{7,3},{8,12},{9,13},{10,... | collective-permute-start | bytes 1572872 | tf_op jit(solution)/shard_map/ppermute | solution.py:190
  29.0 0.0 collective-permute-done.1.refs_7_
  29.0 0.0 collective-permute-done.2.refs_8_.refs_9_
  29.0 2.8 %add_open.2.refs_8_ = f32[1536,384]{1,0:T(8,128)S(1)} custom-call(s32[1]{0:T(128)} %bitcast.me_ref, s32[16,128]{1,0:T(8,128)S(1)} %copy-done.3, bf16[16,8,128,384]{3,2,1,0:T(8,128)(2,1)S(1)} %mix.1.refs_0_.refs_1_.refs_2_.refs_3_.refs_4_.refs_5_.refs_6_, bf16[16,8,128,384]{3,2,1,0:T(8,128)(2,1)S(1)} %mix.1.refs_0_.refs_1_.refs_2_.refs_3_.refs_4_.refs_5_.refs_6_, ...), custom_call_target="tpu_custom_call" | custom-call | flops 40 | bytes 40 | tf_op jit(solution)/shard_map/add_open/pallas_call | solution.py:155
  31.8 1.0 constant_dynamic-slice_fusion.2
  32.8 0.1 pad_maximum_fusion.1
  32.9 1.3 %collective-permute-start.9 = (bf16[2,8,128,128]{3,2,1,0:T(8,128)(2,1)S(1)}, bf16[2,8,128,128]{3,2,1,0:T(8,128)(2,1)S(1)}, u32[]{:S(2)}, u32[]{:S(2)}) collective-permute-start(bf16[2,8,128,128]{3,2,1,0:T(8,128)(2,1)S(1)} %pad_maximum_fusion.1), channel_id=1, source_target_pairs={{0,2},{1,3},{2,0},{3,1},{4,6},{5,7},{6,4},{7,5},{8,10},{9,11},{10,... | collective-permute-start | bytes 1572872 | tf_op jit(solution)/shard_map/ppermute | solution.py:190
  34.2 0.0 collective-permute-start.8
  34.2 2.1 %collective-permute-done.12.refs_6_.refs_7_ = bf16[2,4,128,128]{3,2,1,0:T(8,128)(2,1)S(1)} collective-permute-done((bf16[2,4,128,128]{3,2,1,0:T(8,128)(2,1)S(1)}, bf16[2,4,128,128]{3,2,1,0:T(8,128)(2,1)S(1)}, u32[]{:S(2)}, u32[]{:S(2)}) %collective-permute-start.12) | collective-permute-done | bytes 262176 | tf_op jit(solution)/shard_map/ppermute | solution.py:190
  36.3 3.4 %collective-permute-start.7 = (bf16[1,8,128,128]{3,2,1,0:T(8,128)(2,1)S(1)}, bf16[1,8,128,128]{3,2,1,0:T(8,128)(2,1)S(1)}, u32[]{:S(2)}, u32[]{:S(2)}) collective-permute-start(bf16[1,8,128,128]{3,2,1,0:T(8,128)(2,1)S(1)} %get-tuple-element.38), channel_id=1, source_target_pairs={{0,8},{1,9},{2,10},{3,11},{4,12},{5,13},{6,14},{7,15},{8,0},{9,1},... | collective-permute-start | bytes 786440 | tf_op jit(solution)/shard_map/ppermute | solution.py:190
  39.7 1.1 %constant_dynamic-slice_fusion.5 = (bf16[1,4,128,128]{3,2,1,0:T(8,128)(2,1)S(1)}, bf16[1,4,128,128]{3,2,1,0:T(8,128)(2,1)S(1)}, bf16[1,4,128,128]{3,2,1,0:T(8,128)(2,1)S(1)}) fusion(bf16[16,8,128,128]{3,2,1,0:T(8,128)(2,1)} %collective-permute-done.refs_6_, s32[]{:T(128)S(6)} %select_n.17, s32[]{:T(128)S(6)} %select_n.15, s32[]{:T(128)S(6)} %select_n.18), kind=kLoop, calls=%fused_computation.13 | loop fusion | bytes 786444 | tf_op jit(solution)/shard_map/dynamic_slice | solution.py:193
  40.8 2.8 %collective-permute-start.5 = (bf16[2,4,128,128]{3,2,1,0:T(8,128)(2,1)S(1)}, bf16[2,4,128,128]{3,2,1,0:T(8,128)(2,1)S(1)}, u32[]{:S(2)}, u32[]{:S(2)}) collective-permute-start(bf16[2,4,128,128]{3,2,1,0:T(8,128)(2,1)S(1)} %pad_maximum_fusion.3), channel_id=1, source_target_pairs={{0,12},{1,13},{2,14},{3,15},{4,8},{5,9},{6,10},{7,11},{8,4},{9,5},... | collective-permute-start | bytes 786440 | tf_op jit(solution)/shard_map/ppermute | solution.py:190
  43.6 1.6 %add_open.3.refs_14_ = f32[1536,384]{1,0:T(8,128)S(1)} custom-call(s32[1]{0:T(128)} %bitcast.me_ref, s32[16,128]{1,0:T(8,128)S(1)} %copy-done.3, bf16[16,8,128,384]{3,2,1,0:T(8,128)(2,1)S(1)} %mix.1.refs_0_.refs_1_.refs_2_.refs_3_.refs_4_.refs_5_.refs_6_, bf16[16,8,128,384]{3,2,1,0:T(8,128)(2,1)S(1)} %mix.1.refs_0_.refs_1_.refs_2_.refs_3_.refs_4_.refs_5_.refs_6_, ...), custom_call_target="tpu_custom_call" | custom-call | flops 32 | bytes 32 | tf_op jit(solution)/shard_map/add_open/pallas_call | solution.py:155
  45.2 18.3 %collective-permute-done.7.refs_7_ = bf16[1,8,128,128]{3,2,1,0:T(8,128)(2,1)S(1)} collective-permute-done((bf16[1,8,128,128]{3,2,1,0:T(8,128)(2,1)S(1)}, bf16[1,8,128,128]{3,2,1,0:T(8,128)(2,1)S(1)}, u32[]{:S(2)}, u32[]{:S(2)}) %collective-permute-start.7) | collective-permute-done | bytes 262176 | tf_op jit(solution)/shard_map/ppermute | solution.py:190
  63.5 0.0 collective-permute-done.8.refs_8_.refs_9_
  63.5 2.4 %add_split.1 = (f32[1024,384]{1,0:T(8,128)S(1)}, bf16[256,384]{1,0:T(8,128)(2,1)S(1)}, bf16[256,384]{1,0:T(8,128)(2,1)S(1)}) custom-call(s32[1]{0:T(128)} %bitcast.me_ref, s32[16,128]{1,0:T(8,128)S(1)} %copy-done.3, bf16[16,8,128,384]{3,2,1,0:T(8,128)(2,1)S(1)} %mix.1.refs_0_.refs_1_.refs_2_.refs_3_.refs_4_.refs_5_.refs_6_, ...), custom_call_target="tpu_custom_call" | custom-call | flops 56 | bytes 56 | tf_op jit(solution)/shard_map/add_split/pallas_call | solution.py:155
  66.0 1.8 %collective-permute-start.13 = (bf16[256,384]{1,0:T(8,128)(2,1)S(1)}, bf16[256,384]{1,0:T(8,128)(2,1)S(1)}, u32[]{:S(2)}, u32[]{:S(2)}) collective-permute-start(bf16[256,384]{1,0:T(8,128)(2,1)S(1)} %get-tuple-element.35), channel_id=1, source_target_pairs={{0,1},{1,0},{2,3},{3,2},{4,5},{5,4},{6,7},{7,6},{8,9},{9,8},{10,11... | collective-permute-start | bytes 589832 | tf_op jit(solution)/shard_map/ppermute | solution.py:172
  67.8 4.0 %collective-permute-start.6 = (bf16[2,4,128,128]{3,2,1,0:T(8,128)(2,1)S(1)}, bf16[2,4,128,128]{3,2,1,0:T(8,128)(2,1)S(1)}, u32[]{:S(2)}, u32[]{:S(2)}) collective-permute-start(bf16[2,4,128,128]{3,2,1,0:T(8,128)(2,1)S(1)} %pad_maximum_fusion.4), channel_id=1, source_target_pairs={{0,10},{1,11},{2,8},{3,9},{4,14},{5,15},{6,12},{7,13},{8,2},{9,3},... | collective-permute-start | bytes 786440 | tf_op jit(solution)/shard_map/ppermute | solution.py:190
  71.8 2.5 %collective-permute-start.14 = (bf16[256,384]{1,0:T(8,128)(2,1)S(1)}, bf16[256,384]{1,0:T(8,128)(2,1)S(1)}, u32[]{:S(2)}, u32[]{:S(2)}) collective-permute-start(bf16[256,384]{1,0:T(8,128)(2,1)S(1)} %get-tuple-element.36), channel_id=1, source_target_pairs={{1,2},{3,4},{5,6},{7,8},{9,10},{11,12},{13,14},{2,1},{4,3},{6,5},{... | collective-permute-start | bytes 589832 | tf_op jit(solution)/shard_map/ppermute | solution.py:174
  74.3 2.0 %collective-permute-start.3 = (bf16[1,4,128,128]{3,2,1,0:T(8,128)(2,1)S(1)}, bf16[1,4,128,128]{3,2,1,0:T(8,128)(2,1)S(1)}, u32[]{:S(2)}, u32[]{:S(2)}) collective-permute-start(bf16[1,4,128,128]{3,2,1,0:T(8,128)(2,1)S(1)} %get-tuple-element.41), channel_id=1, source_target_pairs={{0,14},{1,15},{2,12},{3,13},{4,10},{5,11},{6,8},{7,9},{8,6},{9,7},... | collective-permute-start | bytes 393224 | tf_op jit(solution)/shard_map/ppermute | solution.py:190
  76.3 0.4 collective-permute-start.4
  76.7 0.8 add_core.2.refs_8_
  77.5 6.6 %collective-permute-done.5.refs_4_.refs_5_ = bf16[2,4,128,128]{3,2,1,0:T(8,128)(2,1)S(1)} collective-permute-done((bf16[2,4,128,128]{3,2,1,0:T(8,128)(2,1)S(1)}, bf16[2,4,128,128]{3,2,1,0:T(8,128)(2,1)S(1)}, u32[]{:S(2)}, u32[]{:S(2)}) %collective-permute-start.5) | collective-permute-done | bytes 262176 | tf_op jit(solution)/shard_map/ppermute | solution.py:190
  84.1 4.7 %collective-permute-done.6.refs_6_.refs_7_ = bf16[2,4,128,128]{3,2,1,0:T(8,128)(2,1)S(1)} collective-permute-done((bf16[2,4,128,128]{3,2,1,0:T(8,128)(2,1)S(1)}, bf16[2,4,128,128]{3,2,1,0:T(8,128)(2,1)S(1)}, u32[]{:S(2)}, u32[]{:S(2)}) %collective-permute-start.6) | collective-permute-done | bytes 262176 | tf_op jit(solution)/shard_map/ppermute | solution.py:190
  88.8 1.4 %add_core.3.refs_4_ = f32[1024,384]{1,0:T(8,128)S(1)} custom-call(s32[1]{0:T(128)} %bitcast.me_ref, s32[16,128]{1,0:T(8,128)S(1)} %copy-done.3, bf16[16,8,128,384]{3,2,1,0:T(8,128)(2,1)S(1)} %mix.1.refs_0_.refs_1_.refs_2_.refs_3_.refs_4_.refs_5_.refs_6_, bf16[16,8,128,384]{3,2,1,0:T(8,128)(2,1)S(1)} %mix.1.refs_0_.refs_1_.refs_2_.refs_3_.refs_4_.refs_5_.refs_6_, ...), custom_call_target="tpu_custom_call" | custom-call | flops 32 | bytes 32 | tf_op jit(solution)/shard_map/add_core/pallas_call | solution.py:155
  90.2 6.5 %collective-permute-done.3.refs_2_ = bf16[1,4,128,128]{3,2,1,0:T(8,128)(2,1)S(1)} collective-permute-done((bf16[1,4,128,128]{3,2,1,0:T(8,128)(2,1)S(1)}, bf16[1,4,128,128]{3,2,1,0:T(8,128)(2,1)S(1)}, u32[]{:S(2)}, u32[]{:S(2)}) %collective-permute-start.3) | collective-permute-done | bytes 131104 | tf_op jit(solution)/shard_map/ppermute | solution.py:190
  96.8 1.4 %collective-permute-done.4.refs_3_ = bf16[1,4,128,128]{3,2,1,0:T(8,128)(2,1)S(1)} collective-permute-done((bf16[1,4,128,128]{3,2,1,0:T(8,128)(2,1)S(1)}, bf16[1,4,128,128]{3,2,1,0:T(8,128)(2,1)S(1)}, u32[]{:S(2)}, u32[]{:S(2)}) %collective-permute-start.4) | collective-permute-done | bytes 131104 | tf_op jit(solution)/shard_map/ppermute | solution.py:190
  98.2 2.1 %add_final.1 = bf16[1024,384]{1,0:T(8,128)(2,1)} custom-call(s32[1]{0:T(128)} %bitcast.me_ref, s32[16,128]{1,0:T(8,128)S(1)} %copy-done.3, bf16[16,8,128,384]{3,2,1,0:T(8,128)(2,1)S(1)} %mix.1.refs_0_.refs_1_.refs_2_.refs_3_.refs_4_.refs_5_.refs_6_, bf16[16,8,128,384]{3,2,1,0:T(8,128)(2,1)S(1)} %mix.1.refs_0_.refs_1_.refs_2_.refs_3_.refs_4_.refs_5_.refs_6_, ...), custom_call_target="tpu_custom_call" | custom-call | flops 16 | bytes 16 | tf_op jit(solution)/shard_map/add_final/pallas_call | solution.py:155
  (19 shorter events, 0.3 us)
Async XLA Ops:
  0.0 18.1 %copy-start.2 = (bf16[1024,384]{1,0:T(8,128)(2,1)S(1)}, bf16[1024,384]{1,0:T(8,128)(2,1)}, u32[]{:S(2)}) copy-start(bf16[1024,384]{1,0:T(8,128)(2,1)} %param.4) | copy-start | bytes 2359300
  0.0 7.8 %collective-permute-start = (bf16[16,8,128,128]{3,2,1,0:T(8,128)(2,1)}, bf16[16,8,128,128]{3,2,1,0:T(8,128)(2,1)}, u32[]{:S(2)}, u32[]{:S(2)}) collective-permute-start(bf16[16,8,128,128]{3,2,1,0:T(8,128)(2,1)} %bitcast.4), channel_id=1, source_target_pairs={{0,1},{1,0},{2,3},{3,2},{4,5},{5,4},{6,7},{7,6},{8,9},{9,8},{10,11... | collective-permute-start | bytes 12582920 | tf_op jit(solution)/shard_map/ppermute | solution.py:190
  1.6 27.4 %collective-permute-start.1 = (bf16[1,8,128,128]{3,2,1,0:T(8,128)(2,1)S(1)}, bf16[1,8,128,128]{3,2,1,0:T(8,128)(2,1)S(1)}, u32[]{:S(2)}, u32[]{:S(2)}) collective-permute-start(bf16[1,8,128,128]{3,2,1,0:T(8,128)(2,1)S(1)} %constant_dynamic-slice_fusion.25), channel_id=1, source_target_pairs={{0,8},{1,9},{2,10},{3,11},{4,12},{5,13},{6,14},{7,15},{8,0},{9,1},... | collective-permute-start | bytes 786440 | tf_op jit(solution)/shard_map/ppermute | solution.py:190
  1.8 16.3 %copy-start = (bf16[16384,128]{1,0:T(8,128)(2,1)S(1)}, bf16[16384,128]{1,0:T(8,128)(2,1)}, u32[]{:S(2)}) copy-start(bf16[16384,128]{1,0:T(8,128)(2,1)} %param.6) | copy-start | bytes 12582916
  8.8 20.2 %collective-permute-start.2 = (bf16[2,4,128,128]{3,2,1,0:T(8,128)(2,1)S(1)}, bf16[2,4,128,128]{3,2,1,0:T(8,128)(2,1)S(1)}, u32[]{:S(2)}, u32[]{:S(2)}) collective-permute-start(bf16[2,4,128,128]{3,2,1,0:T(8,128)(2,1)S(1)} %maximum_maximum_fusion), channel_id=1, source_target_pairs={{0,12},{1,13},{2,14},{3,15},{4,8},{5,9},{6,10},{7,11},{8,4},{9,5},... | collective-permute-start | bytes 786440 | tf_op jit(solution)/shard_map/ppermute | solution.py:190
  11.0 29.8 %collective-permute-start.11 = (bf16[2,8,128,128]{3,2,1,0:T(8,128)(2,1)S(1)}, bf16[2,8,128,128]{3,2,1,0:T(8,128)(2,1)S(1)}, u32[]{:S(2)}, u32[]{:S(2)}) collective-permute-start(bf16[2,8,128,128]{3,2,1,0:T(8,128)(2,1)S(1)} %pad_maximum_fusion), channel_id=1, source_target_pairs={{0,6},{1,7},{2,4},{3,5},{4,2},{5,3},{6,0},{7,1},{8,14},{9,15},{10,... | collective-permute-start | bytes 1572872 | tf_op jit(solution)/shard_map/ppermute | solution.py:190
  15.0 21.3 %collective-permute-start.12 = (bf16[2,4,128,128]{3,2,1,0:T(8,128)(2,1)S(1)}, bf16[2,4,128,128]{3,2,1,0:T(8,128)(2,1)S(1)}, u32[]{:S(2)}, u32[]{:S(2)}) collective-permute-start(bf16[2,4,128,128]{3,2,1,0:T(8,128)(2,1)S(1)} %maximum_maximum_fusion.1), channel_id=1, source_target_pairs={{0,10},{1,11},{2,8},{3,9},{4,14},{5,15},{6,12},{7,13},{8,2},{9,3},... | collective-permute-start | bytes 786440 | tf_op jit(solution)/shard_map/ppermute | solution.py:190
  18.1 2.2 %copy-start.1 = (bf16[16,1024,128]{2,1,0:T(8,128)(2,1)S(1)}, bf16[16,1024,128]{2,1,0:T(8,128)(2,1)}, u32[]{:S(2)}) copy-start(bf16[16,1024,128]{2,1,0:T(8,128)(2,1)} %param.5) | copy-start | bytes 12582916
  20.3 8.7 %copy-start.3 = (s32[16,128]{1,0:T(8,128)S(1)}, s32[16,128]{1,0:T(8,128)}, u32[]{:S(2)}) copy-start(s32[16,128]{1,0:T(8,128)} %target_ref.11) | copy-start | bytes 24580
  27.6 36.0 %collective-permute-start.10 = (bf16[2,8,128,128]{3,2,1,0:T(8,128)(2,1)S(1)}, bf16[2,8,128,128]{3,2,1,0:T(8,128)(2,1)S(1)}, u32[]{:S(2)}, u32[]{:S(2)}) collective-permute-start(bf16[2,8,128,128]{3,2,1,0:T(8,128)(2,1)S(1)} %pad_maximum_fusion.2), channel_id=1, source_target_pairs={{0,4},{1,5},{2,6},{3,7},{4,0},{5,1},{6,2},{7,3},{8,12},{9,13},{10,... | collective-permute-start | bytes 1572872 | tf_op jit(solution)/shard_map/ppermute | solution.py:190
  32.9 30.7 %collective-permute-start.9 = (bf16[2,8,128,128]{3,2,1,0:T(8,128)(2,1)S(1)}, bf16[2,8,128,128]{3,2,1,0:T(8,128)(2,1)S(1)}, u32[]{:S(2)}, u32[]{:S(2)}) collective-permute-start(bf16[2,8,128,128]{3,2,1,0:T(8,128)(2,1)S(1)} %pad_maximum_fusion.1), channel_id=1, source_target_pairs={{0,2},{1,3},{2,0},{3,1},{4,6},{5,7},{6,4},{7,5},{8,10},{9,11},{10,... | collective-permute-start | bytes 1572872 | tf_op jit(solution)/shard_map/ppermute | solution.py:190
  34.2 29.3 %collective-permute-start.8 = (bf16[2,4,128,128]{3,2,1,0:T(8,128)(2,1)S(1)}, bf16[2,4,128,128]{3,2,1,0:T(8,128)(2,1)S(1)}, u32[]{:S(2)}, u32[]{:S(2)}) collective-permute-start(bf16[2,4,128,128]{3,2,1,0:T(8,128)(2,1)S(1)} %maximum_maximum_fusion.2), channel_id=1, source_target_pairs={{0,14},{1,15},{2,12},{3,13},{4,10},{5,11},{6,8},{7,9},{8,6},{9,7},... | collective-permute-start | bytes 786440 | tf_op jit(solution)/shard_map/ppermute | solution.py:190
  36.3 27.2 %collective-permute-start.7 = (bf16[1,8,128,128]{3,2,1,0:T(8,128)(2,1)S(1)}, bf16[1,8,128,128]{3,2,1,0:T(8,128)(2,1)S(1)}, u32[]{:S(2)}, u32[]{:S(2)}) collective-permute-start(bf16[1,8,128,128]{3,2,1,0:T(8,128)(2,1)S(1)} %get-tuple-element.38), channel_id=1, source_target_pairs={{0,8},{1,9},{2,10},{3,11},{4,12},{5,13},{6,14},{7,15},{8,0},{9,1},... | collective-permute-start | bytes 786440 | tf_op jit(solution)/shard_map/ppermute | solution.py:190
  40.8 43.3 %collective-permute-start.5 = (bf16[2,4,128,128]{3,2,1,0:T(8,128)(2,1)S(1)}, bf16[2,4,128,128]{3,2,1,0:T(8,128)(2,1)S(1)}, u32[]{:S(2)}, u32[]{:S(2)}) collective-permute-start(bf16[2,4,128,128]{3,2,1,0:T(8,128)(2,1)S(1)} %pad_maximum_fusion.3), channel_id=1, source_target_pairs={{0,12},{1,13},{2,14},{3,15},{4,8},{5,9},{6,10},{7,11},{8,4},{9,5},... | collective-permute-start | bytes 786440 | tf_op jit(solution)/shard_map/ppermute | solution.py:190
  66.0 10.3 %collective-permute-start.13 = (bf16[256,384]{1,0:T(8,128)(2,1)S(1)}, bf16[256,384]{1,0:T(8,128)(2,1)S(1)}, u32[]{:S(2)}, u32[]{:S(2)}) collective-permute-start(bf16[256,384]{1,0:T(8,128)(2,1)S(1)} %get-tuple-element.35), channel_id=1, source_target_pairs={{0,1},{1,0},{2,3},{3,2},{4,5},{5,4},{6,7},{7,6},{8,9},{9,8},{10,11... | collective-permute-start | bytes 589832 | tf_op jit(solution)/shard_map/ppermute | solution.py:172
  67.8 21.0 %collective-permute-start.6 = (bf16[2,4,128,128]{3,2,1,0:T(8,128)(2,1)S(1)}, bf16[2,4,128,128]{3,2,1,0:T(8,128)(2,1)S(1)}, u32[]{:S(2)}, u32[]{:S(2)}) collective-permute-start(bf16[2,4,128,128]{3,2,1,0:T(8,128)(2,1)S(1)} %pad_maximum_fusion.4), channel_id=1, source_target_pairs={{0,10},{1,11},{2,8},{3,9},{4,14},{5,15},{6,12},{7,13},{8,2},{9,3},... | collective-permute-start | bytes 786440 | tf_op jit(solution)/shard_map/ppermute | solution.py:190
  71.8 17.0 %collective-permute-start.14 = (bf16[256,384]{1,0:T(8,128)(2,1)S(1)}, bf16[256,384]{1,0:T(8,128)(2,1)S(1)}, u32[]{:S(2)}, u32[]{:S(2)}) collective-permute-start(bf16[256,384]{1,0:T(8,128)(2,1)S(1)} %get-tuple-element.36), channel_id=1, source_target_pairs={{1,2},{3,4},{5,6},{7,8},{9,10},{11,12},{13,14},{2,1},{4,3},{6,5},{... | collective-permute-start | bytes 589832 | tf_op jit(solution)/shard_map/ppermute | solution.py:174
  74.3 22.5 %collective-permute-start.3 = (bf16[1,4,128,128]{3,2,1,0:T(8,128)(2,1)S(1)}, bf16[1,4,128,128]{3,2,1,0:T(8,128)(2,1)S(1)}, u32[]{:S(2)}, u32[]{:S(2)}) collective-permute-start(bf16[1,4,128,128]{3,2,1,0:T(8,128)(2,1)S(1)} %get-tuple-element.41), channel_id=1, source_target_pairs={{0,14},{1,15},{2,12},{3,13},{4,10},{5,11},{6,8},{7,9},{8,6},{9,7},... | collective-permute-start | bytes 393224 | tf_op jit(solution)/shard_map/ppermute | solution.py:190
  76.3 21.9 %collective-permute-start.4 = (bf16[1,4,128,128]{3,2,1,0:T(8,128)(2,1)S(1)}, bf16[1,4,128,128]{3,2,1,0:T(8,128)(2,1)S(1)}, u32[]{:S(2)}, u32[]{:S(2)}) collective-permute-start(bf16[1,4,128,128]{3,2,1,0:T(8,128)(2,1)S(1)} %get-tuple-element.44), channel_id=1, source_target_pairs={{0,14},{1,15},{2,12},{3,13},{4,10},{5,11},{6,8},{7,9},{8,6},{9,7},... | collective-permute-start | bytes 393224 | tf_op jit(solution)/shard_map/ppermute | solution.py:190

commit v5 on v4

--- a/solution.py
+++ b/solution.py
@@ -231,16 +231,16 @@
     sums = add(mixed, items((0, "all"), (1, "all"), (FIRST, "all"), *pairs(EARLY[:1])), None, "open")
     source, relayed = after(right, sums), after(exchanged, sums)
     send(source, relayed, *LATE[0])
-    send(source, relayed, 12, "inner")
     send(source, relayed, 10, "inner")
-    send_single(source, 14, "inner", 14)
-    send_single(relayed, 14, "inner", 15)
+    send(source, relayed, 14, "inner")
+    send_single(source, 12, "inner", 12)
+    send_single(relayed, 12, "inner", 13)
     sums = add(mixed, items(*pairs(EARLY[1:3])), sums, "open")
     core, to_pair, to_other = add(mixed, items((FIRST + 1, "all"), *pairs(EARLY[3:] + LATE)), sums, "split")
     halos = neighbours(to_pair, to_other)
     core = add(mixed, [], core, "core", halos[:1])
-    core = add(mixed, items(*pairs([(12, "inner"), (10, "inner")])), core, "core", halos[1:])
-    return add(mixed, items(*pairs([(14, "inner")])), core, "final")
+    core = add(mixed, items(*pairs([(10, "inner"), (14, "inner")])), core, "core", halos[1:])
+    return add(mixed, items(*pairs([(12, "inner")])), core, "final")
 
 
 def solution(mesh):

time: 101 us -> 100 us (0.990)
  the two profiles are of different devices: /device:TPU:17 before, /device:TPU:8 now
where the time goes in v5:
time: 100 us; the launch traced here: 99.5 us
  waiting for transfers between devices  42.8 us (43%)
  starting transfers between devices  27 us (27%)
  Pallas kernels  17.2 us (17%)
  local copies, waits for them, and re-layouts  12 us (12%)
    ppermute x13, waiting for transfers between devices, move(): return lax.ppermute(operand, 'terms', [(i, i ^ s) for i in range(devices)])  42.8 us
    ppermute x13, starting transfers between devices, move(): return lax.ppermute(operand, 'terms', [(i, i ^ s) for i in range(devices)])  20.2 us
    pallas_call x6, Pallas kernels, add(): pl.pallas_call(functools.partial(add_kernel, width, tuple(items), terms_o...  11.1 us
    dynamic_slice x14, local copies, waits for them, and re-layouts, pick(): lax.dynamic_slice(source, (index, start, 0, 0), (1, count, width, width))  9.8 us
    ppermute x1, starting transfers between devices, neighbours(): lax.ppermute(to_other, 'terms', others + [(b, a) for a, b in others])  6.66 us
    pallas_call x1, Pallas kernels, mix(): pl.pallas_call(functools.partial(mix_kernel, min(4, terms)), grid=(blocks...  6.07 us
    unnamed x8, local copies, waits for them, and re-layouts  2.19 us
  transfers between devices with their start and end apart: 15, of which 6 were waited for; matrix products, arithmetic and copies ran while one was open for 10% of the time, Pallas kernels for 15%

profile of v5, /device:TPU:8, one launch (start us, length us, event | category | flops | bytes accessed | tf_op | source)
XLA Modules:
  0.0 99.5 jit_solution(2843591499404958364)
XLA Ops:
  0.0 1.0 %constant_dynamic-slice_fusion.25 = bf16[1,8,128,128]{3,2,1,0:T(8,128)(2,1)S(1)} fusion(bf16[16,8,128,128]{3,2,1,0:T(8,128)(2,1)} %bitcast.5, s32[]{:T(128)S(6)} %select_n.14), kind=kLoop, calls=%fused_computation.33 | loop fusion | bytes 524292 | tf_op jit(solution)/shard_map/dynamic_slice | solution.py:193
  1.1 2.7 %collective-permute-start.1 = (bf16[1,8,128,128]{3,2,1,0:T(8,128)(2,1)S(1)}, bf16[1,8,128,128]{3,2,1,0:T(8,128)(2,1)S(1)}, u32[]{:S(2)}, u32[]{:S(2)}) collective-permute-start(bf16[1,8,128,128]{3,2,1,0:T(8,128)(2,1)S(1)} %constant_dynamic-slice_fusion.25), channel_id=1, source_target_pairs={{0,8},{1,9},{2,10},{3,11},{4,12},{5,13},{6,14},{7,15},{8,0},{9,1},... | collective-permute-start | bytes 786440 | tf_op jit(solution)/shard_map/ppermute | solution.py:190
  3.7 3.8 %collective-permute-done.refs_6_ = bf16[16,8,128,128]{3,2,1,0:T(8,128)(2,1)} collective-permute-done((bf16[16,8,128,128]{3,2,1,0:T(8,128)(2,1)}, bf16[16,8,128,128]{3,2,1,0:T(8,128)(2,1)}, u32[]{:S(2)}, u32[]{:S(2)}) %collective-permute-start) | collective-permute-done | bytes 4194336 | tf_op jit(solution)/shard_map/ppermute | solution.py:190
  7.5 1.0 constant_dynamic-slice_fusion.22
  8.5 1.6 %collective-permute-start.2 = (bf16[2,4,128,128]{3,2,1,0:T(8,128)(2,1)S(1)}, bf16[2,4,128,128]{3,2,1,0:T(8,128)(2,1)S(1)}, u32[]{:S(2)}, u32[]{:S(2)}) collective-permute-start(bf16[2,4,128,128]{3,2,1,0:T(8,128)(2,1)S(1)} %maximum_maximum_fusion), channel_id=1, source_target_pairs={{0,12},{1,13},{2,14},{3,15},{4,8},{5,9},{6,10},{7,11},{8,4},{9,5},... | collective-permute-start | bytes 786440 | tf_op jit(solution)/shard_map/ppermute | solution.py:190
  10.1 1.0 constant_dynamic-slice_fusion.19
  11.1 1.0 constant_dynamic-slice_fusion.20
  12.1 0.1 pad_maximum_fusion
  12.1 3.5 %collective-permute-start.11 = (bf16[2,8,128,128]{3,2,1,0:T(8,128)(2,1)S(1)}, bf16[2,8,128,128]{3,2,1,0:T(8,128)(2,1)S(1)}, u32[]{:S(2)}, u32[]{:S(2)}) collective-permute-start(bf16[2,8,128,128]{3,2,1,0:T(8,128)(2,1)S(1)} %pad_maximum_fusion), channel_id=1, source_target_pairs={{0,6},{1,7},{2,4},{3,5},{4,2},{5,3},{6,0},{7,1},{8,14},{9,15},{10,... | collective-permute-start | bytes 1572872 | tf_op jit(solution)/shard_map/ppermute | solution.py:190
  15.6 0.9 constant_dynamic-slice_fusion.16
  16.5 0.9 constant_dynamic-slice_fusion.18
  17.5 0.1 collective-permute-start.12
  17.5 0.9 constant_dynamic-slice_fusion.12
  18.5 0.0 copy-start.1
  18.5 2.2 %copy-done.1 = bf16[16,1024,128]{2,1,0:T(8,128)(2,1)S(1)} copy-done((bf16[16,1024,128]{2,1,0:T(8,128)(2,1)S(1)}, bf16[16,1024,128]{2,1,0:T(8,128)(2,1)}, u32[]{:S(2)}) %copy-start.1) | copy-done | bytes 4194328
  20.7 6.1 %mix.1.refs_0_.refs_1_.refs_2_.refs_3_.refs_4_.refs_5_.refs_6_ = bf16[16,8,128,384]{3,2,1,0:T(8,128)(2,1)S(1)} custom-call(bf16[16,8,128,128]{3,2,1,0:T(8,128)(2,1)S(1)} %bitcast.14, bf16[8,128,384]{2,1,0:T(8,128)(2,1)S(1)} %bitcast.15), custom_call_target="tpu_custom_call" | custom-call | flops 128 | bytes 128 | tf_op jit(solution)/shard_map/mix/pallas_call | solution.py:45
  26.8 1.1 %constant_dynamic-slice_fusion = (bf16[1,8,128,128]{3,2,1,0:T(8,128)(2,1)S(1)}, bf16[1,8,128,128]{3,2,1,0:T(8,128)(2,1)S(1)}) fusion(bf16[16,8,128,128]{3,2,1,0:T(8,128)(2,1)} %collective-permute-done.refs_6_, s32[]{:T(128)S(6)} %select_n.20, s32[]{:T(128)S(6)} %select_n.14), kind=kLoop, calls=%fused_computation.8 | loop fusion | bytes 1048584 | tf_op jit(solution)/shard_map/dynamic_slice | solution.py:193
  27.9 0.1 pad_maximum_fusion.2
  27.9 0.6 collective-permute-start.10
  28.5 0.0 collective-permute-done.1.refs_7_
  28.5 0.0 collective-permute-done.2.refs_8_.refs_9_
  28.5 2.8 %add_open.2.refs_8_ = f32[1536,384]{1,0:T(8,128)S(1)} custom-call(s32[1]{0:T(128)} %bitcast.me_ref, s32[16,128]{1,0:T(8,128)S(1)} %copy-done.3, bf16[16,8,128,384]{3,2,1,0:T(8,128)(2,1)S(1)} %mix.1.refs_0_.refs_1_.refs_2_.refs_3_.refs_4_.refs_5_.refs_6_, bf16[16,8,128,384]{3,2,1,0:T(8,128)(2,1)S(1)} %mix.1.refs_0_.refs_1_.refs_2_.refs_3_.refs_4_.refs_5_.refs_6_, ...), custom_call_target="tpu_custom_call" | custom-call | flops 40 | bytes 40 | tf_op jit(solution)/shard_map/add_open/pallas_call | solution.py:155
  31.3 1.0 constant_dynamic-slice_fusion.2
  32.3 0.1 pad_maximum_fusion.1
  32.4 1.8 %collective-permute-start.9 = (bf16[2,8,128,128]{3,2,1,0:T(8,128)(2,1)S(1)}, bf16[2,8,128,128]{3,2,1,0:T(8,128)(2,1)S(1)}, u32[]{:S(2)}, u32[]{:S(2)}) collective-permute-start(bf16[2,8,128,128]{3,2,1,0:T(8,128)(2,1)S(1)} %pad_maximum_fusion.1), channel_id=1, source_target_pairs={{0,2},{1,3},{2,0},{3,1},{4,6},{5,7},{6,4},{7,5},{8,10},{9,11},{10,... | collective-permute-start | bytes 1572872 | tf_op jit(solution)/shard_map/ppermute | solution.py:190
  34.2 2.6 %collective-permute-start.8 = (bf16[2,4,128,128]{3,2,1,0:T(8,128)(2,1)S(1)}, bf16[2,4,128,128]{3,2,1,0:T(8,128)(2,1)S(1)}, u32[]{:S(2)}, u32[]{:S(2)}) collective-permute-start(bf16[2,4,128,128]{3,2,1,0:T(8,128)(2,1)S(1)} %maximum_maximum_fusion.2), channel_id=1, source_target_pairs={{0,14},{1,15},{2,12},{3,13},{4,10},{5,11},{6,8},{7,9},{8,6},{9,7},... | collective-permute-start | bytes 786440 | tf_op jit(solution)/shard_map/ppermute | solution.py:190
  36.8 1.2 %collective-permute-done.12.refs_6_.refs_7_ = bf16[2,4,128,128]{3,2,1,0:T(8,128)(2,1)S(1)} collective-permute-done((bf16[2,4,128,128]{3,2,1,0:T(8,128)(2,1)S(1)}, bf16[2,4,128,128]{3,2,1,0:T(8,128)(2,1)S(1)}, u32[]{:S(2)}, u32[]{:S(2)}) %collective-permute-start.12) | collective-permute-done | bytes 262176 | tf_op jit(solution)/shard_map/ppermute | solution.py:190
  38.0 4.4 %collective-permute-start.7 = (bf16[1,8,128,128]{3,2,1,0:T(8,128)(2,1)S(1)}, bf16[1,8,128,128]{3,2,1,0:T(8,128)(2,1)S(1)}, u32[]{:S(2)}, u32[]{:S(2)}) collective-permute-start(bf16[1,8,128,128]{3,2,1,0:T(8,128)(2,1)S(1)} %get-tuple-element.38), channel_id=1, source_target_pairs={{0,8},{1,9},{2,10},{3,11},{4,12},{5,13},{6,14},{7,15},{8,0},{9,1},... | collective-permute-start | bytes 786440 | tf_op jit(solution)/shard_map/ppermute | solution.py:190
  42.4 1.1 %constant_dynamic-slice_fusion.5 = (bf16[1,4,128,128]{3,2,1,0:T(8,128)(2,1)S(1)}, bf16[1,4,128,128]{3,2,1,0:T(8,128)(2,1)S(1)}, bf16[1,4,128,128]{3,2,1,0:T(8,128)(2,1)S(1)}) fusion(bf16[16,8,128,128]{3,2,1,0:T(8,128)(2,1)} %collective-permute-done.refs_6_, s32[]{:T(128)S(6)} %select_n.18, s32[]{:T(128)S(6)} %select_n.17, s32[]{:T(128)S(6)} %select_n.15), kind=kLoop, calls=%fused_computation.13 | loop fusion | bytes 786444 | tf_op jit(solution)/shard_map/dynamic_slice | solution.py:193
  43.5 0.0 collective-permute-done.11.refs_4_.refs_5_
  43.5 0.1 collective-permute-start.5
  43.6 1.6 %add_open.3.refs_14_ = f32[1536,384]{1,0:T(8,128)S(1)} custom-call(s32[1]{0:T(128)} %bitcast.me_ref, s32[16,128]{1,0:T(8,128)S(1)} %copy-done.3, bf16[16,8,128,384]{3,2,1,0:T(8,128)(2,1)S(1)} %mix.1.refs_0_.refs_1_.refs_2_.refs_3_.refs_4_.refs_5_.refs_6_, bf16[16,8,128,384]{3,2,1,0:T(8,128)(2,1)S(1)} %mix.1.refs_0_.refs_1_.refs_2_.refs_3_.refs_4_.refs_5_.refs_6_, ...), custom_call_target="tpu_custom_call" | custom-call | flops 32 | bytes 32 | tf_op jit(solution)/shard_map/add_open/pallas_call | solution.py:155
  45.2 21.0 %collective-permute-done.7.refs_7_ = bf16[1,8,128,128]{3,2,1,0:T(8,128)(2,1)S(1)} collective-permute-done((bf16[1,8,128,128]{3,2,1,0:T(8,128)(2,1)S(1)}, bf16[1,8,128,128]{3,2,1,0:T(8,128)(2,1)S(1)}, u32[]{:S(2)}, u32[]{:S(2)}) %collective-permute-start.7) | collective-permute-done | bytes 262176 | tf_op jit(solution)/shard_map/ppermute | solution.py:190
  66.2 0.0 collective-permute-done.8.refs_8_.refs_9_
  66.2 2.4 %add_split.1 = (f32[1024,384]{1,0:T(8,128)S(1)}, bf16[256,384]{1,0:T(8,128)(2,1)S(1)}, bf16[256,384]{1,0:T(8,128)(2,1)S(1)}) custom-call(s32[1]{0:T(128)} %bitcast.me_ref, s32[16,128]{1,0:T(8,128)S(1)} %copy-done.3, bf16[16,8,128,384]{3,2,1,0:T(8,128)(2,1)S(1)} %mix.1.refs_0_.refs_1_.refs_2_.refs_3_.refs_4_.refs_5_.refs_6_, ...), custom_call_target="tpu_custom_call" | custom-call | flops 56 | bytes 56 | tf_op jit(solution)/shard_map/add_split/pallas_call | solution.py:155
  68.6 0.1 collective-permute-start.13
  68.7 0.9 collective-permute-start.6
  69.6 6.7 %collective-permute-start.14 = (bf16[256,384]{1,0:T(8,128)(2,1)S(1)}, bf16[256,384]{1,0:T(8,128)(2,1)S(1)}, u32[]{:S(2)}, u32[]{:S(2)}) collective-permute-start(bf16[256,384]{1,0:T(8,128)(2,1)S(1)} %get-tuple-element.36), channel_id=1, source_target_pairs={{1,2},{3,4},{5,6},{7,8},{9,10},{11,12},{13,14},{2,1},{4,3},{6,5},{... | collective-permute-start | bytes 589832 | tf_op jit(solution)/shard_map/ppermute | solution.py:174
  76.3 0.1 collective-permute-start.3
  76.3 0.0 collective-permute-done.13.refs_1_
  76.4 2.0 %collective-permute-start.4 = (bf16[1,4,128,128]{3,2,1,0:T(8,128)(2,1)S(1)}, bf16[1,4,128,128]{3,2,1,0:T(8,128)(2,1)S(1)}, u32[]{:S(2)}, u32[]{:S(2)}) collective-permute-start(bf16[1,4,128,128]{3,2,1,0:T(8,128)(2,1)S(1)} %get-tuple-element.44), channel_id=1, source_target_pairs={{0,12},{1,13},{2,14},{3,15},{4,8},{5,9},{6,10},{7,11},{8,4},{9,5},... | collective-permute-start | bytes 393224 | tf_op jit(solution)/shard_map/ppermute | solution.py:190
  78.4 0.8 add_core.2.refs_8_
  79.2 0.0 collective-permute-done.5.refs_4_.refs_5_
  79.2 10.9 %collective-permute-done.6.refs_6_.refs_7_ = bf16[2,4,128,128]{3,2,1,0:T(8,128)(2,1)S(1)} collective-permute-done((bf16[2,4,128,128]{3,2,1,0:T(8,128)(2,1)S(1)}, bf16[2,4,128,128]{3,2,1,0:T(8,128)(2,1)S(1)}, u32[]{:S(2)}, u32[]{:S(2)}) %collective-permute-start.6) | collective-permute-done | bytes 262176 | tf_op jit(solution)/shard_map/ppermute | solution.py:190
  90.0 1.4 %add_core.3.refs_4_ = f32[1024,384]{1,0:T(8,128)S(1)} custom-call(s32[1]{0:T(128)} %bitcast.me_ref, s32[16,128]{1,0:T(8,128)S(1)} %copy-done.3, bf16[16,8,128,384]{3,2,1,0:T(8,128)(2,1)S(1)} %mix.1.refs_0_.refs_1_.refs_2_.refs_3_.refs_4_.refs_5_.refs_6_, bf16[16,8,128,384]{3,2,1,0:T(8,128)(2,1)S(1)} %mix.1.refs_0_.refs_1_.refs_2_.refs_3_.refs_4_.refs_5_.refs_6_, ...), custom_call_target="tpu_custom_call" | custom-call | flops 32 | bytes 32 | tf_op jit(solution)/shard_map/add_core/pallas_call | solution.py:155
  91.5 4.5 %collective-permute-done.3.refs_2_ = bf16[1,4,128,128]{3,2,1,0:T(8,128)(2,1)S(1)} collective-permute-done((bf16[1,4,128,128]{3,2,1,0:T(8,128)(2,1)S(1)}, bf16[1,4,128,128]{3,2,1,0:T(8,128)(2,1)S(1)}, u32[]{:S(2)}, u32[]{:S(2)}) %collective-permute-start.3) | collective-permute-done | bytes 131104 | tf_op jit(solution)/shard_map/ppermute | solution.py:190
  96.0 1.4 %collective-permute-done.4.refs_3_ = bf16[1,4,128,128]{3,2,1,0:T(8,128)(2,1)S(1)} collective-permute-done((bf16[1,4,128,128]{3,2,1,0:T(8,128)(2,1)S(1)}, bf16[1,4,128,128]{3,2,1,0:T(8,128)(2,1)S(1)}, u32[]{:S(2)}, u32[]{:S(2)}) %collective-permute-start.4) | collective-permute-done | bytes 131104 | tf_op jit(solution)/shard_map/ppermute | solution.py:190
  97.4 2.1 %add_final.1 = bf16[1024,384]{1,0:T(8,128)(2,1)} custom-call(s32[1]{0:T(128)} %bitcast.me_ref, s32[16,128]{1,0:T(8,128)S(1)} %copy-done.3, bf16[16,8,128,384]{3,2,1,0:T(8,128)(2,1)S(1)} %mix.1.refs_0_.refs_1_.refs_2_.refs_3_.refs_4_.refs_5_.refs_6_, bf16[16,8,128,384]{3,2,1,0:T(8,128)(2,1)S(1)} %mix.1.refs_0_.refs_1_.refs_2_.refs_3_.refs_4_.refs_5_.refs_6_, ...), custom_call_target="tpu_custom_call" | custom-call | flops 16 | bytes 16 | tf_op jit(solution)/shard_map/add_final/pallas_call | solution.py:155
  (19 shorter events, 0.3 us)
Async XLA Ops:
  0.0 18.5 %copy-start.2 = (bf16[1024,384]{1,0:T(8,128)(2,1)S(1)}, bf16[1024,384]{1,0:T(8,128)(2,1)}, u32[]{:S(2)}) copy-start(bf16[1024,384]{1,0:T(8,128)(2,1)} %param.4) | copy-start | bytes 2359300
  0.0 7.5 %collective-permute-start = (bf16[16,8,128,128]{3,2,1,0:T(8,128)(2,1)}, bf16[16,8,128,128]{3,2,1,0:T(8,128)(2,1)}, u32[]{:S(2)}, u32[]{:S(2)}) collective-permute-start(bf16[16,8,128,128]{3,2,1,0:T(8,128)(2,1)} %bitcast.4), channel_id=1, source_target_pairs={{0,1},{1,0},{2,3},{3,2},{4,5},{5,4},{6,7},{7,6},{8,9},{9,8},{10,11... | collective-permute-start | bytes 12582920 | tf_op jit(solution)/shard_map/ppermute | solution.py:190
  1.1 27.5 %collective-permute-start.1 = (bf16[1,8,128,128]{3,2,1,0:T(8,128)(2,1)S(1)}, bf16[1,8,128,128]{3,2,1,0:T(8,128)(2,1)S(1)}, u32[]{:S(2)}, u32[]{:S(2)}) collective-permute-start(bf16[1,8,128,128]{3,2,1,0:T(8,128)(2,1)S(1)} %constant_dynamic-slice_fusion.25), channel_id=1, source_target_pairs={{0,8},{1,9},{2,10},{3,11},{4,12},{5,13},{6,14},{7,15},{8,0},{9,1},... | collective-permute-start | bytes 786440 | tf_op jit(solution)/shard_map/ppermute | solution.py:190
  3.7 14.7 %copy-start = (bf16[16384,128]{1,0:T(8,128)(2,1)S(1)}, bf16[16384,128]{1,0:T(8,128)(2,1)}, u32[]{:S(2)}) copy-start(bf16[16384,128]{1,0:T(8,128)(2,1)} %param.6) | copy-start | bytes 12582916
  8.5 20.0 %collective-permute-start.2 = (bf16[2,4,128,128]{3,2,1,0:T(8,128)(2,1)S(1)}, bf16[2,4,128,128]{3,2,1,0:T(8,128)(2,1)S(1)}, u32[]{:S(2)}, u32[]{:S(2)}) collective-permute-start(bf16[2,4,128,128]{3,2,1,0:T(8,128)(2,1)S(1)} %maximum_maximum_fusion), channel_id=1, source_target_pairs={{0,12},{1,13},{2,14},{3,15},{4,8},{5,9},{6,10},{7,11},{8,4},{9,5},... | collective-permute-start | bytes 786440 | tf_op jit(solution)/shard_map/ppermute | solution.py:190
  12.1 31.4 %collective-permute-start.11 = (bf16[2,8,128,128]{3,2,1,0:T(8,128)(2,1)S(1)}, bf16[2,8,128,128]{3,2,1,0:T(8,128)(2,1)S(1)}, u32[]{:S(2)}, u32[]{:S(2)}) collective-permute-start(bf16[2,8,128,128]{3,2,1,0:T(8,128)(2,1)S(1)} %pad_maximum_fusion), channel_id=1, source_target_pairs={{0,6},{1,7},{2,4},{3,5},{4,2},{5,3},{6,0},{7,1},{8,14},{9,15},{10,... | collective-permute-start | bytes 1572872 | tf_op jit(solution)/shard_map/ppermute | solution.py:190
  17.5 20.5 %collective-permute-start.12 = (bf16[2,4,128,128]{3,2,1,0:T(8,128)(2,1)S(1)}, bf16[2,4,128,128]{3,2,1,0:T(8,128)(2,1)S(1)}, u32[]{:S(2)}, u32[]{:S(2)}) collective-permute-start(bf16[2,4,128,128]{3,2,1,0:T(8,128)(2,1)S(1)} %maximum_maximum_fusion.1), channel_id=1, source_target_pairs={{0,10},{1,11},{2,8},{3,9},{4,14},{5,15},{6,12},{7,13},{8,2},{9,3},... | collective-permute-start | bytes 786440 | tf_op jit(solution)/shard_map/ppermute | solution.py:190
  18.5 2.2 %copy-start.1 = (bf16[16,1024,128]{2,1,0:T(8,128)(2,1)S(1)}, bf16[16,1024,128]{2,1,0:T(8,128)(2,1)}, u32[]{:S(2)}) copy-start(bf16[16,1024,128]{2,1,0:T(8,128)(2,1)} %param.5) | copy-start | bytes 12582916
  20.7 7.8 %copy-start.3 = (s32[16,128]{1,0:T(8,128)S(1)}, s32[16,128]{1,0:T(8,128)}, u32[]{:S(2)}) copy-start(s32[16,128]{1,0:T(8,128)} %target_ref.11) | copy-start | bytes 24580
  27.9 38.2 %collective-permute-start.10 = (bf16[2,8,128,128]{3,2,1,0:T(8,128)(2,1)S(1)}, bf16[2,8,128,128]{3,2,1,0:T(8,128)(2,1)S(1)}, u32[]{:S(2)}, u32[]{:S(2)}) collective-permute-start(bf16[2,8,128,128]{3,2,1,0:T(8,128)(2,1)S(1)} %pad_maximum_fusion.2), channel_id=1, source_target_pairs={{0,4},{1,5},{2,6},{3,7},{4,0},{5,1},{6,2},{7,3},{8,12},{9,13},{10,... | collective-permute-start | bytes 1572872 | tf_op jit(solution)/shard_map/ppermute | solution.py:190
  32.4 33.8 %collective-permute-start.9 = (bf16[2,8,128,128]{3,2,1,0:T(8,128)(2,1)S(1)}, bf16[2,8,128,128]{3,2,1,0:T(8,128)(2,1)S(1)}, u32[]{:S(2)}, u32[]{:S(2)}) collective-permute-start(bf16[2,8,128,128]{3,2,1,0:T(8,128)(2,1)S(1)} %pad_maximum_fusion.1), channel_id=1, source_target_pairs={{0,2},{1,3},{2,0},{3,1},{4,6},{5,7},{6,4},{7,5},{8,10},{9,11},{10,... | collective-permute-start | bytes 1572872 | tf_op jit(solution)/shard_map/ppermute | solution.py:190
  34.2 32.0 %collective-permute-start.8 = (bf16[2,4,128,128]{3,2,1,0:T(8,128)(2,1)S(1)}, bf16[2,4,128,128]{3,2,1,0:T(8,128)(2,1)S(1)}, u32[]{:S(2)}, u32[]{:S(2)}) collective-permute-start(bf16[2,4,128,128]{3,2,1,0:T(8,128)(2,1)S(1)} %maximum_maximum_fusion.2), channel_id=1, source_target_pairs={{0,14},{1,15},{2,12},{3,13},{4,10},{5,11},{6,8},{7,9},{8,6},{9,7},... | collective-permute-start | bytes 786440 | tf_op jit(solution)/shard_map/ppermute | solution.py:190
  38.0 28.2 %collective-permute-start.7 = (bf16[1,8,128,128]{3,2,1,0:T(8,128)(2,1)S(1)}, bf16[1,8,128,128]{3,2,1,0:T(8,128)(2,1)S(1)}, u32[]{:S(2)}, u32[]{:S(2)}) collective-permute-start(bf16[1,8,128,128]{3,2,1,0:T(8,128)(2,1)S(1)} %get-tuple-element.38), channel_id=1, source_target_pairs={{0,8},{1,9},{2,10},{3,11},{4,12},{5,13},{6,14},{7,15},{8,0},{9,1},... | collective-permute-start | bytes 786440 | tf_op jit(solution)/shard_map/ppermute | solution.py:190
  43.5 35.7 %collective-permute-start.5 = (bf16[2,4,128,128]{3,2,1,0:T(8,128)(2,1)S(1)}, bf16[2,4,128,128]{3,2,1,0:T(8,128)(2,1)S(1)}, u32[]{:S(2)}, u32[]{:S(2)}) collective-permute-start(bf16[2,4,128,128]{3,2,1,0:T(8,128)(2,1)S(1)} %pad_maximum_fusion.3), channel_id=1, source_target_pairs={{0,10},{1,11},{2,8},{3,9},{4,14},{5,15},{6,12},{7,13},{8,2},{9,3},... | collective-permute-start | bytes 786440 | tf_op jit(solution)/shard_map/ppermute | solution.py:190
  68.6 7.7 %collective-permute-start.13 = (bf16[256,384]{1,0:T(8,128)(2,1)S(1)}, bf16[256,384]{1,0:T(8,128)(2,1)S(1)}, u32[]{:S(2)}, u32[]{:S(2)}) collective-permute-start(bf16[256,384]{1,0:T(8,128)(2,1)S(1)} %get-tuple-element.35), channel_id=1, source_target_pairs={{0,1},{1,0},{2,3},{3,2},{4,5},{5,4},{6,7},{7,6},{8,9},{9,8},{10,11... | collective-permute-start | bytes 589832 | tf_op jit(solution)/shard_map/ppermute | solution.py:172
  68.7 21.3 %collective-permute-start.6 = (bf16[2,4,128,128]{3,2,1,0:T(8,128)(2,1)S(1)}, bf16[2,4,128,128]{3,2,1,0:T(8,128)(2,1)S(1)}, u32[]{:S(2)}, u32[]{:S(2)}) collective-permute-start(bf16[2,4,128,128]{3,2,1,0:T(8,128)(2,1)S(1)} %pad_maximum_fusion.4), channel_id=1, source_target_pairs={{0,14},{1,15},{2,12},{3,13},{4,10},{5,11},{6,8},{7,9},{8,6},{9,7},... | collective-permute-start | bytes 786440 | tf_op jit(solution)/shard_map/ppermute | solution.py:190
  69.6 20.4 %collective-permute-start.14 = (bf16[256,384]{1,0:T(8,128)(2,1)S(1)}, bf16[256,384]{1,0:T(8,128)(2,1)S(1)}, u32[]{:S(2)}, u32[]{:S(2)}) collective-permute-start(bf16[256,384]{1,0:T(8,128)(2,1)S(1)} %get-tuple-element.36), channel_id=1, source_target_pairs={{1,2},{3,4},{5,6},{7,8},{9,10},{11,12},{13,14},{2,1},{4,3},{6,5},{... | collective-permute-start | bytes 589832 | tf_op jit(solution)/shard_map/ppermute | solution.py:174
  76.3 19.7 %collective-permute-start.3 = (bf16[1,4,128,128]{3,2,1,0:T(8,128)(2,1)S(1)}, bf16[1,4,128,128]{3,2,1,0:T(8,128)(2,1)S(1)}, u32[]{:S(2)}, u32[]{:S(2)}) collective-permute-start(bf16[1,4,128,128]{3,2,1,0:T(8,128)(2,1)S(1)} %get-tuple-element.41), channel_id=1, source_target_pairs={{0,12},{1,13},{2,14},{3,15},{4,8},{5,9},{6,10},{7,11},{8,4},{9,5},... | collective-permute-start | bytes 393224 | tf_op jit(solution)/shard_map/ppermute | solution.py:190
  76.4 21.1 %collective-permute-start.4 = (bf16[1,4,128,128]{3,2,1,0:T(8,128)(2,1)S(1)}, bf16[1,4,128,128]{3,2,1,0:T(8,128)(2,1)S(1)}, u32[]{:S(2)}, u32[]{:S(2)}) collective-permute-start(bf16[1,4,128,128]{3,2,1,0:T(8,128)(2,1)S(1)} %get-tuple-element.44), channel_id=1, source_target_pairs={{0,12},{1,13},{2,14},{3,15},{4,8},{5,9},{6,10},{7,11},{8,4},{9,5},... | collective-permute-start | bytes 393224 | tf_op jit(solution)/shard_map/ppermute | solution.py:190
